TPU v7x, 128 devices: a whole 4x4x4 slice. The times are simulated.
128 devices in a mesh: ctx: 16 (over x, y), tp: 8 (over z, core).
Axes of the slice: x: 4, y: 4, z: 4, core: 2. Of those that a mesh axis runs over, the one named last changes fastest.
Arguments:
- hidden_states: bfloat16 [32, 8192], P(None, 'ctx'), may hold values from -24 to 24
- norm_gain: bfloat16 [8192], P('ctx'), may hold values from 0.25 to 1.75
- prompt_lengths: int32 [8], replicated, may hold values from 1 to 16384, 73728 in all
- kv_cache: bfloat16 [8, 16384, 2, 1024], P(None, ('ctx', 'tp')), may hold values from -124 to 124
- w_qkv: bfloat16 [8192, 10240], P('ctx', 'tp'), may hold values from -0.0625 to 0.0625
- w_out: bfloat16 [8192, 8192], P('tp', 'ctx'), may hold values from -0.0625 to 0.0625
Outputs:
- block_out: bfloat16 [32, 8192], P(None, 'ctx')
- kv_decode: bfloat16 [16, 128, 64, 2, 1024], P('ctx', None, None, None, 'tp')
Inputs may be any that keep to these rules, and one draw needn't show every extreme that they name: `prompt_lengths`: cache positions at or beyond a request's length are padding. Some request has exactly 16384.
All inputs are finite; a program needn't handle non-finite values.
Results may differ from a plain program's by a relative error of at most 0.012.
The roundings to bfloat16 on the way count: a program that leaves them out, or rounds other values in their place, can miss the bound.
Values may be sent and summed in bfloat16 or wider, within the bound.
No kernel may reach another device: no remote copies, remote signals or barrier semaphores. Data moves between devices by JAX's collectives and lax.ppermute only.
A program may use at most 64 MiB of HBM per device.

v0:
```python
from functools import reduce
import math

import jax
import jax.numpy as jnp
from jax import lax
from jax.sharding import PartitionSpec as P

D = 8192
HD = 128
STEPS = 4
GQA = 8


ROPE_BASE = 500000.0
ROPE_FACTOR = 8.0
LOW_FACTOR = 1.0
HIGH_FACTOR = 4.0
ROPE_ANCHOR = 8192.0
NEGATIVE = -1e30


def angles(positions, width):
    base_freq = ROPE_BASE ** (-(2.0 * jnp.arange(width // 2, dtype=jnp.float32)) / width)
    wavelength = 2.0 * math.pi / base_freq
    blend = (ROPE_ANCHOR / wavelength - LOW_FACTOR) / (HIGH_FACTOR - LOW_FACTOR)
    middle = (1.0 - blend) * base_freq / ROPE_FACTOR + blend * base_freq
    freq = jnp.where(
        wavelength > ROPE_ANCHOR / LOW_FACTOR,
        base_freq / ROPE_FACTOR,
        jnp.where(wavelength < ROPE_ANCHOR / HIGH_FACTOR, base_freq, middle),
    )
    return positions.astype(jnp.float32)[..., None] * freq


def rotate(vec, angle):
    half = vec.shape[-1] // 2
    first = vec[..., :half]
    second = vec[..., half:]
    cosine = jnp.cos(angle)
    sine = jnp.sin(angle)
    return jnp.concatenate(
        [first * cosine - second * sine, second * cosine + first * sine], axis=-1
    )


def combine(first, second):
    top_a, total_a, acc_a = first
    top_b, total_b, acc_b = second
    top = jnp.maximum(top_a, top_b)
    scale_a = jnp.exp(top_a - top)
    scale_b = jnp.exp(top_b - top)
    return (
        top,
        total_a * scale_a + total_b * scale_b,
        acc_a * scale_a[..., None] + acc_b * scale_b[..., None],
    )


def block_partial(queries, keys, values, live, scale):
    scores = (
        jnp.einsum("bhrd,bkhd->bhrk", queries, keys, preferred_element_type=jnp.float32) * scale
    )
    scores = jnp.where(live, scores, NEGATIVE)
    top = jnp.max(scores, axis=-1)
    weights = jnp.where(live, jnp.exp(scores - top[..., None]), 0.0)
    total = jnp.sum(weights, axis=-1)
    acc = jnp.einsum(
        "bhrk,bkhd->bhrd", weights.astype(jnp.bfloat16), values, preferred_element_type=jnp.float32
    )
    return (top, total, acc)


def empty_state(batch, heads, rows, width):
    return (
        jnp.full((batch, heads, rows), NEGATIVE, jnp.float32),
        jnp.zeros((batch, heads, rows), jnp.float32),
        jnp.zeros((batch, heads, rows, width), jnp.float32),
    )


def per_device(hidden_states, norm_gain, prompt_lengths, kv_cache, w_qkv, w_out):
    ctx_count = lax.axis_size("ctx")
    tp_count = lax.axis_size("tp")
    batch = kv_cache.shape[0]
    local_len = kv_cache.shape[1]
    head_dim = HD
    local_heads = kv_cache.shape[3] // (tp_count * head_dim)
    group = GQA
    steps = STEPS
    rows = steps * group
    scale = HD ** (-0.5)
    parts = ctx_count // batch
    piece = local_len // parts
    values_in = hidden_states.astype(jnp.float32)
    square_part = jnp.sum(values_in * values_in, axis=1)
    scaled = (values_in * norm_gain.astype(jnp.float32)).astype(jnp.bfloat16)
    partial_value = jnp.dot(scaled, w_qkv, preferred_element_type=jnp.float32)
    square, proj = lax.psum((square_part, partial_value), "ctx")
    proj = proj * lax.rsqrt(square / D + 1e-05)[:, None]
    proj = proj.reshape(steps, batch, local_heads, group + 2, head_dim)
    step_index = jnp.arange(steps, dtype=jnp.int32)
    positions = prompt_lengths[None, :] + step_index[:, None]
    angle = angles(positions, head_dim)[:, :, None, None, :]
    query = rotate(proj[:, :, :, :group], angle).astype(jnp.bfloat16)
    key_new = rotate(proj[:, :, :, group], angle[:, :, :, 0]).astype(jnp.bfloat16)
    value_new = proj[:, :, :, group + 1].astype(jnp.bfloat16)
    query_rows = jnp.transpose(query, (1, 2, 0, 3, 4)).reshape(batch, local_heads, rows, head_dim)
    split = kv_cache.reshape(batch, parts, piece, 2, tp_count, local_heads, head_dim)
    ordered = jnp.transpose(split, (0, 1, 4, 2, 3, 5, 6))
    moved = ordered.reshape(ctx_count * tp_count, piece, 2, local_heads, head_dim)
    moved = lax.all_to_all(moved, ("ctx", "tp"), split_axis=0, concat_axis=0, tiled=True)
    kv_decode = moved.reshape(1, ctx_count * tp_count, piece, 2, local_heads * head_dim)
    held = moved.reshape(ctx_count * tp_count * piece, 2, local_heads, head_dim)
    held_len = held.shape[0]
    mine = lax.axis_index("ctx") // parts
    part = lax.axis_index("ctx") % parts
    length = lax.dynamic_index_in_dim(prompt_lengths, mine, 0, keepdims=False)
    sources = jnp.arange(ctx_count * tp_count, dtype=jnp.int32)
    live_count = jnp.sum(jnp.clip(length - sources * local_len - part * piece, 0, piece))
    block = min(1024, held_len)
    block_count = (live_count + block - 1) // block
    queries_mine = lax.dynamic_index_in_dim(query_rows, mine, 0, keepdims=True)

    def step_block(index, carry):
        start = index * block
        window = lax.dynamic_slice_in_dim(held, start, block, 0)[None]
        local_index = start + jnp.arange(block, dtype=jnp.int32)
        position = local_index // piece * local_len + part * piece + local_index % piece
        live = (position < length)[None, None, None, :]
        return combine(
            carry, block_partial(queries_mine, window[:, :, 0], window[:, :, 1], live, scale)
        )

    state = lax.fori_loop(0, block_count, step_block, empty_state(1, local_heads, rows, head_dim))
    tops, totals, accs = (
        lax.all_gather(state[0], "ctx", axis=0, tiled=True),
        lax.all_gather(state[1], "ctx", axis=0, tiled=True),
        lax.all_gather(state[2], "ctx", axis=0, tiled=True),
    )
    tops = tops.reshape(batch, parts, local_heads, rows)
    totals = totals.reshape(batch, parts, local_heads, rows)
    accs = accs.reshape(batch, parts, local_heads, rows, head_dim)
    pieces = [(tops[:, index], totals[:, index], accs[:, index]) for index in range(parts)]
    state = reduce(combine, pieces)
    causal = step_index[:, None] >= step_index[None, :]
    causal = jnp.broadcast_to(causal[:, None, :], (steps, group, steps)).reshape(1, 1, rows, steps)
    fresh = block_partial(
        query_rows,
        jnp.transpose(key_new, (1, 0, 2, 3)),
        jnp.transpose(value_new, (1, 0, 2, 3)),
        causal,
        scale,
    )
    top, total, acc = combine(state, fresh)
    attn = acc / total[..., None]
    attn = attn.reshape(batch, local_heads, steps, group, head_dim)
    attn = (
        jnp.transpose(attn, (2, 0, 1, 3, 4))
        .reshape(steps * batch, local_heads * group * head_dim)
        .astype(jnp.bfloat16)
    )
    partial_out = jnp.dot(attn, w_out, preferred_element_type=jnp.float32)
    block_out = lax.psum(partial_out, "tp").astype(jnp.bfloat16)
    return (block_out, kv_decode)


def solution(mesh):
    return jax.shard_map(
        per_device,
        mesh=mesh,
        in_specs=(
            P(None, "ctx"),
            P("ctx"),
            P(),
            P(None, ("ctx", "tp"), None, None),
            P("ctx", "tp"),
            P("tp", "ctx"),
        ),
        out_specs=(P(None, "ctx"), P("ctx", None, None, None, "tp")),
        check_vma=False,
    )
```

profile of v0, /device:TPU:1, one launch (start us, length us, event | category | flops | bytes accessed | tf_op | source)
XLA Modules:
  0.0 274.5 jit_solution(5599802487959281279)
XLA Ops:
  7.2 0.0 copy-start
  7.2 7.7 %reshape.442 = bf16[8,2,64,2,8,1,128]{6,4,3,2,1,0,5:T(8,128)(2,1)} reshape(bf16[8,128,2,1024]{3,2,1,0:T(2,128)(2,1)} %param.11) | data formatting | bytes 8388608 | tf_op jit(solution)/shard_map/reshape | solution.py:109
  14.9 8.7 %copy.34 = bf16[8,2,64,2,8,1,128]{6,3,2,4,1,0,5:T(2,128)(2,1)} copy(bf16[8,2,64,2,8,1,128]{6,4,3,2,1,0,5:T(8,128)(2,1)} %reshape.442) | data formatting | bytes 8388608 | tf_op jit(solution)/shard_map/reshape | solution.py:109
  23.5 0.0 copy-start.3
  23.5 0.0 copy-start.2
  23.5 0.0 copy-start.4
  23.5 12.0 %all-to-all-start = ((bf16[128,64,2,1,128]{4,2,1,3,0:T(2,128)(2,1)}), bf16[128,64,2,1,128]{4,2,1,3,0:T(2,128)(2,1)}, u32[]{:S(2)}, u32[]{:S(2)}) async-start(bf16[128,64,2,1,128]{4,2,1,3,0:T(2,128)(2,1)} %bitcast.139), calls=%async_computation | async-start | bytes 8388608 | tf_op jit(solution)/shard_map/all_to_all | solution.py:112
  35.5 0.0 all-reduce.2.cloned.1.call-start
  35.5 0.0 copy-done.3
  35.6 0.0 copy-done
  35.6 0.0 copy-done.2
  35.6 1.0 fusion.40
  36.6 0.0 all-reduce.2.cloned.1.call-update
  36.6 0.0 copy-done.4
  36.6 0.6 dynamic_slice.14
  37.3 1.3 clamp_reduce_fusion
  39.1 0.1 add_convert_fusion.1
  39.2 0.1 copy.35
  39.3 0.1 broadcast_in_dim.89
  39.4 0.1 broadcast_in_dim.90
  39.5 0.1 fusion.34
  39.6 70.6 %psum.22 = f32[32]{0:T(128)S(1)} all-reduce(f32[32]{0:T(128)S(1)} %fusion.34), channel_id=1, replica_groups=mesh['ctx'=16,'tp'=8] {'ctx'}, use_global_device_ids=true, to_apply=%region_3.4 | all-reduce | flops 32 | bytes 256 | tf_op jit(solution)/shard_map/psum | solution.py:99
  110.2 0.1 multiply_cosine_fusion
  110.4 35.9 %all-reduce.2.cloned.1.call-done = f32[32,1280]{1,0:T(8,128)} async-done(((f32[32,1280]{1,0:T(8,128)}), f32[32,1280]{1,0:T(8,128)}) %all-reduce.2.cloned.1.call-update) | async-done | bytes 163856 | tf_op jit(solution)/shard_map/psum | solution.py:99
  146.3 1.0 multiply_bitcast_fusion
  147.4 0.1 subtract_convert_fusion
  147.5 0.1 maximum_bitcast_fusion
  147.6 0.2 fusion.48
  147.8 0.2 fusion.68
  148.1 0.0 all-to-all-done
  148.1 0.0 copy-start.1
  148.1 8.9 %while.16 = (s32[]{:T(128)}, f32[1,1,32]{2,1,0:T(1,128)S(1)}, f32[1,1,32]{2,1,0:T(1,128)S(1)}, f32[1,1,32,128]{3,2,1,0:T(8,128)S(1)}, s32[]{:T(128)}, /*index=5*...) while((s32[]{:T(128)}, f32[1,1,32]{2,1,0:T(1,128)S(1)}, ...), condition=%wide.region_7.8_spmd, body=%wide.region_4.7_spmd.sunk | while | flops 17109156 | bytes 3063491 | solution.py:135
  148.1 1.5 constant_dynamic-slice_fusion.3
  149.6 0.1 copy.80
  149.7 0.6 fusion.79
  150.4 0.3 fusion.80
  150.7 0.2 fusion.82
  150.9 0.2 fusion.84
  151.2 1.4 constant_dynamic-slice_fusion.3
  152.6 0.1 copy.80
  152.7 0.6 fusion.79
  153.3 0.3 fusion.80
  153.6 0.2 fusion.82
  153.9 0.2 fusion.84
  154.1 1.4 constant_dynamic-slice_fusion.3
  155.5 0.1 copy.80
  155.6 0.6 fusion.79
  156.2 0.3 fusion.80
  156.6 0.2 fusion.82
  156.8 0.2 fusion.84
  157.0 31.4 %all_gather.9 = f32[16,1,32,128]{3,2,1,0:T(8,128)S(1)} all-gather(f32[1,1,32,128]{3,2,1,0:T(8,128)S(1)} %get-tuple-element.125), channel_id=1, replica_groups=mesh['ctx'=16,'tp'=8] {'ctx'}, dimensions={0}, use_global_device_ids=true | all-gather | bytes 278528 | tf_op jit(solution)/shard_map/all_gather | solution.py:139
  188.4 14.5 %all_gather.11 = f32[16,1,32]{2,1,0:T(1,128)S(1)} all-gather(f32[1,1,32]{2,1,0:T(1,128)S(1)} %get-tuple-element.127), channel_id=1, replica_groups=mesh['ctx'=16,'tp'=8] {'ctx'}, dimensions={0}, use_global_device_ids=true | all-gather | bytes 2176 | tf_op jit(solution)/shard_map/all_gather | solution.py:138
  203.0 14.2 %all_gather.10 = f32[16,1,32]{2,1,0:T(1,128)S(1)} all-gather(f32[1,1,32]{2,1,0:T(1,128)S(1)} %get-tuple-element.126), channel_id=1, replica_groups=mesh['ctx'=16,'tp'=8] {'ctx'}, dimensions={0}, use_global_device_ids=true | all-gather | bytes 2176 | tf_op jit(solution)/shard_map/all_gather | solution.py:137
  217.3 0.3 fusion.27
  217.6 0.0 copy-done.1
  217.6 0.3 fusion.35
  217.9 38.1 %psum.23 = bf16[32,512]{1,0:T(8,128)(2,1)} all-reduce(f32[32,512]{1,0:T(8,128)S(1)} %fusion.35), channel_id=1, replica_groups=mesh['ctx'=16,'tp'=8] {'tp'}, use_global_device_ids=true, to_apply=%region_10.11 | all-reduce | flops 16384 | bytes 98304 | tf_op jit(solution)/shard_map/psum | solution.py:164
  256.0 11.6 %copy.95 = bf16[1,128,64,2,128]{4,3,2,1,0:T(2,128)(2,1)} copy(bf16[1,128,64,2,128]{4,3,2,1,0:T(2,128)(2,1)} %bitcast.34) | data formatting | bytes 8388608
  (26 shorter events, 0.2 us)
Async XLA Ops:
  7.2 28.4 %copy-start = (bf16[512,1280]{1,0:T(8,128)(2,1)S(1)}, bf16[512,1280]{1,0:T(8,128)(2,1)}, u32[]{:S(2)}) copy-start(bf16[512,1280]{1,0:T(8,128)(2,1)} %param.12) | copy-start | bytes 3932164
  23.5 12.0 %copy-start.3 = (bf16[512]{0:T(512)(128)(2,1)S(1)}, bf16[512]{0:T(512)(128)(2,1)}, u32[]{:S(2)}) copy-start(bf16[512]{0:T(512)(128)(2,1)} %param.9) | copy-start | bytes 3076
  23.5 12.1 %copy-start.2 = (bf16[32,512]{1,0:T(8,128)(2,1)S(1)}, bf16[32,512]{1,0:T(8,128)(2,1)}, u32[]{:S(2)}) copy-start(bf16[32,512]{1,0:T(8,128)(2,1)} %param.8) | copy-start | bytes 98308
  23.5 13.1 %copy-start.4 = (s32[8]{0:T(128)S(1)}, s32[8]{0:T(128)}, u32[]{:S(2)}) copy-start(s32[8]{0:T(128)} %param.10) | copy-start | bytes 100
  23.5 124.5 %all-to-all-start = ((bf16[128,64,2,1,128]{4,2,1,3,0:T(2,128)(2,1)}), bf16[128,64,2,1,128]{4,2,1,3,0:T(2,128)(2,1)}, u32[]{:S(2)}, u32[]{:S(2)}) async-start(bf16[128,64,2,1,128]{4,2,1,3,0:T(2,128)(2,1)} %bitcast.139), calls=%async_computation | async-start | bytes 8388608 | tf_op jit(solution)/shard_map/all_to_all | solution.py:112
  35.5 110.8 %all-reduce.2.cloned.1.call-start = ((), (), s32[]{:S(2)}) async-start(), calls=%async_computation.1 | async-start | bytes 327680 | tf_op jit(solution)/shard_map/psum | solution.py:99
  148.1 69.5 %copy-start.1 = (bf16[1024,512]{1,0:T(8,128)(2,1)S(1)}, bf16[1024,512]{1,0:T(8,128)(2,1)}, u32[]{:S(2)}) copy-start(bf16[1024,512]{1,0:T(8,128)(2,1)} %param.13) | copy-start | bytes 3145732
Sparse Core Ops, SparseCore 0:
  40.1 106.1 all-reduce.1
where the time goes:
time: 277 us; the launch traced here: 274 us
  blocking collectives  169 us (61%)
  waiting for transfers between devices  36 us (13%)
  local copies, waits for them, and re-layouts  33.5 us (12%)
  between operations  14.9 us (5%)
  starting transfers between devices  12 us (4%)
  other arithmetic  5.66 us (2%)
  matrix products  3.4 us (1%)
    psum x1, blocking collectives, per_device(): square, proj = lax.psum((square_part, partial_value), 'ctx')  70.6 us
    psum x1, blocking collectives, per_device(): block_out = lax.psum(partial_out, 'tp').astype(jnp.bfloat16)  38.1 us
    psum x1, waiting for transfers between devices, per_device(): square, proj = lax.psum((square_part, partial_value), 'ctx')  35.9 us
    all_gather x1, blocking collectives, per_device(): lax.all_gather(state[2], 'ctx', axis=0, tiled=True)  31.4 us
    reshape x2, local copies, waits for them, and re-layouts, per_device(): kv_cache.reshape(batch, parts, piece, 2, tp_count, local_heads, head_dim)  16.3 us
    all_gather x1, blocking collectives, per_device(): lax.all_gather(state[1], 'ctx', axis=0, tiled=True)  14.5 us
    all_gather x1, blocking collectives, per_device(): lax.all_gather(state[0], 'ctx', axis=0, tiled=True)  14.2 us
    all_to_all x1, starting transfers between devices, per_device(): lax.all_to_all(moved, ('ctx', 'tp'), split_axis=0, concat_axis=0, tiled=T...  12 us
  transfers between devices with their start and end apart: 2, of which 1 were waited for; matrix products, arithmetic and copies ran while one was open for 2% of the time, Pallas kernels for 0%

commit v1 on v0

v1 whole, which is shorter than its diff:
```python
import math

import jax
import jax.numpy as jnp
from jax import lax
from jax.experimental import pallas as pl
from jax.experimental.pallas import tpu as pltpu
from jax.sharding import PartitionSpec as P

D = 8192
HD = 128
STEPS = 4
GQA = 8
REQUESTS = 8
SOURCES = 128
PIECE = 64
TP = 8
CTX = 16
HEAD_ROWS = STEPS * GQA

ROPE_BASE = 500000.0
ROPE_FACTOR = 8.0
LOW_FACTOR = 1.0
HIGH_FACTOR = 4.0
ROPE_ANCHOR = 8192.0
NEGATIVE = -1e30
SCALE = HD ** (-0.5)


def angles(positions, width):
    base_freq = ROPE_BASE ** (-(2.0 * jnp.arange(width // 2, dtype=jnp.float32)) / width)
    wavelength = 2.0 * math.pi / base_freq
    blend = (ROPE_ANCHOR / wavelength - LOW_FACTOR) / (HIGH_FACTOR - LOW_FACTOR)
    middle = (1.0 - blend) * base_freq / ROPE_FACTOR + blend * base_freq
    freq = jnp.where(
        wavelength > ROPE_ANCHOR / LOW_FACTOR,
        base_freq / ROPE_FACTOR,
        jnp.where(wavelength < ROPE_ANCHOR / HIGH_FACTOR, base_freq, middle),
    )
    return positions.astype(jnp.float32)[..., None] * freq


COLUMNS = (GQA + 2) * HD
SIDE = 4


def partial_kernel(x_ref, hidden_ref, gain_ref, w_ref, *out_refs):
    rows = STEPS * REQUESTS
    share = rows // SIDE
    target = lax.broadcasted_iota(jnp.int32, (rows, rows), 0)
    origin = lax.broadcasted_iota(jnp.int32, (rows, rows), 1)
    receiver = jnp.bitwise_xor(target // share, x_ref[0])
    request = receiver * (REQUESTS // SIDE) + target % share // STEPS
    moves = jnp.where(origin == target % STEPS * REQUESTS + request, 1.0, 0.0)
    values = jnp.dot(
        moves.astype(jnp.bfloat16), hidden_ref[...], preferred_element_type=jnp.float32
    )
    square = jnp.sum(values * values, axis=1, keepdims=True)
    gain = gain_ref[...].astype(jnp.float32).reshape(1, -1)
    scaled = (values * gain).astype(jnp.bfloat16)
    proj = jnp.dot(scaled, w_ref[...], preferred_element_type=jnp.float32)
    square = jnp.broadcast_to(square, (rows, HD))
    for index, out_ref in enumerate(out_refs):
        out_ref[:, pl.ds(0, COLUMNS)] = proj[index * share:(index + 1) * share]
        out_ref[:, pl.ds(COLUMNS, HD)] = square[index * share:(index + 1) * share]


def partial_projection(x, hidden_states, norm_gain, w_qkv):
    vmem = pl.BlockSpec(memory_space=pltpu.VMEM)
    shape = jax.ShapeDtypeStruct((STEPS * REQUESTS // SIDE, COLUMNS + HD), jnp.float32)
    return pl.pallas_call(
        partial_kernel,
        in_specs=[pl.BlockSpec(memory_space=pltpu.SMEM), vmem, vmem, vmem],
        out_specs=[vmem] * SIDE,
        out_shape=[shape] * SIDE,
        compiler_params=pltpu.CompilerParams(vmem_limit_bytes=8 * 1024 * 1024),
        name="partial_projection",
    )(x.reshape(1), hidden_states, norm_gain, w_qkv)


def swap(value, axis, other):
    pairs = [(index, index ^ other) for index in range(lax.axis_size(axis))]
    return lax.ppermute(value, axis, pairs)


def prep_kernel(kv_ref, out_ref, held, ready, in_sems, head_sems, out_sems):
    def fetch(receiver):
        return pltpu.make_async_copy(
            kv_ref.at[receiver], held.at[receiver // 2], in_sems.at[receiver // 2]
        )

    def fetch_head(receiver, head):
        return pltpu.make_async_copy(
            kv_ref.at[receiver, :, :, pl.ds(head * HD, HD)],
            ready.at[receiver, head],
            head_sems.at[receiver // 2, head],
        )

    def place(receiver):
        return pltpu.make_async_copy(
            ready.at[receiver], out_ref.at[receiver], out_sems.at[receiver]
        )

    for receiver in range(0, CTX, 2):
        fetch(receiver).start()
        for head in range(TP):
            fetch_head(receiver + 1, head).start()
    for receiver in range(0, CTX, 2):
        fetch(receiver).wait()
        for head in range(TP):
            ready[receiver, head] = held[receiver // 2, :, :, pl.ds(head * HD, HD)]
        place(receiver).start()
        for head in range(TP):
            fetch_head(receiver + 1, head).wait()
        place(receiver + 1).start()
    for receiver in range(CTX):
        place(receiver).wait()


def prep(kv_cache):
    split = kv_cache.reshape(CTX, PIECE, 2, TP * HD)
    return pl.pallas_call(
        prep_kernel,
        out_shape=jax.ShapeDtypeStruct((CTX, TP, PIECE, 2, HD), jnp.bfloat16),
        in_specs=[pl.BlockSpec(memory_space=pl.ANY)],
        out_specs=pl.BlockSpec(memory_space=pl.ANY),
        scratch_shapes=[
            pltpu.VMEM((CTX // 2, PIECE, 2, TP * HD), jnp.bfloat16),
            pltpu.VMEM((CTX, TP, PIECE, 2, HD), jnp.bfloat16),
            pltpu.SemaphoreType.DMA((CTX // 2,)),
            pltpu.SemaphoreType.DMA((CTX // 2, TP)),
            pltpu.SemaphoreType.DMA((CTX,)),
        ],
        compiler_params=pltpu.CompilerParams(vmem_limit_bytes=56 * 1024 * 1024),
        cost_estimate=pl.CostEstimate(
            flops=0, transcendentals=0, bytes_accessed=4 * kv_cache.size
        ),
        name="cache_by_receiver",
    )(split)


CHUNKS = 4
CHUNK_CTX = CTX // CHUNKS
CHUNK_SOURCES = SOURCES // CHUNKS
CHUNK_KEYS = CHUNK_SOURCES * PIECE
CHUNK_ROWS = CHUNK_KEYS * 2
STATE_ROWS = HEAD_ROWS + 16


def attend_kernel(
    info_ref, kv_ref, own_ref, first_ref, second_ref, third_ref, cos_ref, sin_ref,
    kv_out_ref, out_ref,
    held, wide, pairs, query, scores, peaks, top, total, acc, in_sems, out_sems,
):
    length = info_ref[0]
    part = info_ref[1]
    left = length - part * PIECE

    def fetch(ctx):
        return pltpu.make_async_copy(kv_ref.at[ctx], held.at[ctx], in_sems.at[ctx])

    def place(ctx):
        return pltpu.make_async_copy(held.at[ctx], kv_out_ref.at[ctx], out_sems.at[ctx])

    for ctx in range(CTX):
        fetch(ctx).start()

    row = lax.broadcasted_iota(jnp.int32, (HEAD_ROWS, HD), 0)
    lane = lax.broadcasted_iota(jnp.int32, (HEAD_ROWS, HD), 1)
    slot = lane // PIECE * (2 * PIECE) + lane % PIECE

    summed = own_ref[...] + first_ref[...] + second_ref[...] + third_ref[...]
    norm = lax.rsqrt(summed[:, COLUMNS:] / D + 1e-05)

    def head(index):
        return summed[:, index * HD:(index + 1) * HD] * norm

    def turn(vec):
        return vec * cos_ref[...] + pltpu.roll(vec, HD // 2, 1) * sin_ref[...]

    query[...] = jnp.concatenate([turn(head(g)) for g in range(GQA)], axis=0).astype(jnp.bfloat16)
    rest = jnp.zeros((HD - STEPS, HD), jnp.float32)
    keys = jnp.concatenate([turn(head(GQA)), rest], axis=0).astype(jnp.bfloat16)
    values = jnp.concatenate([head(GQA + 1), rest], axis=0).astype(jnp.bfloat16)
    fresh = lax.dot_general(
        query[...], keys, (((1,), (1,)), ((), ())), preferred_element_type=jnp.float32
    ) * SCALE
    live = jnp.logical_and(lane <= row % STEPS, part == 0)
    fresh = jnp.where(live, fresh, NEGATIVE)
    high = jnp.max(fresh, axis=1, keepdims=True)
    weight = jnp.where(live, jnp.exp(fresh - high), 0.0)
    top[...] = jnp.broadcast_to(high, (HEAD_ROWS, HD))
    total[...] = weight
    acc[...] = jnp.dot(weight.astype(jnp.bfloat16), values, preferred_element_type=jnp.float32)

    def arrive(chunk):
        for ctx in range(chunk * CHUNK_CTX, (chunk + 1) * CHUNK_CTX):
            fetch(ctx).wait()
            place(ctx).start()

    def score(chunk):
        wide[...] = held[pl.ds(chunk * CHUNK_CTX, CHUNK_CTX)].reshape(CHUNK_ROWS, HD).astype(
            jnp.float32
        )
        for index in range(2):
            pairs[chunk % 2, index] = wide[pl.ds(index, CHUNK_KEYS, stride=2), :].astype(
                jnp.bfloat16
            )
        found = lax.dot_general(
            query[...],
            pairs[chunk % 2, 0],
            (((1,), (1,)), ((), ())),
            preferred_element_type=jnp.float32,
        )
        peak = None
        for index in range(CHUNK_KEYS // HD):
            source = chunk * CHUNK_SOURCES + index * 2
            piece = found[:, index * HD:(index + 1) * HD] * SCALE
            piece = jnp.where(slot < left - source * (2 * PIECE), piece, NEGATIVE)
            scores[chunk % 2, :, pl.ds(index * HD, HD)] = piece
            peak = piece if peak is None else jnp.maximum(peak, piece)
        peaks[chunk % 2] = peak

    def fold(chunk):
        high = jnp.maximum(top[...], jnp.max(peaks[chunk % 2], axis=1, keepdims=True))
        fade = jnp.exp(top[...] - high)
        summed = total[...] * fade
        pieces = []
        for index in range(CHUNK_KEYS // HD):
            weight = jnp.exp(scores[chunk % 2, :, pl.ds(index * HD, HD)] - high)
            summed = summed + weight
            pieces.append(weight.astype(jnp.bfloat16))
        top[...] = high
        total[...] = summed
        acc[...] = acc[...] * fade + jnp.dot(
            jnp.concatenate(pieces, axis=1),
            pairs[chunk % 2, 1],
            preferred_element_type=jnp.float32,
        )

    arrive(0)

    @pl.when(left > 0)
    def _():
        score(0)

    for chunk in range(CHUNKS):
        if chunk + 1 < CHUNKS:
            arrive(chunk + 1)

        @pl.when(chunk * CHUNK_SOURCES * 2 * PIECE < left)
        def _(chunk=chunk):
            if chunk + 1 < CHUNKS:
                score(chunk + 1)
            fold(chunk)

    count = jnp.sum(total[...], axis=1, keepdims=True)
    some = count > 0.0
    safe = jnp.where(some, count, 1.0)
    out_ref[pl.ds(0, HEAD_ROWS), :] = (acc[...] / safe).astype(jnp.bfloat16)
    level = jnp.where(some, top[...] + jnp.log(safe), NEGATIVE)
    level = jnp.sum(jnp.where(row == lane, level, 0.0), axis=0, keepdims=True)
    first = level.astype(jnp.bfloat16).astype(jnp.float32)
    second = (level - first).astype(jnp.bfloat16).astype(jnp.float32)
    third = level - first - second
    place_in = lax.broadcasted_iota(jnp.int32, (16, HD), 0)
    parts = jnp.where(place_in == 0, first, jnp.where(place_in == 1, second, third))
    out_ref[pl.ds(HEAD_ROWS, 16), :] = parts.astype(jnp.bfloat16)

    for ctx in range(CTX):
        place(ctx).wait()


def attend(info, moved, sums, cosine, sine):
    anywhere = pl.BlockSpec(memory_space=pl.ANY)
    vmem = pl.BlockSpec(memory_space=pltpu.VMEM)
    return pl.pallas_call(
        attend_kernel,
        in_specs=[pl.BlockSpec(memory_space=pltpu.SMEM), anywhere] + [vmem] * 6,
        out_specs=[anywhere, vmem],
        scratch_shapes=[
            pltpu.VMEM((CTX, TP, 2 * PIECE, HD), jnp.bfloat16),
            pltpu.VMEM((CHUNK_ROWS, HD), jnp.float32),
            pltpu.VMEM((2, 2, CHUNK_KEYS, HD), jnp.bfloat16),
            pltpu.VMEM((HEAD_ROWS, HD), jnp.bfloat16),
            pltpu.VMEM((2, HEAD_ROWS, CHUNK_KEYS), jnp.float32),
            pltpu.VMEM((2, HEAD_ROWS, HD), jnp.float32),
            pltpu.VMEM((HEAD_ROWS, HD), jnp.float32),
            pltpu.VMEM((HEAD_ROWS, HD), jnp.float32),
            pltpu.VMEM((HEAD_ROWS, HD), jnp.float32),
            pltpu.SemaphoreType.DMA((CTX,)),
            pltpu.SemaphoreType.DMA((CTX,)),
        ],
        out_shape=[
            jax.ShapeDtypeStruct((CTX, TP, 2 * PIECE, HD), jnp.bfloat16),
            jax.ShapeDtypeStruct((STATE_ROWS, HD), jnp.bfloat16),
        ],
        compiler_params=pltpu.CompilerParams(vmem_limit_bytes=24 * 1024 * 1024),
        name="attend",
    )(info, moved, *sums, cosine, sine)


def project_kernel(own_states_ref, mate_states_ref, own_ref, mate_ref, out_ref):
    row = lax.broadcasted_iota(jnp.int32, (HEAD_ROWS, HD), 0)
    lane = lax.broadcasted_iota(jnp.int32, (HEAD_ROWS, HD), 1)
    many = REQUESTS * HEAD_ROWS
    target = lax.broadcasted_iota(jnp.int32, (many, many), 0)
    origin = lax.broadcasted_iota(jnp.int32, (many, many), 1)
    head = target // (STEPS * REQUESTS)
    step = target // REQUESTS % STEPS
    request = target % REQUESTS
    moves = jnp.where(origin == request * HEAD_ROWS + head * STEPS + step, 1.0, 0.0)
    moves = moves.astype(jnp.bfloat16)
    totals = []
    for states_ref, w_ref in ((own_states_ref, own_ref), (mate_states_ref, mate_ref)):
        rows = []
        for request in range(REQUESTS):
            spots = [2 * request + part for part in range(2)]
            levels = []
            for spot in spots:
                coded = states_ref[spot, pl.ds(HEAD_ROWS, 16), :].astype(jnp.float32)
                level = coded[0:1] + coded[1:2] + coded[2:3]
                levels.append(jnp.sum(jnp.where(row == lane, level, 0.0), axis=1, keepdims=True))
            high = jnp.maximum(levels[0], levels[1])
            shares = [jnp.exp(level - high) for level in levels]
            whole = shares[0] + shares[1]
            mixed = sum(
                states_ref[spot, pl.ds(0, HEAD_ROWS), :].astype(jnp.float32) * (share / whole)
                for spot, share in zip(spots, shares)
            )
            rows.append(mixed.astype(jnp.bfloat16))
        attn = jnp.dot(
            moves, jnp.concatenate(rows, axis=0), preferred_element_type=jnp.float32
        ).astype(jnp.bfloat16)
        total = jnp.zeros(out_ref.shape, jnp.float32)
        for index in range(GQA):
            total = total + jnp.dot(
                attn[index * HEAD_ROWS:(index + 1) * HEAD_ROWS],
                w_ref[pl.ds(index * HD, HD), :],
                preferred_element_type=jnp.float32,
            )
        totals.append(total)
    out_ref[...] = (totals[0] + totals[1]).astype(jnp.bfloat16)


def project(states, mate_states, w_own, w_mate):
    vmem = pl.BlockSpec(memory_space=pltpu.VMEM)
    return pl.pallas_call(
        project_kernel,
        in_specs=[vmem] * 4,
        out_specs=vmem,
        out_shape=jax.ShapeDtypeStruct((STEPS * REQUESTS, w_own.shape[1]), jnp.bfloat16),
        compiler_params=pltpu.CompilerParams(vmem_limit_bytes=8 * 1024 * 1024),
        name="project",
    )(states, mate_states, w_own, w_mate)


def per_device(hidden_states, norm_gain, prompt_lengths, kv_cache, w_qkv, w_out):
    x = lax.axis_index("x")
    y = lax.axis_index("y")
    mine = x * (REQUESTS // SIDE) + y // 2
    part = y % 2
    length = lax.dynamic_index_in_dim(prompt_lengths, mine, 0, keepdims=False)

    ready = prep(kv_cache).reshape(CTX * TP, 2 * PIECE, HD)
    everyone = ("x", "y", "z", "core")
    moved = lax.all_to_all(ready, everyone, split_axis=0, concat_axis=0, tiled=True)
    moved = moved.reshape(CTX, TP, 2 * PIECE, HD)

    _, hidden_states = lax.optimization_barrier((ready, hidden_states))
    packed = partial_projection(x, hidden_states, norm_gain, w_qkv)
    packed, w_out = lax.optimization_barrier((packed, w_out))
    along_x = packed[0] + sum(swap(packed[k], "x", k) for k in range(1, SIDE))
    w_mate = swap(w_out, "core", 1)
    along_x = along_x.reshape(2, STEPS, COLUMNS + HD)
    own = lax.dynamic_index_in_dim(along_x, y // 2, 0, keepdims=False)
    far = lax.dynamic_index_in_dim(along_x, 1 - y // 2, 0, keepdims=False)
    sums = [own, swap(own, "y", 1), swap(far, "y", 2), swap(far, "y", 3)]

    angle = angles(length + jnp.arange(STEPS, dtype=jnp.int32), HD)
    cosine = jnp.cos(angle)
    sine = jnp.sin(angle)
    cosine = jnp.concatenate([cosine, cosine], axis=1)
    sine = jnp.concatenate([-sine, sine], axis=1)
    info = jnp.stack([length, part]).astype(jnp.int32)
    kv_decode, state = attend(info, moved, sums, cosine, sine)
    kv_decode = kv_decode.reshape(1, SOURCES, PIECE, 2, HD)

    states = jnp.broadcast_to(state[None], (CTX, STATE_ROWS, HD))
    states = lax.all_to_all(states, ("x", "y"), split_axis=0, concat_axis=0, tiled=True)
    out = project(states, swap(states, "core", 1), w_out, w_mate)
    terms = [out] + [swap(out, "z", other) for other in range(1, SIDE)]
    terms = [term.astype(jnp.float32) for term in terms]
    block_out = ((terms[0] + terms[1]) + (terms[2] + terms[3])).astype(jnp.bfloat16)
    return (block_out, kv_decode)


def solution(mesh):
    fine = jax.sharding.Mesh(
        mesh.devices.reshape(SIDE, SIDE, SIDE, 2), ("x", "y", "z", "core")
    )
    ctx, tp = ("x", "y"), ("z", "core")
    return jax.shard_map(
        per_device,
        mesh=fine,
        in_specs=(
            P(None, ctx),
            P(ctx),
            P(),
            P(None, ctx + tp, None, None),
            P(ctx, tp),
            P(tp, ctx),
        ),
        out_specs=(P(None, ctx), P(ctx, None, None, None, tp)),
        check_vma=False,
    )
```

time: 277 us -> 103 us (0.37)
  blocking collectives: 169 us -> 10.2 us
  local copies, waits for them, and re-layouts: 33.5 us -> 0.76 us
  starting transfers between devices: 12 us -> 29 us
  between operations: 14.9 us -> 0.77 us
  waiting for transfers between devices: 36 us -> 48.8 us
  Pallas kernels: 0 us -> 10.8 us
  matrix products: 3.4 us -> 0 us
  other arithmetic: 5.66 us -> 2.33 us
    psum x2 -> x0, blocking collectives: 109 us -> none  [the longest x1 70.6 us: per_device(): square, proj = lax.psum((square_part, partial_value), 'ctx')]
    all_gather x3 -> x0, blocking collectives: 60.2 us -> none  [the longest x1 31.4 us: per_device(): lax.all_gather(state[2], 'ctx', axis=0, tiled=True)]
    ppermute x0 -> x11, waiting for transfers between devices: none -> 48.8 us  [swap(): return lax.ppermute(value, axis, pairs)]
    psum x1 -> x0, waiting for transfers between devices: 35.9 us -> none  [per_device(): square, proj = lax.psum((square_part, partial_value), 'ctx')]
    ppermute x0 -> x11, starting transfers between devices: none -> 17 us  [swap(): return lax.ppermute(value, axis, pairs)]
    reshape x2 -> x1, local copies, waits for them, and re-layouts: 16.3 us -> 0.02 us  [per_device(): along_x = along_x.reshape(2, STEPS, COLUMNS + HD)]
    unnamed x12 -> x10, local copies, waits for them, and re-layouts: 11.7 us -> 0.03 us
    pallas_call x0 -> x4, Pallas kernels: none -> 10.8 us  [the longest x1 4.74 us: prep(): pl.pallas_call(prep_kernel, out_shape=jax.ShapeDtypeStruct((CTX, TP, PIEC...]
  transfers between devices with their start and end apart: 2 -> 12, of which waited for: 1 -> 7; matrix products, arithmetic and copies ran while one was open for 2% -> 2% of each run, Pallas kernels for 0% -> 5%
where the time goes in v1:
time: 103 us
  waiting for transfers between devices  48.8 us (47%)
  starting transfers between devices  29 us (28%)
  Pallas kernels  10.8 us (10%)
  blocking collectives  10.2 us (10%)
  other arithmetic  2.33 us (2%)
    ppermute x11, waiting for transfers between devices, swap(): return lax.ppermute(value, axis, pairs)  48.8 us
    ppermute x11, starting transfers between devices, swap(): return lax.ppermute(value, axis, pairs)  17 us
    all_to_all x1, starting transfers between devices, per_device(): lax.all_to_all(ready, everyone, split_axis=0, concat_axis=0, tiled=True)  12 us
    all_to_all x1, blocking collectives, per_device(): lax.all_to_all(states, ('x', 'y'), split_axis=0, concat_axis=0, tiled=True)  10.2 us
    pallas_call x1, Pallas kernels, prep(): pl.pallas_call(prep_kernel, out_shape=jax.ShapeDtypeStruct((CTX, TP, PIEC...  4.74 us
    pallas_call x1, Pallas kernels, attend(): pl.pallas_call(attend_kernel, in_specs=[pl.BlockSpec(memory_space=pltpu.S...  4.67 us
  transfers between devices with their start and end apart: 12, of which 7 were waited for; matrix products, arithmetic and copies ran while one was open for 2% of the time, Pallas kernels for 5%

profile of v1, /device:TPU:1, one launch (start us, length us, event | category | flops | bytes accessed | tf_op | source)
XLA Modules:
  0.0 102.7 jit_solution(7533110151761708516)
XLA Ops:
  0.6 4.7 %cache_by_receiver.1 = bf16[16,8,64,2,128]{4,3,2,1,0:T(2,128)(2,1)} custom-call(bf16[16,64,2,1024]{3,2,1,0:T(2,128)(2,1)} %bitcast.12), custom_call_target="tpu_custom_call" | custom-call | bytes 8388608 | tf_op jit(solution)/shard_map/cache_by_receiver/pallas_call | solution.py:122
  5.4 0.0 copy-start
  5.4 0.0 copy-start.2
  5.4 0.0 copy-start.3
  5.4 0.0 copy-start.1
  5.4 0.0 copy-start.4
  5.4 12.0 %all-to-all-start = ((bf16[128,128,128]{2,1,0:T(8,128)(2,1)}), bf16[128,128,128]{2,1,0:T(8,128)(2,1)}, u32[]{:S(2)}, u32[]{:S(2)}) async-start(bf16[128,128,128]{2,1,0:T(8,128)(2,1)} %bitcast.11), calls=%async_computation | async-start | bytes 8388608 | tf_op jit(solution)/shard_map/all_to_all | solution.py:367
  17.4 0.0 copy-done
  17.4 0.0 copy-done.2
  17.4 0.0 copy-done.3
  17.4 0.4 partial_projection.1
  17.9 1.4 %collective-permute-start = (f32[8,1408]{1,0:T(8,128)S(1)}, f32[8,1408]{1,0:T(8,128)S(1)}, u32[]{:S(2)}, u32[]{:S(2)}) collective-permute-start(f32[8,1408]{1,0:T(8,128)S(1)} %get-tuple-element.20), channel_id=1, source_target_pairs={{0,32},{32,0},{64,96},{96,64},{1,33},{33,1},{65,97},{97,65},{2,34}... | collective-permute-start | bytes 135176 | tf_op jit(solution)/shard_map/ppermute | solution.py:83
  19.3 2.4 %collective-permute-start.1 = (f32[8,1408]{1,0:T(8,128)S(1)}, f32[8,1408]{1,0:T(8,128)S(1)}, u32[]{:S(2)}, u32[]{:S(2)}) collective-permute-start(f32[8,1408]{1,0:T(8,128)S(1)} %get-tuple-element.21), channel_id=1, source_target_pairs={{0,64},{32,96},{64,0},{96,32},{1,65},{33,97},{65,1},{97,33},{2,66}... | collective-permute-start | bytes 135176 | tf_op jit(solution)/shard_map/ppermute | solution.py:83
  21.7 0.1 collective-permute-start.2
  21.7 0.0 copy-done.1
  21.8 2.0 %collective-permute-start.7 = (bf16[1024,512]{1,0:T(8,128)(2,1)S(1)}, bf16[1024,512]{1,0:T(8,128)(2,1)S(1)}, u32[]{:S(2)}, u32[]{:S(2)}) collective-permute-start(bf16[1024,512]{1,0:T(8,128)(2,1)S(1)} %copy-done.1), channel_id=1, source_target_pairs={{0,1},{1,0},{2,3},{3,2},{4,5},{5,4},{6,7},{7,6},{8,9},{9,8},{10,11... | collective-permute-start | bytes 3145736 | tf_op jit(solution)/shard_map/ppermute | solution.py:83
  23.7 0.0 copy-done.4
  23.7 0.7 dynamic_slice.11
  24.4 0.7 add_convert_fusion.1
  25.1 0.1 fusion
  25.2 0.1 pad_maximum_fusion
  25.3 39.1 %collective-permute-done = f32[8,1408]{1,0:T(8,128)S(1)} collective-permute-done((f32[8,1408]{1,0:T(8,128)S(1)}, f32[8,1408]{1,0:T(8,128)S(1)}, u32[]{:S(2)}, u32[]{:S(2)}) %collective-permute-start) | collective-permute-done | bytes 45088 | tf_op jit(solution)/shard_map/ppermute | solution.py:83
  64.5 2.5 %collective-permute-done.1 = f32[8,1408]{1,0:T(8,128)S(1)} collective-permute-done((f32[8,1408]{1,0:T(8,128)S(1)}, f32[8,1408]{1,0:T(8,128)S(1)}, u32[]{:S(2)}, u32[]{:S(2)}) %collective-permute-start.1) | collective-permute-done | bytes 45088 | tf_op jit(solution)/shard_map/ppermute | solution.py:83
  66.9 0.0 collective-permute-done.2
  67.0 2.5 %collective-permute-start.5 = (f32[4,1408]{1,0:T(4,128)S(1)}, f32[4,1408]{1,0:T(4,128)S(1)}, u32[]{:S(2)}, u32[]{:S(2)}) collective-permute-start(f32[4,1408]{1,0:T(4,128)S(1)} %get-tuple-element.26), channel_id=1, source_target_pairs={{0,24},{8,16},{16,8},{24,0},{1,25},{9,17},{17,9},{25,1},{2,26},{10... | collective-permute-start | bytes 67592 | tf_op jit(solution)/shard_map/ppermute | solution.py:83
  69.4 0.5 collective-permute-start.4
  69.9 0.4 collective-permute-start.3
  70.3 0.8 pad_add_fusion.info_ref
  71.1 0.2 collective-permute-done.5.third_ref
  71.3 2.3 %collective-permute-done.4.second_ref = f32[4,1408]{1,0:T(4,128)S(1)} collective-permute-done((f32[4,1408]{1,0:T(4,128)S(1)}, f32[4,1408]{1,0:T(4,128)S(1)}, u32[]{:S(2)}, u32[]{:S(2)}) %collective-permute-start.4) | collective-permute-done | bytes 22560 | tf_op jit(solution)/shard_map/ppermute | solution.py:83
  73.6 0.0 collective-permute-done.3.first_ref
  73.6 0.0 all-to-all-done
  73.6 4.7 %attend.1 = (bf16[16,8,128,128]{3,2,1,0:T(8,128)(2,1)}, bf16[48,128]{1,0:T(8,128)(2,1)S(1)}) custom-call(s32[2]{0:T(128)S(1)} %pad_add_fusion.info_ref, bf16[16,8,128,128]{3,2,1,0:T(8,128)(2,1)} %bitcast.3.kv_ref, f32[4,1408]{1,0:T(4,128)S(1)} %get-tuple-element.27.own_ref, f32[4,1408]{1,0:T(4,128)S(1)} %collective-permute-done.3.first_ref, ...), custom_call_target="tpu_custom_call" | custom-call | tf_op jit(solution)/shard_map/attend/pallas_call | solution.py:277
  78.3 10.2 %all_to_all.10.own_states_ref = bf16[16,48,128]{2,1,0:T(8,128)(2,1)S(1)} all-to-all(bf16[16,48,128]{2,1,0:T(8,128)(2,1)S(1)} %broadcast_in_dim.2), channel_id=1, replica_groups=mesh['x'=4,'y'=4,'z'=4,'core'=2] {'x','y'}, dimensions={0} | all-to-all | bytes 393216 | tf_op jit(solution)/shard_map/all_to_all | solution.py:390
  88.5 3.9 %collective-permute-start.6 = (bf16[16,48,128]{2,1,0:T(8,128)(2,1)S(1)}, bf16[16,48,128]{2,1,0:T(8,128)(2,1)S(1)}, u32[]{:S(2)}, u32[]{:S(2)}) collective-permute-start(bf16[16,48,128]{2,1,0:T(8,128)(2,1)S(1)} %all_to_all.10.own_states_ref), channel_id=1, source_target_pairs={{0,1},{1,0},{2,3},{3,2},{4,5},{5,4},{6,7},{7,6},{8,9},{9,8},{10,11... | collective-permute-start | bytes 589832 | tf_op jit(solution)/shard_map/ppermute | solution.py:83
  92.5 0.0 collective-permute-done.7.mate_ref
  92.5 1.1 %collective-permute-done.6.mate_states_ref = bf16[16,48,128]{2,1,0:T(8,128)(2,1)S(1)} collective-permute-done((bf16[16,48,128]{2,1,0:T(8,128)(2,1)S(1)}, bf16[16,48,128]{2,1,0:T(8,128)(2,1)S(1)}, u32[]{:S(2)}, u32[]{:S(2)}) %collective-permute-start.6) | collective-permute-done | bytes 196640 | tf_op jit(solution)/shard_map/ppermute | solution.py:83
  93.5 1.0 project.1
  94.5 3.3 %collective-permute-start.10 = (bf16[32,512]{1,0:T(8,128)(2,1)S(1)}, bf16[32,512]{1,0:T(8,128)(2,1)S(1)}, u32[]{:S(2)}, u32[]{:S(2)}) collective-permute-start(bf16[32,512]{1,0:T(8,128)(2,1)S(1)} %project.1), channel_id=1, source_target_pairs={{0,6},{2,4},{4,2},{6,0},{1,7},{3,5},{5,3},{7,1},{8,14},{10,12},{12... | collective-permute-start | bytes 98312 | tf_op jit(solution)/shard_map/ppermute | solution.py:83
  97.8 0.1 collective-permute-start.9
  97.9 0.6 collective-permute-start.8
  98.5 0.6 collective-permute-done.10
  99.1 3.0 %collective-permute-done.9 = bf16[32,512]{1,0:T(8,128)(2,1)S(1)} collective-permute-done((bf16[32,512]{1,0:T(8,128)(2,1)S(1)}, bf16[32,512]{1,0:T(8,128)(2,1)S(1)}, u32[]{:S(2)}, u32[]{:S(2)}) %collective-permute-start.9) | collective-permute-done | bytes 32800 | tf_op jit(solution)/shard_map/ppermute | solution.py:83
  102.0 0.0 collective-permute-done.8
  102.1 0.6 add_convert_fusion
  (5 shorter events, 0.1 us)
Async XLA Ops:
  5.4 12.0 %copy-start = (bf16[512,1280]{1,0:T(8,128)(2,1)S(1)}, bf16[512,1280]{1,0:T(8,128)(2,1)}, u32[]{:S(2)}) copy-start(bf16[512,1280]{1,0:T(8,128)(2,1)} %w_ref.1) | copy-start | bytes 3932164
  5.4 12.0 %copy-start.2 = (bf16[32,512]{1,0:T(8,128)(2,1)S(1)}, bf16[32,512]{1,0:T(8,128)(2,1)}, u32[]{:S(2)}) copy-start(bf16[32,512]{1,0:T(8,128)(2,1)} %hidden_ref) | copy-start | bytes 98308
  5.4 12.0 %copy-start.3 = (bf16[512]{0:T(512)(128)(2,1)S(1)}, bf16[512]{0:T(512)(128)(2,1)}, u32[]{:S(2)}) copy-start(bf16[512]{0:T(512)(128)(2,1)} %gain_ref.1) | copy-start | bytes 3076
  5.4 16.3 %copy-start.1 = (bf16[1024,512]{1,0:T(8,128)(2,1)S(1)}, bf16[1024,512]{1,0:T(8,128)(2,1)}, u32[]{:S(2)}) copy-start(bf16[1024,512]{1,0:T(8,128)(2,1)} %own_ref) | copy-start | bytes 3145732
  5.4 18.3 %copy-start.4 = (s32[8]{0:T(128)S(1)}, s32[8]{0:T(128)}, u32[]{:S(2)}) copy-start(s32[8]{0:T(128)} %param.8) | copy-start | bytes 100
  5.4 68.2 %all-to-all-start = ((bf16[128,128,128]{2,1,0:T(8,128)(2,1)}), bf16[128,128,128]{2,1,0:T(8,128)(2,1)}, u32[]{:S(2)}, u32[]{:S(2)}) async-start(bf16[128,128,128]{2,1,0:T(8,128)(2,1)} %bitcast.11), calls=%async_computation | async-start | bytes 8388608 | tf_op jit(solution)/shard_map/all_to_all | solution.py:367
  17.9 46.6 %collective-permute-start = (f32[8,1408]{1,0:T(8,128)S(1)}, f32[8,1408]{1,0:T(8,128)S(1)}, u32[]{:S(2)}, u32[]{:S(2)}) collective-permute-start(f32[8,1408]{1,0:T(8,128)S(1)} %get-tuple-element.20), channel_id=1, source_target_pairs={{0,32},{32,0},{64,96},{96,64},{1,33},{33,1},{65,97},{97,65},{2,34}... | collective-permute-start | bytes 135176 | tf_op jit(solution)/shard_map/ppermute | solution.py:83
  19.3 47.7 %collective-permute-start.1 = (f32[8,1408]{1,0:T(8,128)S(1)}, f32[8,1408]{1,0:T(8,128)S(1)}, u32[]{:S(2)}, u32[]{:S(2)}) collective-permute-start(f32[8,1408]{1,0:T(8,128)S(1)} %get-tuple-element.21), channel_id=1, source_target_pairs={{0,64},{32,96},{64,0},{96,32},{1,65},{33,97},{65,1},{97,33},{2,66}... | collective-permute-start | bytes 135176 | tf_op jit(solution)/shard_map/ppermute | solution.py:83
  21.7 45.3 %collective-permute-start.2 = (f32[8,1408]{1,0:T(8,128)S(1)}, f32[8,1408]{1,0:T(8,128)S(1)}, u32[]{:S(2)}, u32[]{:S(2)}) collective-permute-start(f32[8,1408]{1,0:T(8,128)S(1)} %get-tuple-element.22), channel_id=1, source_target_pairs={{0,96},{32,64},{64,32},{96,0},{1,97},{33,65},{65,33},{97,1},{2,98}... | collective-permute-start | bytes 135176 | tf_op jit(solution)/shard_map/ppermute | solution.py:83
  21.8 70.7 %collective-permute-start.7 = (bf16[1024,512]{1,0:T(8,128)(2,1)S(1)}, bf16[1024,512]{1,0:T(8,128)(2,1)S(1)}, u32[]{:S(2)}, u32[]{:S(2)}) collective-permute-start(bf16[1024,512]{1,0:T(8,128)(2,1)S(1)} %copy-done.1), channel_id=1, source_target_pairs={{0,1},{1,0},{2,3},{3,2},{4,5},{5,4},{6,7},{7,6},{8,9},{9,8},{10,11... | collective-permute-start | bytes 3145736 | tf_op jit(solution)/shard_map/ppermute | solution.py:83
  67.0 4.3 %collective-permute-start.5 = (f32[4,1408]{1,0:T(4,128)S(1)}, f32[4,1408]{1,0:T(4,128)S(1)}, u32[]{:S(2)}, u32[]{:S(2)}) collective-permute-start(f32[4,1408]{1,0:T(4,128)S(1)} %get-tuple-element.26), channel_id=1, source_target_pairs={{0,24},{8,16},{16,8},{24,0},{1,25},{9,17},{17,9},{25,1},{2,26},{10... | collective-permute-start | bytes 67592 | tf_op jit(solution)/shard_map/ppermute | solution.py:83
  69.4 4.2 %collective-permute-start.4 = (f32[4,1408]{1,0:T(4,128)S(1)}, f32[4,1408]{1,0:T(4,128)S(1)}, u32[]{:S(2)}, u32[]{:S(2)}) collective-permute-start(f32[4,1408]{1,0:T(4,128)S(1)} %get-tuple-element.26), channel_id=1, source_target_pairs={{0,16},{8,24},{16,0},{24,8},{1,17},{9,25},{17,1},{25,9},{2,18},{10... | collective-permute-start | bytes 67592 | tf_op jit(solution)/shard_map/ppermute | solution.py:83
  69.9 3.7 %collective-permute-start.3 = (f32[4,1408]{1,0:T(4,128)S(1)}, f32[4,1408]{1,0:T(4,128)S(1)}, u32[]{:S(2)}, u32[]{:S(2)}) collective-permute-start(f32[4,1408]{1,0:T(4,128)S(1)} %get-tuple-element.27.own_ref), channel_id=1, source_target_pairs={{0,8},{8,0},{16,24},{24,16},{1,9},{9,1},{17,25},{25,17},{2,10},{10... | collective-permute-start | bytes 67592 | tf_op jit(solution)/shard_map/ppermute | solution.py:83
  88.5 5.0 %collective-permute-start.6 = (bf16[16,48,128]{2,1,0:T(8,128)(2,1)S(1)}, bf16[16,48,128]{2,1,0:T(8,128)(2,1)S(1)}, u32[]{:S(2)}, u32[]{:S(2)}) collective-permute-start(bf16[16,48,128]{2,1,0:T(8,128)(2,1)S(1)} %all_to_all.10.own_states_ref), channel_id=1, source_target_pairs={{0,1},{1,0},{2,3},{3,2},{4,5},{5,4},{6,7},{7,6},{8,9},{9,8},{10,11... | collective-permute-start | bytes 589832 | tf_op jit(solution)/shard_map/ppermute | solution.py:83
  94.5 4.6 %collective-permute-start.10 = (bf16[32,512]{1,0:T(8,128)(2,1)S(1)}, bf16[32,512]{1,0:T(8,128)(2,1)S(1)}, u32[]{:S(2)}, u32[]{:S(2)}) collective-permute-start(bf16[32,512]{1,0:T(8,128)(2,1)S(1)} %project.1), channel_id=1, source_target_pairs={{0,6},{2,4},{4,2},{6,0},{1,7},{3,5},{5,3},{7,1},{8,14},{10,12},{12... | collective-permute-start | bytes 98312 | tf_op jit(solution)/shard_map/ppermute | solution.py:83
  97.8 4.3 %collective-permute-start.9 = (bf16[32,512]{1,0:T(8,128)(2,1)S(1)}, bf16[32,512]{1,0:T(8,128)(2,1)S(1)}, u32[]{:S(2)}, u32[]{:S(2)}) collective-permute-start(bf16[32,512]{1,0:T(8,128)(2,1)S(1)} %project.1), channel_id=1, source_target_pairs={{0,4},{2,6},{4,0},{6,2},{1,5},{3,7},{5,1},{7,3},{8,12},{10,14},{12... | collective-permute-start | bytes 98312 | tf_op jit(solution)/shard_map/ppermute | solution.py:83
  97.9 4.2 %collective-permute-start.8 = (bf16[32,512]{1,0:T(8,128)(2,1)S(1)}, bf16[32,512]{1,0:T(8,128)(2,1)S(1)}, u32[]{:S(2)}, u32[]{:S(2)}) collective-permute-start(bf16[32,512]{1,0:T(8,128)(2,1)S(1)} %project.1), channel_id=1, source_target_pairs={{0,2},{2,0},{4,6},{6,4},{1,3},{3,1},{5,7},{7,5},{8,10},{10,8},{12,... | collective-permute-start | bytes 98312 | tf_op jit(solution)/shard_map/ppermute | solution.py:83

commit v2 on v1

--- a/solution.py
+++ b/solution.py
@@ -389,9 +389,15 @@
     states = jnp.broadcast_to(state[None], (CTX, STATE_ROWS, HD))
     states = lax.all_to_all(states, ("x", "y"), split_axis=0, concat_axis=0, tiled=True)
     out = project(states, swap(states, "core", 1), w_out, w_mate)
-    terms = [out] + [swap(out, "z", other) for other in range(1, SIDE)]
-    terms = [term.astype(jnp.float32) for term in terms]
-    block_out = ((terms[0] + terms[1]) + (terms[2] + terms[3])).astype(jnp.bfloat16)
+    pairs = [(z * 2 + c, (z ^ (1 + 2 * c)) * 2 + c) for z in range(SIDE) for c in range(2)]
+    near = lax.ppermute(out, ("z", "core"), pairs)
+    across = swap(out, "z", 2)
+    shared = swap(near, "core", 1)
+    first = lax.axis_index("core") == 0
+    one = jnp.where(first, near, shared).astype(jnp.float32)
+    three = jnp.where(first, shared, near).astype(jnp.float32)
+    block_out = (out.astype(jnp.float32) + one) + (across.astype(jnp.float32) + three)
+    block_out = block_out.astype(jnp.bfloat16)
     return (block_out, kv_decode)
 
 

time: 103 us -> 103 us (level)
    ppermute x0 -> x1, starting transfers between devices: none -> 3.28 us  [per_device(): near = lax.ppermute(out, ('z', 'core'), pairs)]
    ppermute x11 -> x10, starting transfers between devices: 17 us -> 14 us  [swap(): return lax.ppermute(value, axis, pairs)]
    ppermute x11 -> x10, waiting for transfers between devices: 48.8 us -> 47.4 us  [swap(): return lax.ppermute(value, axis, pairs)]
    ppermute x0 -> x1, waiting for transfers between devices: none -> 1.18 us  [per_device(): near = lax.ppermute(out, ('z', 'core'), pairs)]
where the time goes in v2:
time: 103 us
  waiting for transfers between devices  48.5 us (47%)
  starting transfers between devices  29.3 us (28%)
  blocking collectives  10.6 us (10%)
  Pallas kernels  10.5 us (10%)
  other arithmetic  2.33 us (2%)
    ppermute x10, waiting for transfers between devices, swap(): return lax.ppermute(value, axis, pairs)  47.4 us
    ppermute x10, starting transfers between devices, swap(): return lax.ppermute(value, axis, pairs)  14 us
    all_to_all x1, starting transfers between devices, per_device(): lax.all_to_all(ready, everyone, split_axis=0, concat_axis=0, tiled=True)  12 us
    all_to_all x1, blocking collectives, per_device(): lax.all_to_all(states, ('x', 'y'), split_axis=0, concat_axis=0, tiled=True)  10.6 us
    pallas_call x1, Pallas kernels, prep(): pl.pallas_call(prep_kernel, out_shape=jax.ShapeDtypeStruct((CTX, TP, PIEC...  4.74 us
    pallas_call x1, Pallas kernels, attend(): pl.pallas_call(attend_kernel, in_specs=[pl.BlockSpec(memory_space=pltpu.S...  4.38 us
    ppermute x1, starting transfers between devices, per_device(): near = lax.ppermute(out, ('z', 'core'), pairs)  3.28 us
  transfers between devices with their start and end apart: 12, of which 7 were waited for; matrix products, arithmetic and copies ran while one was open for 2% of the time, Pallas kernels for 5%

profile of v2, /device:TPU:1, one launch (start us, length us, event | category | flops | bytes accessed | tf_op | source)
XLA Modules:
  0.0 102.7 jit_solution(2104685391640514091)
XLA Ops:
  0.6 4.7 %cache_by_receiver.1 = bf16[16,8,64,2,128]{4,3,2,1,0:T(2,128)(2,1)} custom-call(bf16[16,64,2,1024]{3,2,1,0:T(2,128)(2,1)} %bitcast.12), custom_call_target="tpu_custom_call" | custom-call | bytes 8388608 | tf_op jit(solution)/shard_map/cache_by_receiver/pallas_call | solution.py:122
  5.4 0.0 copy-start
  5.4 0.0 copy-start.2
  5.4 0.0 copy-start.3
  5.4 0.0 copy-start.1
  5.4 0.0 copy-start.4
  5.4 12.0 %all-to-all-start = ((bf16[128,128,128]{2,1,0:T(8,128)(2,1)}), bf16[128,128,128]{2,1,0:T(8,128)(2,1)}, u32[]{:S(2)}, u32[]{:S(2)}) async-start(bf16[128,128,128]{2,1,0:T(8,128)(2,1)} %bitcast.11), calls=%async_computation | async-start | bytes 8388608 | tf_op jit(solution)/shard_map/all_to_all | solution.py:367
  17.4 0.0 copy-done
  17.4 0.0 copy-done.2
  17.4 0.0 copy-done.3
  17.4 0.4 partial_projection.1
  17.9 1.4 %collective-permute-start = (f32[8,1408]{1,0:T(8,128)S(1)}, f32[8,1408]{1,0:T(8,128)S(1)}, u32[]{:S(2)}, u32[]{:S(2)}) collective-permute-start(f32[8,1408]{1,0:T(8,128)S(1)} %get-tuple-element.20), channel_id=1, source_target_pairs={{0,32},{32,0},{64,96},{96,64},{1,33},{33,1},{65,97},{97,65},{2,34}... | collective-permute-start | bytes 135176 | tf_op jit(solution)/shard_map/ppermute | solution.py:83
  19.3 2.4 %collective-permute-start.1 = (f32[8,1408]{1,0:T(8,128)S(1)}, f32[8,1408]{1,0:T(8,128)S(1)}, u32[]{:S(2)}, u32[]{:S(2)}) collective-permute-start(f32[8,1408]{1,0:T(8,128)S(1)} %get-tuple-element.21), channel_id=1, source_target_pairs={{0,64},{32,96},{64,0},{96,32},{1,65},{33,97},{65,1},{97,33},{2,66}... | collective-permute-start | bytes 135176 | tf_op jit(solution)/shard_map/ppermute | solution.py:83
  21.7 0.1 collective-permute-start.2
  21.7 0.0 copy-done.1
  21.8 2.0 %collective-permute-start.7 = (bf16[1024,512]{1,0:T(8,128)(2,1)S(1)}, bf16[1024,512]{1,0:T(8,128)(2,1)S(1)}, u32[]{:S(2)}, u32[]{:S(2)}) collective-permute-start(bf16[1024,512]{1,0:T(8,128)(2,1)S(1)} %copy-done.1), channel_id=1, source_target_pairs={{0,1},{1,0},{2,3},{3,2},{4,5},{5,4},{6,7},{7,6},{8,9},{9,8},{10,11... | collective-permute-start | bytes 3145736 | tf_op jit(solution)/shard_map/ppermute | solution.py:83
  23.7 0.0 copy-done.4
  23.7 0.7 dynamic_slice.11
  24.4 0.7 add_convert_fusion.1
  25.1 0.1 fusion
  25.2 0.1 pad_maximum_fusion
  25.3 39.1 %collective-permute-done = f32[8,1408]{1,0:T(8,128)S(1)} collective-permute-done((f32[8,1408]{1,0:T(8,128)S(1)}, f32[8,1408]{1,0:T(8,128)S(1)}, u32[]{:S(2)}, u32[]{:S(2)}) %collective-permute-start) | collective-permute-done | bytes 45088 | tf_op jit(solution)/shard_map/ppermute | solution.py:83
  64.5 2.5 %collective-permute-done.1 = f32[8,1408]{1,0:T(8,128)S(1)} collective-permute-done((f32[8,1408]{1,0:T(8,128)S(1)}, f32[8,1408]{1,0:T(8,128)S(1)}, u32[]{:S(2)}, u32[]{:S(2)}) %collective-permute-start.1) | collective-permute-done | bytes 45088 | tf_op jit(solution)/shard_map/ppermute | solution.py:83
  66.9 0.0 collective-permute-done.2
  67.0 2.5 %collective-permute-start.5 = (f32[4,1408]{1,0:T(4,128)S(1)}, f32[4,1408]{1,0:T(4,128)S(1)}, u32[]{:S(2)}, u32[]{:S(2)}) collective-permute-start(f32[4,1408]{1,0:T(4,128)S(1)} %get-tuple-element.26), channel_id=1, source_target_pairs={{0,24},{8,16},{16,8},{24,0},{1,25},{9,17},{17,9},{25,1},{2,26},{10... | collective-permute-start | bytes 67592 | tf_op jit(solution)/shard_map/ppermute | solution.py:83
  69.4 0.5 collective-permute-start.4
  69.9 0.4 collective-permute-start.3
  70.3 0.8 pad_add_fusion.info_ref
  71.1 0.2 collective-permute-done.5.third_ref
  71.3 2.3 %collective-permute-done.4.second_ref = f32[4,1408]{1,0:T(4,128)S(1)} collective-permute-done((f32[4,1408]{1,0:T(4,128)S(1)}, f32[4,1408]{1,0:T(4,128)S(1)}, u32[]{:S(2)}, u32[]{:S(2)}) %collective-permute-start.4) | collective-permute-done | bytes 22560 | tf_op jit(solution)/shard_map/ppermute | solution.py:83
  73.6 0.0 collective-permute-done.3.first_ref
  73.6 0.0 all-to-all-done
  73.6 4.4 %attend.1 = (bf16[16,8,128,128]{3,2,1,0:T(8,128)(2,1)}, bf16[48,128]{1,0:T(8,128)(2,1)S(1)}) custom-call(s32[2]{0:T(128)S(1)} %pad_add_fusion.info_ref, bf16[16,8,128,128]{3,2,1,0:T(8,128)(2,1)} %bitcast.3.kv_ref, f32[4,1408]{1,0:T(4,128)S(1)} %get-tuple-element.27.own_ref, f32[4,1408]{1,0:T(4,128)S(1)} %collective-permute-done.3.first_ref, ...), custom_call_target="tpu_custom_call" | custom-call | tf_op jit(solution)/shard_map/attend/pallas_call | solution.py:277
  78.0 10.6 %all_to_all.10.own_states_ref = bf16[16,48,128]{2,1,0:T(8,128)(2,1)S(1)} all-to-all(bf16[16,48,128]{2,1,0:T(8,128)(2,1)S(1)} %broadcast_in_dim.2), channel_id=1, replica_groups=mesh['x'=4,'y'=4,'z'=4,'core'=2] {'x','y'}, dimensions={0} | all-to-all | bytes 393216 | tf_op jit(solution)/shard_map/all_to_all | solution.py:390
  88.6 3.9 %collective-permute-start.6 = (bf16[16,48,128]{2,1,0:T(8,128)(2,1)S(1)}, bf16[16,48,128]{2,1,0:T(8,128)(2,1)S(1)}, u32[]{:S(2)}, u32[]{:S(2)}) collective-permute-start(bf16[16,48,128]{2,1,0:T(8,128)(2,1)S(1)} %all_to_all.10.own_states_ref), channel_id=1, source_target_pairs={{0,1},{1,0},{2,3},{3,2},{4,5},{5,4},{6,7},{7,6},{8,9},{9,8},{10,11... | collective-permute-start | bytes 589832 | tf_op jit(solution)/shard_map/ppermute | solution.py:83
  92.5 0.0 collective-permute-done.7.mate_ref
  92.5 1.1 %collective-permute-done.6.mate_states_ref = bf16[16,48,128]{2,1,0:T(8,128)(2,1)S(1)} collective-permute-done((bf16[16,48,128]{2,1,0:T(8,128)(2,1)S(1)}, bf16[16,48,128]{2,1,0:T(8,128)(2,1)S(1)}, u32[]{:S(2)}, u32[]{:S(2)}) %collective-permute-start.6) | collective-permute-done | bytes 196640 | tf_op jit(solution)/shard_map/ppermute | solution.py:83
  93.6 1.0 project.1
  94.5 3.3 %collective-permute-start.8 = (bf16[32,512]{1,0:T(8,128)(2,1)S(1)}, bf16[32,512]{1,0:T(8,128)(2,1)S(1)}, u32[]{:S(2)}, u32[]{:S(2)}) collective-permute-start(bf16[32,512]{1,0:T(8,128)(2,1)S(1)} %project.1), channel_id=1, source_target_pairs={{0,2},{1,7},{2,0},{3,5},{4,6},{5,3},{6,4},{7,1},{8,10},{9,15},{10,... | collective-permute-start | bytes 98312 | tf_op jit(solution)/shard_map/ppermute | solution.py:393
  97.8 0.1 collective-permute-start.10
  97.9 1.2 %collective-permute-done.8 = bf16[32,512]{1,0:T(8,128)(2,1)S(1)} collective-permute-done((bf16[32,512]{1,0:T(8,128)(2,1)S(1)}, bf16[32,512]{1,0:T(8,128)(2,1)S(1)}, u32[]{:S(2)}, u32[]{:S(2)}) %collective-permute-start.8) | collective-permute-done | bytes 32800 | tf_op jit(solution)/shard_map/ppermute | solution.py:393
  99.1 0.8 collective-permute-start.9
  99.9 2.2 %collective-permute-done.10 = bf16[32,512]{1,0:T(8,128)(2,1)S(1)} collective-permute-done((bf16[32,512]{1,0:T(8,128)(2,1)S(1)}, bf16[32,512]{1,0:T(8,128)(2,1)S(1)}, u32[]{:S(2)}, u32[]{:S(2)}) %collective-permute-start.10) | collective-permute-done | bytes 32800 | tf_op jit(solution)/shard_map/ppermute | solution.py:83
  102.1 0.0 collective-permute-done.9
  102.1 0.6 add_convert_fusion
  (5 shorter events, 0.1 us)
Async XLA Ops:
  5.4 12.0 %copy-start = (bf16[512,1280]{1,0:T(8,128)(2,1)S(1)}, bf16[512,1280]{1,0:T(8,128)(2,1)}, u32[]{:S(2)}) copy-start(bf16[512,1280]{1,0:T(8,128)(2,1)} %w_ref.1) | copy-start | bytes 3932164
  5.4 12.0 %copy-start.2 = (bf16[32,512]{1,0:T(8,128)(2,1)S(1)}, bf16[32,512]{1,0:T(8,128)(2,1)}, u32[]{:S(2)}) copy-start(bf16[32,512]{1,0:T(8,128)(2,1)} %hidden_ref) | copy-start | bytes 98308
  5.4 12.0 %copy-start.3 = (bf16[512]{0:T(512)(128)(2,1)S(1)}, bf16[512]{0:T(512)(128)(2,1)}, u32[]{:S(2)}) copy-start(bf16[512]{0:T(512)(128)(2,1)} %gain_ref.1) | copy-start | bytes 3076
  5.4 16.3 %copy-start.1 = (bf16[1024,512]{1,0:T(8,128)(2,1)S(1)}, bf16[1024,512]{1,0:T(8,128)(2,1)}, u32[]{:S(2)}) copy-start(bf16[1024,512]{1,0:T(8,128)(2,1)} %own_ref) | copy-start | bytes 3145732
  5.4 18.3 %copy-start.4 = (s32[8]{0:T(128)S(1)}, s32[8]{0:T(128)}, u32[]{:S(2)}) copy-start(s32[8]{0:T(128)} %param.8) | copy-start | bytes 100
  5.4 68.2 %all-to-all-start = ((bf16[128,128,128]{2,1,0:T(8,128)(2,1)}), bf16[128,128,128]{2,1,0:T(8,128)(2,1)}, u32[]{:S(2)}, u32[]{:S(2)}) async-start(bf16[128,128,128]{2,1,0:T(8,128)(2,1)} %bitcast.11), calls=%async_computation | async-start | bytes 8388608 | tf_op jit(solution)/shard_map/all_to_all | solution.py:367
  17.9 46.6 %collective-permute-start = (f32[8,1408]{1,0:T(8,128)S(1)}, f32[8,1408]{1,0:T(8,128)S(1)}, u32[]{:S(2)}, u32[]{:S(2)}) collective-permute-start(f32[8,1408]{1,0:T(8,128)S(1)} %get-tuple-element.20), channel_id=1, source_target_pairs={{0,32},{32,0},{64,96},{96,64},{1,33},{33,1},{65,97},{97,65},{2,34}... | collective-permute-start | bytes 135176 | tf_op jit(solution)/shard_map/ppermute | solution.py:83
  19.3 47.7 %collective-permute-start.1 = (f32[8,1408]{1,0:T(8,128)S(1)}, f32[8,1408]{1,0:T(8,128)S(1)}, u32[]{:S(2)}, u32[]{:S(2)}) collective-permute-start(f32[8,1408]{1,0:T(8,128)S(1)} %get-tuple-element.21), channel_id=1, source_target_pairs={{0,64},{32,96},{64,0},{96,32},{1,65},{33,97},{65,1},{97,33},{2,66}... | collective-permute-start | bytes 135176 | tf_op jit(solution)/shard_map/ppermute | solution.py:83
  21.7 45.3 %collective-permute-start.2 = (f32[8,1408]{1,0:T(8,128)S(1)}, f32[8,1408]{1,0:T(8,128)S(1)}, u32[]{:S(2)}, u32[]{:S(2)}) collective-permute-start(f32[8,1408]{1,0:T(8,128)S(1)} %get-tuple-element.22), channel_id=1, source_target_pairs={{0,96},{32,64},{64,32},{96,0},{1,97},{33,65},{65,33},{97,1},{2,98}... | collective-permute-start | bytes 135176 | tf_op jit(solution)/shard_map/ppermute | solution.py:83
  21.8 70.7 %collective-permute-start.7 = (bf16[1024,512]{1,0:T(8,128)(2,1)S(1)}, bf16[1024,512]{1,0:T(8,128)(2,1)S(1)}, u32[]{:S(2)}, u32[]{:S(2)}) collective-permute-start(bf16[1024,512]{1,0:T(8,128)(2,1)S(1)} %copy-done.1), channel_id=1, source_target_pairs={{0,1},{1,0},{2,3},{3,2},{4,5},{5,4},{6,7},{7,6},{8,9},{9,8},{10,11... | collective-permute-start | bytes 3145736 | tf_op jit(solution)/shard_map/ppermute | solution.py:83
  67.0 4.3 %collective-permute-start.5 = (f32[4,1408]{1,0:T(4,128)S(1)}, f32[4,1408]{1,0:T(4,128)S(1)}, u32[]{:S(2)}, u32[]{:S(2)}) collective-permute-start(f32[4,1408]{1,0:T(4,128)S(1)} %get-tuple-element.26), channel_id=1, source_target_pairs={{0,24},{8,16},{16,8},{24,0},{1,25},{9,17},{17,9},{25,1},{2,26},{10... | collective-permute-start | bytes 67592 | tf_op jit(solution)/shard_map/ppermute | solution.py:83
  69.4 4.2 %collective-permute-start.4 = (f32[4,1408]{1,0:T(4,128)S(1)}, f32[4,1408]{1,0:T(4,128)S(1)}, u32[]{:S(2)}, u32[]{:S(2)}) collective-permute-start(f32[4,1408]{1,0:T(4,128)S(1)} %get-tuple-element.26), channel_id=1, source_target_pairs={{0,16},{8,24},{16,0},{24,8},{1,17},{9,25},{17,1},{25,9},{2,18},{10... | collective-permute-start | bytes 67592 | tf_op jit(solution)/shard_map/ppermute | solution.py:83
  69.9 3.7 %collective-permute-start.3 = (f32[4,1408]{1,0:T(4,128)S(1)}, f32[4,1408]{1,0:T(4,128)S(1)}, u32[]{:S(2)}, u32[]{:S(2)}) collective-permute-start(f32[4,1408]{1,0:T(4,128)S(1)} %get-tuple-element.27.own_ref), channel_id=1, source_target_pairs={{0,8},{8,0},{16,24},{24,16},{1,9},{9,1},{17,25},{25,17},{2,10},{10... | collective-permute-start | bytes 67592 | tf_op jit(solution)/shard_map/ppermute | solution.py:83
  88.6 5.0 %collective-permute-start.6 = (bf16[16,48,128]{2,1,0:T(8,128)(2,1)S(1)}, bf16[16,48,128]{2,1,0:T(8,128)(2,1)S(1)}, u32[]{:S(2)}, u32[]{:S(2)}) collective-permute-start(bf16[16,48,128]{2,1,0:T(8,128)(2,1)S(1)} %all_to_all.10.own_states_ref), channel_id=1, source_target_pairs={{0,1},{1,0},{2,3},{3,2},{4,5},{5,4},{6,7},{7,6},{8,9},{9,8},{10,11... | collective-permute-start | bytes 589832 | tf_op jit(solution)/shard_map/ppermute | solution.py:83
  94.5 4.6 %collective-permute-start.8 = (bf16[32,512]{1,0:T(8,128)(2,1)S(1)}, bf16[32,512]{1,0:T(8,128)(2,1)S(1)}, u32[]{:S(2)}, u32[]{:S(2)}) collective-permute-start(bf16[32,512]{1,0:T(8,128)(2,1)S(1)} %project.1), channel_id=1, source_target_pairs={{0,2},{1,7},{2,0},{3,5},{4,6},{5,3},{6,4},{7,1},{8,10},{9,15},{10,... | collective-permute-start | bytes 98312 | tf_op jit(solution)/shard_map/ppermute | solution.py:393
  97.8 4.3 %collective-permute-start.10 = (bf16[32,512]{1,0:T(8,128)(2,1)S(1)}, bf16[32,512]{1,0:T(8,128)(2,1)S(1)}, u32[]{:S(2)}, u32[]{:S(2)}) collective-permute-start(bf16[32,512]{1,0:T(8,128)(2,1)S(1)} %project.1), channel_id=1, source_target_pairs={{0,4},{2,6},{4,0},{6,2},{1,5},{3,7},{5,1},{7,3},{8,12},{10,14},{12... | collective-permute-start | bytes 98312 | tf_op jit(solution)/shard_map/ppermute | solution.py:83
  99.1 3.0 %collective-permute-start.9 = (bf16[32,512]{1,0:T(8,128)(2,1)S(1)}, bf16[32,512]{1,0:T(8,128)(2,1)S(1)}, u32[]{:S(2)}, u32[]{:S(2)}) collective-permute-start(bf16[32,512]{1,0:T(8,128)(2,1)S(1)} %collective-permute-done.8), channel_id=1, source_target_pairs={{0,1},{1,0},{2,3},{3,2},{4,5},{5,4},{6,7},{7,6},{8,9},{9,8},{10,11... | collective-permute-start | bytes 98312 | tf_op jit(solution)/shard_map/ppermute | solution.py:83

commit v3 on v1

--- a/solution.py
+++ b/solution.py
@@ -300,7 +300,8 @@
     )(info, moved, *sums, cosine, sine)
 
 
-def project_kernel(own_states_ref, mate_states_ref, own_ref, mate_ref, out_ref):
+def project_kernel(states_ref, w_ref, *refs):
+    base_ref, out_ref = refs if len(refs) == 2 else (None, refs[0])
     row = lax.broadcasted_iota(jnp.int32, (HEAD_ROWS, HD), 0)
     lane = lax.broadcasted_iota(jnp.int32, (HEAD_ROWS, HD), 1)
     many = REQUESTS * HEAD_ROWS
@@ -310,49 +311,51 @@
     step = target // REQUESTS % STEPS
     request = target % REQUESTS
     moves = jnp.where(origin == request * HEAD_ROWS + head * STEPS + step, 1.0, 0.0)
-    moves = moves.astype(jnp.bfloat16)
-    totals = []
-    for states_ref, w_ref in ((own_states_ref, own_ref), (mate_states_ref, mate_ref)):
-        rows = []
-        for request in range(REQUESTS):
-            spots = [2 * request + part for part in range(2)]
-            levels = []
-            for spot in spots:
-                coded = states_ref[spot, pl.ds(HEAD_ROWS, 16), :].astype(jnp.float32)
-                level = coded[0:1] + coded[1:2] + coded[2:3]
-                levels.append(jnp.sum(jnp.where(row == lane, level, 0.0), axis=1, keepdims=True))
-            high = jnp.maximum(levels[0], levels[1])
-            shares = [jnp.exp(level - high) for level in levels]
-            whole = shares[0] + shares[1]
-            mixed = sum(
-                states_ref[spot, pl.ds(0, HEAD_ROWS), :].astype(jnp.float32) * (share / whole)
-                for spot, share in zip(spots, shares)
-            )
-            rows.append(mixed.astype(jnp.bfloat16))
-        attn = jnp.dot(
-            moves, jnp.concatenate(rows, axis=0), preferred_element_type=jnp.float32
-        ).astype(jnp.bfloat16)
-        total = jnp.zeros(out_ref.shape, jnp.float32)
-        for index in range(GQA):
-            total = total + jnp.dot(
-                attn[index * HEAD_ROWS:(index + 1) * HEAD_ROWS],
-                w_ref[pl.ds(index * HD, HD), :],
-                preferred_element_type=jnp.float32,
-            )
-        totals.append(total)
-    out_ref[...] = (totals[0] + totals[1]).astype(jnp.bfloat16)
-
-
-def project(states, mate_states, w_own, w_mate):
+    rows = []
+    for request in range(REQUESTS):
+        spots = [2 * request + part for part in range(2)]
+        levels = []
+        for spot in spots:
+            coded = states_ref[spot, pl.ds(HEAD_ROWS, 16), :].astype(jnp.float32)
+            level = coded[0:1] + coded[1:2] + coded[2:3]
+            levels.append(jnp.sum(jnp.where(row == lane, level, 0.0), axis=1, keepdims=True))
+        high = jnp.maximum(levels[0], levels[1])
+        shares = [jnp.exp(level - high) for level in levels]
+        whole = shares[0] + shares[1]
+        mixed = sum(
+            states_ref[spot, pl.ds(0, HEAD_ROWS), :].astype(jnp.float32) * (share / whole)
+            for spot, share in zip(spots, shares)
+        )
+        rows.append(mixed.astype(jnp.bfloat16))
+    attn = jnp.dot(
+        moves.astype(jnp.bfloat16),
+        jnp.concatenate(rows, axis=0),
+        preferred_element_type=jnp.float32,
+    ).astype(jnp.bfloat16)
+    total = jnp.zeros(out_ref.shape, jnp.float32)
+    for index in range(GQA):
+        total = total + jnp.dot(
+            attn[index * HEAD_ROWS:(index + 1) * HEAD_ROWS],
+            w_ref[pl.ds(index * HD, HD), :],
+            preferred_element_type=jnp.float32,
+        )
+    if base_ref is not None:
+        total = total + base_ref[...]
+    out_ref[...] = total.astype(out_ref.dtype)
+
+
+def project(states, w, base=None):
     vmem = pl.BlockSpec(memory_space=pltpu.VMEM)
+    operands = (states, w) if base is None else (states, w, base)
+    kind = jnp.float32 if base is None else jnp.bfloat16
     return pl.pallas_call(
         project_kernel,
-        in_specs=[vmem] * 4,
+        in_specs=[vmem] * len(operands),
         out_specs=vmem,
-        out_shape=jax.ShapeDtypeStruct((STEPS * REQUESTS, w_own.shape[1]), jnp.bfloat16),
+        out_shape=jax.ShapeDtypeStruct((STEPS * REQUESTS, w.shape[1]), kind),
         compiler_params=pltpu.CompilerParams(vmem_limit_bytes=8 * 1024 * 1024),
         name="project",
-    )(states, mate_states, w_own, w_mate)
+    )(*operands)
 
 
 def per_device(hidden_states, norm_gain, prompt_lengths, kv_cache, w_qkv, w_out):
@@ -375,7 +378,7 @@
     along_x = along_x.reshape(2, STEPS, COLUMNS + HD)
     own = lax.dynamic_index_in_dim(along_x, y // 2, 0, keepdims=False)
     far = lax.dynamic_index_in_dim(along_x, 1 - y // 2, 0, keepdims=False)
-    sums = [own, swap(own, "y", 1), swap(far, "y", 2), swap(far, "y", 3)]
+    sums = [own, swap(own, "y", 1), swap(far, "y", 3), swap(far, "y", 2)]
 
     angle = angles(length + jnp.arange(STEPS, dtype=jnp.int32), HD)
     cosine = jnp.cos(angle)
@@ -388,10 +391,10 @@
 
     states = jnp.broadcast_to(state[None], (CTX, STATE_ROWS, HD))
     states = lax.all_to_all(states, ("x", "y"), split_axis=0, concat_axis=0, tiled=True)
-    out = project(states, swap(states, "core", 1), w_out, w_mate)
-    terms = [out] + [swap(out, "z", other) for other in range(1, SIDE)]
-    terms = [term.astype(jnp.float32) for term in terms]
-    block_out = ((terms[0] + terms[1]) + (terms[2] + terms[3])).astype(jnp.bfloat16)
+    mate_states = swap(states, "core", 1)
+    out = project(mate_states, w_mate, project(states, w_out))
+    one, three, two = [swap(out, "z", other).astype(jnp.float32) for other in (1, 3, 2)]
+    block_out = ((out.astype(jnp.float32) + one) + (two + three)).astype(jnp.bfloat16)
     return (block_out, kv_decode)
 
 

time: 103 us -> 103 us (level)
  transfers between devices with their start and end apart: 12 -> 12, of which waited for: 7 -> 6; matrix products, arithmetic and copies ran while one was open for 2% -> 2% of each run, Pallas kernels for 5% -> 6%
where the time goes in v3:
time: 103 us; the launch traced here: 102 us
  waiting for transfers between devices  48 us (47%)
  starting transfers between devices  29.1 us (28%)
  Pallas kernels  11 us (11%)
  blocking collectives  10.3 us (10%)
  other arithmetic  2.33 us (2%)
    ppermute x11, waiting for transfers between devices, swap(): return lax.ppermute(value, axis, pairs)  48 us
    ppermute x11, starting transfers between devices, swap(): return lax.ppermute(value, axis, pairs)  17.1 us
    all_to_all x1, starting transfers between devices, per_device(): lax.all_to_all(ready, everyone, split_axis=0, concat_axis=0, tiled=True)  12 us
    all_to_all x1, blocking collectives, per_device(): lax.all_to_all(states, ('x', 'y'), split_axis=0, concat_axis=0, tiled=True)  10.3 us
    pallas_call x1, Pallas kernels, prep(): pl.pallas_call(prep_kernel, out_shape=jax.ShapeDtypeStruct((CTX, TP, PIEC...  4.74 us
    pallas_call x1, Pallas kernels, attend(): pl.pallas_call(attend_kernel, in_specs=[pl.BlockSpec(memory_space=pltpu.S...  4.68 us
  transfers between devices with their start and end apart: 12, of which 6 were waited for; matrix products, arithmetic and copies ran while one was open for 2% of the time, Pallas kernels for 6%

profile of v3, /device:TPU:1, one launch (start us, length us, event | category | flops | bytes accessed | tf_op | source)
XLA Modules:
  0.0 102.3 jit_solution(1147733198947290433)
XLA Ops:
  0.6 4.7 %cache_by_receiver.1 = bf16[16,8,64,2,128]{4,3,2,1,0:T(2,128)(2,1)} custom-call(bf16[16,64,2,1024]{3,2,1,0:T(2,128)(2,1)} %bitcast.12), custom_call_target="tpu_custom_call" | custom-call | bytes 8388608 | tf_op jit(solution)/shard_map/cache_by_receiver/pallas_call | solution.py:122
  5.4 0.0 copy-start
  5.4 0.0 copy-start.2
  5.4 0.0 copy-start.3
  5.4 0.0 copy-start.1
  5.4 0.0 copy-start.4
  5.4 12.0 %all-to-all-start = ((bf16[128,128,128]{2,1,0:T(8,128)(2,1)}), bf16[128,128,128]{2,1,0:T(8,128)(2,1)}, u32[]{:S(2)}, u32[]{:S(2)}) async-start(bf16[128,128,128]{2,1,0:T(8,128)(2,1)} %bitcast.11), calls=%async_computation | async-start | bytes 8388608 | tf_op jit(solution)/shard_map/all_to_all | solution.py:370
  17.4 0.0 copy-done
  17.4 0.0 copy-done.2
  17.4 0.0 copy-done.3
  17.4 0.4 partial_projection.1
  17.9 1.4 %collective-permute-start = (f32[8,1408]{1,0:T(8,128)S(1)}, f32[8,1408]{1,0:T(8,128)S(1)}, u32[]{:S(2)}, u32[]{:S(2)}) collective-permute-start(f32[8,1408]{1,0:T(8,128)S(1)} %get-tuple-element.20), channel_id=1, source_target_pairs={{0,32},{32,0},{64,96},{96,64},{1,33},{33,1},{65,97},{97,65},{2,34}... | collective-permute-start | bytes 135176 | tf_op jit(solution)/shard_map/ppermute | solution.py:83
  19.3 2.4 %collective-permute-start.1 = (f32[8,1408]{1,0:T(8,128)S(1)}, f32[8,1408]{1,0:T(8,128)S(1)}, u32[]{:S(2)}, u32[]{:S(2)}) collective-permute-start(f32[8,1408]{1,0:T(8,128)S(1)} %get-tuple-element.21), channel_id=1, source_target_pairs={{0,64},{32,96},{64,0},{96,32},{1,65},{33,97},{65,1},{97,33},{2,66}... | collective-permute-start | bytes 135176 | tf_op jit(solution)/shard_map/ppermute | solution.py:83
  21.7 0.1 collective-permute-start.2
  21.7 0.0 copy-done.1
  21.8 2.0 %collective-permute-start.7 = (bf16[1024,512]{1,0:T(8,128)(2,1)S(1)}, bf16[1024,512]{1,0:T(8,128)(2,1)S(1)}, u32[]{:S(2)}, u32[]{:S(2)}) collective-permute-start(bf16[1024,512]{1,0:T(8,128)(2,1)S(1)} %copy-done.1), channel_id=1, source_target_pairs={{0,1},{1,0},{2,3},{3,2},{4,5},{5,4},{6,7},{7,6},{8,9},{9,8},{10,11... | collective-permute-start | bytes 3145736 | tf_op jit(solution)/shard_map/ppermute | solution.py:83
  23.7 0.0 copy-done.4
  23.7 0.7 dynamic_slice.11
  24.4 0.7 add_convert_fusion.1
  25.1 0.1 fusion
  25.2 0.1 pad_maximum_fusion
  25.3 39.1 %collective-permute-done = f32[8,1408]{1,0:T(8,128)S(1)} collective-permute-done((f32[8,1408]{1,0:T(8,128)S(1)}, f32[8,1408]{1,0:T(8,128)S(1)}, u32[]{:S(2)}, u32[]{:S(2)}) %collective-permute-start) | collective-permute-done | bytes 45088 | tf_op jit(solution)/shard_map/ppermute | solution.py:83
  64.5 2.5 %collective-permute-done.1 = f32[8,1408]{1,0:T(8,128)S(1)} collective-permute-done((f32[8,1408]{1,0:T(8,128)S(1)}, f32[8,1408]{1,0:T(8,128)S(1)}, u32[]{:S(2)}, u32[]{:S(2)}) %collective-permute-start.1) | collective-permute-done | bytes 45088 | tf_op jit(solution)/shard_map/ppermute | solution.py:83
  66.9 0.0 collective-permute-done.2
  67.0 2.8 %collective-permute-start.5 = (f32[4,1408]{1,0:T(4,128)S(1)}, f32[4,1408]{1,0:T(4,128)S(1)}, u32[]{:S(2)}, u32[]{:S(2)}) collective-permute-start(f32[4,1408]{1,0:T(4,128)S(1)} %get-tuple-element.26), channel_id=1, source_target_pairs={{0,16},{8,24},{16,0},{24,8},{1,17},{9,25},{17,1},{25,9},{2,18},{10... | collective-permute-start | bytes 67592 | tf_op jit(solution)/shard_map/ppermute | solution.py:83
  69.8 0.8 collective-permute-start.4
  70.5 0.0 collective-permute-start.3
  70.5 0.8 pad_add_fusion.info_ref
  71.3 0.0 collective-permute-done.5.third_ref
  71.3 2.3 %collective-permute-done.4.second_ref = f32[4,1408]{1,0:T(4,128)S(1)} collective-permute-done((f32[4,1408]{1,0:T(4,128)S(1)}, f32[4,1408]{1,0:T(4,128)S(1)}, u32[]{:S(2)}, u32[]{:S(2)}) %collective-permute-start.4) | collective-permute-done | bytes 22560 | tf_op jit(solution)/shard_map/ppermute | solution.py:83
  73.6 0.0 collective-permute-done.3.first_ref
  73.6 0.0 all-to-all-done
  73.6 4.7 %attend.1 = (bf16[16,8,128,128]{3,2,1,0:T(8,128)(2,1)}, bf16[48,128]{1,0:T(8,128)(2,1)S(1)}) custom-call(s32[2]{0:T(128)S(1)} %pad_add_fusion.info_ref, bf16[16,8,128,128]{3,2,1,0:T(8,128)(2,1)} %bitcast.3.kv_ref, f32[4,1408]{1,0:T(4,128)S(1)} %get-tuple-element.27.own_ref, f32[4,1408]{1,0:T(4,128)S(1)} %collective-permute-done.3.first_ref, ...), custom_call_target="tpu_custom_call" | custom-call | tf_op jit(solution)/shard_map/attend/pallas_call | solution.py:277
  78.4 10.3 %all_to_all.10.states_ref = bf16[16,48,128]{2,1,0:T(8,128)(2,1)S(1)} all-to-all(bf16[16,48,128]{2,1,0:T(8,128)(2,1)S(1)} %broadcast_in_dim.2), channel_id=1, replica_groups=mesh['x'=4,'y'=4,'z'=4,'core'=2] {'x','y'}, dimensions={0} | all-to-all | bytes 393216 | tf_op jit(solution)/shard_map/all_to_all | solution.py:393
  88.7 3.8 %collective-permute-start.6 = (bf16[16,48,128]{2,1,0:T(8,128)(2,1)S(1)}, bf16[16,48,128]{2,1,0:T(8,128)(2,1)S(1)}, u32[]{:S(2)}, u32[]{:S(2)}) collective-permute-start(bf16[16,48,128]{2,1,0:T(8,128)(2,1)S(1)} %all_to_all.10.states_ref), channel_id=1, source_target_pairs={{0,1},{1,0},{2,3},{3,2},{4,5},{5,4},{6,7},{7,6},{8,9},{9,8},{10,11... | collective-permute-start | bytes 589832 | tf_op jit(solution)/shard_map/ppermute | solution.py:83
  92.4 0.6 project.2.refs_0_
  93.0 0.0 collective-permute-done.7.w_ref
  93.0 0.5 collective-permute-done.6.states_ref
  93.5 0.6 project.3
  94.1 3.3 %collective-permute-start.10 = (bf16[32,512]{1,0:T(8,128)(2,1)S(1)}, bf16[32,512]{1,0:T(8,128)(2,1)S(1)}, u32[]{:S(2)}, u32[]{:S(2)}) collective-permute-start(bf16[32,512]{1,0:T(8,128)(2,1)S(1)} %project.3), channel_id=1, source_target_pairs={{0,6},{2,4},{4,2},{6,0},{1,7},{3,5},{5,3},{7,1},{8,14},{10,12},{12... | collective-permute-start | bytes 98312 | tf_op jit(solution)/shard_map/ppermute | solution.py:83
  97.4 0.1 collective-permute-start.9
  97.5 0.6 collective-permute-start.8
  98.0 0.6 collective-permute-done.10
  98.7 3.0 %collective-permute-done.9 = bf16[32,512]{1,0:T(8,128)(2,1)S(1)} collective-permute-done((bf16[32,512]{1,0:T(8,128)(2,1)S(1)}, bf16[32,512]{1,0:T(8,128)(2,1)S(1)}, u32[]{:S(2)}, u32[]{:S(2)}) %collective-permute-start.9) | collective-permute-done | bytes 32800 | tf_op jit(solution)/shard_map/ppermute | solution.py:83
  101.6 0.0 collective-permute-done.8
  101.6 0.6 add_convert_fusion
  (5 shorter events, 0.1 us)
Async XLA Ops:
  5.4 12.0 %copy-start = (bf16[512,1280]{1,0:T(8,128)(2,1)S(1)}, bf16[512,1280]{1,0:T(8,128)(2,1)}, u32[]{:S(2)}) copy-start(bf16[512,1280]{1,0:T(8,128)(2,1)} %w_ref.1) | copy-start | bytes 3932164
  5.4 12.0 %copy-start.2 = (bf16[32,512]{1,0:T(8,128)(2,1)S(1)}, bf16[32,512]{1,0:T(8,128)(2,1)}, u32[]{:S(2)}) copy-start(bf16[32,512]{1,0:T(8,128)(2,1)} %hidden_ref) | copy-start | bytes 98308
  5.4 12.0 %copy-start.3 = (bf16[512]{0:T(512)(128)(2,1)S(1)}, bf16[512]{0:T(512)(128)(2,1)}, u32[]{:S(2)}) copy-start(bf16[512]{0:T(512)(128)(2,1)} %gain_ref.1) | copy-start | bytes 3076
  5.4 16.3 %copy-start.1 = (bf16[1024,512]{1,0:T(8,128)(2,1)S(1)}, bf16[1024,512]{1,0:T(8,128)(2,1)}, u32[]{:S(2)}) copy-start(bf16[1024,512]{1,0:T(8,128)(2,1)} %w_ref.2) | copy-start | bytes 3145732
  5.4 18.3 %copy-start.4 = (s32[8]{0:T(128)S(1)}, s32[8]{0:T(128)}, u32[]{:S(2)}) copy-start(s32[8]{0:T(128)} %param.8) | copy-start | bytes 100
  5.4 68.2 %all-to-all-start = ((bf16[128,128,128]{2,1,0:T(8,128)(2,1)}), bf16[128,128,128]{2,1,0:T(8,128)(2,1)}, u32[]{:S(2)}, u32[]{:S(2)}) async-start(bf16[128,128,128]{2,1,0:T(8,128)(2,1)} %bitcast.11), calls=%async_computation | async-start | bytes 8388608 | tf_op jit(solution)/shard_map/all_to_all | solution.py:370
  17.9 46.6 %collective-permute-start = (f32[8,1408]{1,0:T(8,128)S(1)}, f32[8,1408]{1,0:T(8,128)S(1)}, u32[]{:S(2)}, u32[]{:S(2)}) collective-permute-start(f32[8,1408]{1,0:T(8,128)S(1)} %get-tuple-element.20), channel_id=1, source_target_pairs={{0,32},{32,0},{64,96},{96,64},{1,33},{33,1},{65,97},{97,65},{2,34}... | collective-permute-start | bytes 135176 | tf_op jit(solution)/shard_map/ppermute | solution.py:83
  19.3 47.7 %collective-permute-start.1 = (f32[8,1408]{1,0:T(8,128)S(1)}, f32[8,1408]{1,0:T(8,128)S(1)}, u32[]{:S(2)}, u32[]{:S(2)}) collective-permute-start(f32[8,1408]{1,0:T(8,128)S(1)} %get-tuple-element.21), channel_id=1, source_target_pairs={{0,64},{32,96},{64,0},{96,32},{1,65},{33,97},{65,1},{97,33},{2,66}... | collective-permute-start | bytes 135176 | tf_op jit(solution)/shard_map/ppermute | solution.py:83
  21.7 45.3 %collective-permute-start.2 = (f32[8,1408]{1,0:T(8,128)S(1)}, f32[8,1408]{1,0:T(8,128)S(1)}, u32[]{:S(2)}, u32[]{:S(2)}) collective-permute-start(f32[8,1408]{1,0:T(8,128)S(1)} %get-tuple-element.22), channel_id=1, source_target_pairs={{0,96},{32,64},{64,32},{96,0},{1,97},{33,65},{65,33},{97,1},{2,98}... | collective-permute-start | bytes 135176 | tf_op jit(solution)/shard_map/ppermute | solution.py:83
  21.8 71.3 %collective-permute-start.7 = (bf16[1024,512]{1,0:T(8,128)(2,1)S(1)}, bf16[1024,512]{1,0:T(8,128)(2,1)S(1)}, u32[]{:S(2)}, u32[]{:S(2)}) collective-permute-start(bf16[1024,512]{1,0:T(8,128)(2,1)S(1)} %copy-done.1), channel_id=1, source_target_pairs={{0,1},{1,0},{2,3},{3,2},{4,5},{5,4},{6,7},{7,6},{8,9},{9,8},{10,11... | collective-permute-start | bytes 3145736 | tf_op jit(solution)/shard_map/ppermute | solution.py:83
  67.0 4.3 %collective-permute-start.5 = (f32[4,1408]{1,0:T(4,128)S(1)}, f32[4,1408]{1,0:T(4,128)S(1)}, u32[]{:S(2)}, u32[]{:S(2)}) collective-permute-start(f32[4,1408]{1,0:T(4,128)S(1)} %get-tuple-element.26), channel_id=1, source_target_pairs={{0,16},{8,24},{16,0},{24,8},{1,17},{9,25},{17,1},{25,9},{2,18},{10... | collective-permute-start | bytes 67592 | tf_op jit(solution)/shard_map/ppermute | solution.py:83
  69.8 3.9 %collective-permute-start.4 = (f32[4,1408]{1,0:T(4,128)S(1)}, f32[4,1408]{1,0:T(4,128)S(1)}, u32[]{:S(2)}, u32[]{:S(2)}) collective-permute-start(f32[4,1408]{1,0:T(4,128)S(1)} %get-tuple-element.26), channel_id=1, source_target_pairs={{0,24},{8,16},{16,8},{24,0},{1,25},{9,17},{17,9},{25,1},{2,26},{10... | collective-permute-start | bytes 67592 | tf_op jit(solution)/shard_map/ppermute | solution.py:83
  70.5 3.1 %collective-permute-start.3 = (f32[4,1408]{1,0:T(4,128)S(1)}, f32[4,1408]{1,0:T(4,128)S(1)}, u32[]{:S(2)}, u32[]{:S(2)}) collective-permute-start(f32[4,1408]{1,0:T(4,128)S(1)} %get-tuple-element.27.own_ref), channel_id=1, source_target_pairs={{0,8},{8,0},{16,24},{24,16},{1,9},{9,1},{17,25},{25,17},{2,10},{10... | collective-permute-start | bytes 67592 | tf_op jit(solution)/shard_map/ppermute | solution.py:83
  88.7 4.9 %collective-permute-start.6 = (bf16[16,48,128]{2,1,0:T(8,128)(2,1)S(1)}, bf16[16,48,128]{2,1,0:T(8,128)(2,1)S(1)}, u32[]{:S(2)}, u32[]{:S(2)}) collective-permute-start(bf16[16,48,128]{2,1,0:T(8,128)(2,1)S(1)} %all_to_all.10.states_ref), channel_id=1, source_target_pairs={{0,1},{1,0},{2,3},{3,2},{4,5},{5,4},{6,7},{7,6},{8,9},{9,8},{10,11... | collective-permute-start | bytes 589832 | tf_op jit(solution)/shard_map/ppermute | solution.py:83
  94.1 4.6 %collective-permute-start.10 = (bf16[32,512]{1,0:T(8,128)(2,1)S(1)}, bf16[32,512]{1,0:T(8,128)(2,1)S(1)}, u32[]{:S(2)}, u32[]{:S(2)}) collective-permute-start(bf16[32,512]{1,0:T(8,128)(2,1)S(1)} %project.3), channel_id=1, source_target_pairs={{0,6},{2,4},{4,2},{6,0},{1,7},{3,5},{5,3},{7,1},{8,14},{10,12},{12... | collective-permute-start | bytes 98312 | tf_op jit(solution)/shard_map/ppermute | solution.py:83
  97.4 4.3 %collective-permute-start.9 = (bf16[32,512]{1,0:T(8,128)(2,1)S(1)}, bf16[32,512]{1,0:T(8,128)(2,1)S(1)}, u32[]{:S(2)}, u32[]{:S(2)}) collective-permute-start(bf16[32,512]{1,0:T(8,128)(2,1)S(1)} %project.3), channel_id=1, source_target_pairs={{0,4},{2,6},{4,0},{6,2},{1,5},{3,7},{5,1},{7,3},{8,12},{10,14},{12... | collective-permute-start | bytes 98312 | tf_op jit(solution)/shard_map/ppermute | solution.py:83
  97.5 4.2 %collective-permute-start.8 = (bf16[32,512]{1,0:T(8,128)(2,1)S(1)}, bf16[32,512]{1,0:T(8,128)(2,1)S(1)}, u32[]{:S(2)}, u32[]{:S(2)}) collective-permute-start(bf16[32,512]{1,0:T(8,128)(2,1)S(1)} %project.3), channel_id=1, source_target_pairs={{0,2},{2,0},{4,6},{6,4},{1,3},{3,1},{5,7},{7,5},{8,10},{10,8},{12,... | collective-permute-start | bytes 98312 | tf_op jit(solution)/shard_map/ppermute | solution.py:83

commit v4 on v3

--- a/solution.py
+++ b/solution.py
@@ -83,38 +83,37 @@
     return lax.ppermute(value, axis, pairs)
 
 
-def prep_kernel(kv_ref, out_ref, held, ready, in_sems, head_sems, out_sems):
-    def fetch(receiver):
+PARTS = 2
+
+
+def prep_kernel(kv_ref, out_ref, held, ready, in_sems, out_sems):
+    depth = PIECE // PARTS
+    heads = TP // PARTS
+
+    def fetch(receiver, part):
+        span = pl.ds(part * depth, depth)
         return pltpu.make_async_copy(
-            kv_ref.at[receiver], held.at[receiver // 2], in_sems.at[receiver // 2]
-        )
-
-    def fetch_head(receiver, head):
+            kv_ref.at[receiver, span], held.at[receiver, span], in_sems.at[receiver, part]
+        )
+
+    def place(receiver, part):
+        span = pl.ds(part * heads, heads)
         return pltpu.make_async_copy(
-            kv_ref.at[receiver, :, :, pl.ds(head * HD, HD)],
-            ready.at[receiver, head],
-            head_sems.at[receiver // 2, head],
-        )
-
-    def place(receiver):
-        return pltpu.make_async_copy(
-            ready.at[receiver], out_ref.at[receiver], out_sems.at[receiver]
-        )
-
-    for receiver in range(0, CTX, 2):
-        fetch(receiver).start()
-        for head in range(TP):
-            fetch_head(receiver + 1, head).start()
-    for receiver in range(0, CTX, 2):
-        fetch(receiver).wait()
-        for head in range(TP):
-            ready[receiver, head] = held[receiver // 2, :, :, pl.ds(head * HD, HD)]
-        place(receiver).start()
-        for head in range(TP):
-            fetch_head(receiver + 1, head).wait()
-        place(receiver + 1).start()
+            ready.at[receiver, span], out_ref.at[receiver, span], out_sems.at[receiver, part]
+        )
+
+    every = [(receiver, part) for receiver in range(CTX) for part in range(PARTS)]
+    for spot in every:
+        fetch(*spot).start()
     for receiver in range(CTX):
-        place(receiver).wait()
+        for part in range(PARTS):
+            fetch(receiver, part).wait()
+        for part in range(PARTS):
+            for head in range(part * heads, (part + 1) * heads):
+                ready[receiver, head] = held[receiver, :, :, pl.ds(head * HD, HD)]
+            place(receiver, part).start()
+    for spot in every:
+        place(*spot).wait()
 
 
 def prep(kv_cache):
@@ -125,11 +124,10 @@
         in_specs=[pl.BlockSpec(memory_space=pl.ANY)],
         out_specs=pl.BlockSpec(memory_space=pl.ANY),
         scratch_shapes=[
-            pltpu.VMEM((CTX // 2, PIECE, 2, TP * HD), jnp.bfloat16),
+            pltpu.VMEM((CTX, PIECE, 2, TP * HD), jnp.bfloat16),
             pltpu.VMEM((CTX, TP, PIECE, 2, HD), jnp.bfloat16),
-            pltpu.SemaphoreType.DMA((CTX // 2,)),
-            pltpu.SemaphoreType.DMA((CTX // 2, TP)),
-            pltpu.SemaphoreType.DMA((CTX,)),
+            pltpu.SemaphoreType.DMA((CTX, PARTS)),
+            pltpu.SemaphoreType.DMA((CTX, PARTS)),
         ],
         compiler_params=pltpu.CompilerParams(vmem_limit_bytes=56 * 1024 * 1024),
         cost_estimate=pl.CostEstimate(
@@ -156,14 +154,21 @@
     part = info_ref[1]
     left = length - part * PIECE
 
-    def fetch(ctx):
-        return pltpu.make_async_copy(kv_ref.at[ctx], held.at[ctx], in_sems.at[ctx])
-
-    def place(ctx):
-        return pltpu.make_async_copy(held.at[ctx], kv_out_ref.at[ctx], out_sems.at[ctx])
-
-    for ctx in range(CTX):
-        fetch(ctx).start()
+    def fetch(ctx, part):
+        span = pl.ds(part * (TP // PARTS), TP // PARTS)
+        return pltpu.make_async_copy(
+            kv_ref.at[ctx, span], held.at[ctx, span], in_sems.at[ctx, part]
+        )
+
+    def place(ctx, part):
+        span = pl.ds(part * (TP // PARTS), TP // PARTS)
+        return pltpu.make_async_copy(
+            held.at[ctx, span], kv_out_ref.at[ctx, span], out_sems.at[ctx, part]
+        )
+
+    every = [(ctx, part) for ctx in range(CTX) for part in range(PARTS)]
+    for spot in every:
+        fetch(*spot).start()
 
     row = lax.broadcasted_iota(jnp.int32, (HEAD_ROWS, HD), 0)
     lane = lax.broadcasted_iota(jnp.int32, (HEAD_ROWS, HD), 1)
@@ -194,9 +199,9 @@
     acc[...] = jnp.dot(weight.astype(jnp.bfloat16), values, preferred_element_type=jnp.float32)
 
     def arrive(chunk):
-        for ctx in range(chunk * CHUNK_CTX, (chunk + 1) * CHUNK_CTX):
-            fetch(ctx).wait()
-            place(ctx).start()
+        for spot in every[chunk * CHUNK_CTX * PARTS:(chunk + 1) * CHUNK_CTX * PARTS]:
+            fetch(*spot).wait()
+            place(*spot).start()
 
     def score(chunk):
         wide[...] = held[pl.ds(chunk * CHUNK_CTX, CHUNK_CTX)].reshape(CHUNK_ROWS, HD).astype(
@@ -267,8 +272,8 @@
     parts = jnp.where(place_in == 0, first, jnp.where(place_in == 1, second, third))
     out_ref[pl.ds(HEAD_ROWS, 16), :] = parts.astype(jnp.bfloat16)
 
-    for ctx in range(CTX):
-        place(ctx).wait()
+    for spot in every:
+        place(*spot).wait()
 
 
 def attend(info, moved, sums, cosine, sine):
@@ -288,8 +293,8 @@
             pltpu.VMEM((HEAD_ROWS, HD), jnp.float32),
             pltpu.VMEM((HEAD_ROWS, HD), jnp.float32),
             pltpu.VMEM((HEAD_ROWS, HD), jnp.float32),
-            pltpu.SemaphoreType.DMA((CTX,)),
-            pltpu.SemaphoreType.DMA((CTX,)),
+            pltpu.SemaphoreType.DMA((CTX, PARTS)),
+            pltpu.SemaphoreType.DMA((CTX, PARTS)),
         ],
         out_shape=[
             jax.ShapeDtypeStruct((CTX, TP, 2 * PIECE, HD), jnp.bfloat16),
@@ -393,8 +398,15 @@
     states = lax.all_to_all(states, ("x", "y"), split_axis=0, concat_axis=0, tiled=True)
     mate_states = swap(states, "core", 1)
     out = project(mate_states, w_mate, project(states, w_out))
-    one, three, two = [swap(out, "z", other).astype(jnp.float32) for other in (1, 3, 2)]
-    block_out = ((out.astype(jnp.float32) + one) + (two + three)).astype(jnp.bfloat16)
+    pairs = [(z * 2 + c, (z ^ (1 + 2 * c)) * 2 + c) for z in range(SIDE) for c in range(2)]
+    near = lax.ppermute(out, ("z", "core"), pairs)
+    across = swap(out, "z", 2)
+    shared = swap(near, "core", 1)
+    first = lax.axis_index("core") == 0
+    one = jnp.where(first, near, shared).astype(jnp.float32)
+    three = jnp.where(first, shared, near).astype(jnp.float32)
+    block_out = (out.astype(jnp.float32) + one) + (across.astype(jnp.float32) + three)
+    block_out = block_out.astype(jnp.bfloat16)
     return (block_out, kv_decode)
 
 

time: 103 us -> 103 us (level)
    ppermute x0 -> x1, starting transfers between devices: none -> 3.27 us  [per_device(): near = lax.ppermute(out, ('z', 'core'), pairs)]
    ppermute x11 -> x10, starting transfers between devices: 17.1 us -> 14.1 us  [swap(): return lax.ppermute(value, axis, pairs)]
    ppermute x11 -> x10, waiting for transfers between devices: 48 us -> 46.6 us  [swap(): return lax.ppermute(value, axis, pairs)]
    ppermute x0 -> x1, waiting for transfers between devices: none -> 1.18 us  [per_device(): near = lax.ppermute(out, ('z', 'core'), pairs)]
where the time goes in v4:
time: 103 us
  waiting for transfers between devices  47.8 us (46%)
  starting transfers between devices  29.4 us (29%)
  Pallas kernels  11.8 us (11%)
  blocking collectives  10.3 us (10%)
  other arithmetic  2.33 us (2%)
    ppermute x10, waiting for transfers between devices, swap(): return lax.ppermute(value, axis, pairs)  46.6 us
    ppermute x10, starting transfers between devices, swap(): return lax.ppermute(value, axis, pairs)  14.1 us
    all_to_all x1, starting transfers between devices, per_device(): lax.all_to_all(ready, everyone, split_axis=0, concat_axis=0, tiled=True)  12 us
    all_to_all x1, blocking collectives, per_device(): lax.all_to_all(states, ('x', 'y'), split_axis=0, concat_axis=0, tiled=True)  10.3 us
    pallas_call x1, Pallas kernels, prep(): pl.pallas_call(prep_kernel, out_shape=jax.ShapeDtypeStruct((CTX, TP, PIEC...  5.13 us
    pallas_call x1, Pallas kernels, attend(): pl.pallas_call(attend_kernel, in_specs=[pl.BlockSpec(memory_space=pltpu.S...  5.13 us
    ppermute x1, starting transfers between devices, per_device(): near = lax.ppermute(out, ('z', 'core'), pairs)  3.27 us
  transfers between devices with their start and end apart: 12, of which 6 were waited for; matrix products, arithmetic and copies ran while one was open for 2% of the time, Pallas kernels for 6%

profile of v4, /device:TPU:1, one launch (start us, length us, event | category | flops | bytes accessed | tf_op | source)
XLA Modules:
  0.0 103.1 jit_solution(11466494523280704842)
XLA Ops:
  0.6 5.1 %cache_by_receiver.1 = bf16[16,8,64,2,128]{4,3,2,1,0:T(2,128)(2,1)} custom-call(bf16[16,64,2,1024]{3,2,1,0:T(2,128)(2,1)} %bitcast.12), custom_call_target="tpu_custom_call" | custom-call | bytes 8388608 | tf_op jit(solution)/shard_map/cache_by_receiver/pallas_call | solution.py:121
  5.8 0.0 copy-start
  5.8 0.0 copy-start.2
  5.8 0.0 copy-start.3
  5.8 0.0 copy-start.1
  5.8 0.0 copy-start.4
  5.8 12.0 %all-to-all-start = ((bf16[128,128,128]{2,1,0:T(8,128)(2,1)}), bf16[128,128,128]{2,1,0:T(8,128)(2,1)}, u32[]{:S(2)}, u32[]{:S(2)}) async-start(bf16[128,128,128]{2,1,0:T(8,128)(2,1)} %bitcast.11), calls=%async_computation | async-start | bytes 8388608 | tf_op jit(solution)/shard_map/all_to_all | solution.py:375
  17.8 0.0 copy-done
  17.8 0.0 copy-done.2
  17.8 0.0 copy-done.3
  17.8 0.4 partial_projection.1
  18.3 1.4 %collective-permute-start = (f32[8,1408]{1,0:T(8,128)S(1)}, f32[8,1408]{1,0:T(8,128)S(1)}, u32[]{:S(2)}, u32[]{:S(2)}) collective-permute-start(f32[8,1408]{1,0:T(8,128)S(1)} %get-tuple-element.20), channel_id=1, source_target_pairs={{0,32},{32,0},{64,96},{96,64},{1,33},{33,1},{65,97},{97,65},{2,34}... | collective-permute-start | bytes 135176 | tf_op jit(solution)/shard_map/ppermute | solution.py:83
  19.7 2.4 %collective-permute-start.1 = (f32[8,1408]{1,0:T(8,128)S(1)}, f32[8,1408]{1,0:T(8,128)S(1)}, u32[]{:S(2)}, u32[]{:S(2)}) collective-permute-start(f32[8,1408]{1,0:T(8,128)S(1)} %get-tuple-element.21), channel_id=1, source_target_pairs={{0,64},{32,96},{64,0},{96,32},{1,65},{33,97},{65,1},{97,33},{2,66}... | collective-permute-start | bytes 135176 | tf_op jit(solution)/shard_map/ppermute | solution.py:83
  22.0 0.1 collective-permute-start.2
  22.1 0.0 copy-done.1
  22.1 2.0 %collective-permute-start.7 = (bf16[1024,512]{1,0:T(8,128)(2,1)S(1)}, bf16[1024,512]{1,0:T(8,128)(2,1)S(1)}, u32[]{:S(2)}, u32[]{:S(2)}) collective-permute-start(bf16[1024,512]{1,0:T(8,128)(2,1)S(1)} %copy-done.1), channel_id=1, source_target_pairs={{0,1},{1,0},{2,3},{3,2},{4,5},{5,4},{6,7},{7,6},{8,9},{9,8},{10,11... | collective-permute-start | bytes 3145736 | tf_op jit(solution)/shard_map/ppermute | solution.py:83
  24.1 0.0 copy-done.4
  24.1 0.7 dynamic_slice.11
  24.8 0.7 add_convert_fusion.1
  25.5 0.1 fusion
  25.6 0.1 pad_maximum_fusion
  25.7 39.1 %collective-permute-done = f32[8,1408]{1,0:T(8,128)S(1)} collective-permute-done((f32[8,1408]{1,0:T(8,128)S(1)}, f32[8,1408]{1,0:T(8,128)S(1)}, u32[]{:S(2)}, u32[]{:S(2)}) %collective-permute-start) | collective-permute-done | bytes 45088 | tf_op jit(solution)/shard_map/ppermute | solution.py:83
  64.8 2.5 %collective-permute-done.1 = f32[8,1408]{1,0:T(8,128)S(1)} collective-permute-done((f32[8,1408]{1,0:T(8,128)S(1)}, f32[8,1408]{1,0:T(8,128)S(1)}, u32[]{:S(2)}, u32[]{:S(2)}) %collective-permute-start.1) | collective-permute-done | bytes 45088 | tf_op jit(solution)/shard_map/ppermute | solution.py:83
  67.3 0.0 collective-permute-done.2
  67.4 2.8 %collective-permute-start.5 = (f32[4,1408]{1,0:T(4,128)S(1)}, f32[4,1408]{1,0:T(4,128)S(1)}, u32[]{:S(2)}, u32[]{:S(2)}) collective-permute-start(f32[4,1408]{1,0:T(4,128)S(1)} %get-tuple-element.26), channel_id=1, source_target_pairs={{0,16},{8,24},{16,0},{24,8},{1,17},{9,25},{17,1},{25,9},{2,18},{10... | collective-permute-start | bytes 67592 | tf_op jit(solution)/shard_map/ppermute | solution.py:83
  70.2 0.8 collective-permute-start.4
  70.9 0.0 collective-permute-start.3
  70.9 0.8 pad_add_fusion.info_ref
  71.7 0.0 collective-permute-done.5.third_ref
  71.7 2.3 %collective-permute-done.4.second_ref = f32[4,1408]{1,0:T(4,128)S(1)} collective-permute-done((f32[4,1408]{1,0:T(4,128)S(1)}, f32[4,1408]{1,0:T(4,128)S(1)}, u32[]{:S(2)}, u32[]{:S(2)}) %collective-permute-start.4) | collective-permute-done | bytes 22560 | tf_op jit(solution)/shard_map/ppermute | solution.py:83
  74.0 0.0 collective-permute-done.3.first_ref
  74.0 0.0 all-to-all-done
  74.0 5.1 %attend.1 = (bf16[16,8,128,128]{3,2,1,0:T(8,128)(2,1)}, bf16[48,128]{1,0:T(8,128)(2,1)S(1)}) custom-call(s32[2]{0:T(128)S(1)} %pad_add_fusion.info_ref, bf16[16,8,128,128]{3,2,1,0:T(8,128)(2,1)} %bitcast.3.kv_ref, f32[4,1408]{1,0:T(4,128)S(1)} %get-tuple-element.27.own_ref, f32[4,1408]{1,0:T(4,128)S(1)} %collective-permute-done.3.first_ref, ...), custom_call_target="tpu_custom_call" | custom-call | tf_op jit(solution)/shard_map/attend/pallas_call | solution.py:282
  79.2 10.3 %all_to_all.10.states_ref = bf16[16,48,128]{2,1,0:T(8,128)(2,1)S(1)} all-to-all(bf16[16,48,128]{2,1,0:T(8,128)(2,1)S(1)} %broadcast_in_dim.2), channel_id=1, replica_groups=mesh['x'=4,'y'=4,'z'=4,'core'=2] {'x','y'}, dimensions={0} | all-to-all | bytes 393216 | tf_op jit(solution)/shard_map/all_to_all | solution.py:398
  89.5 3.8 %collective-permute-start.6 = (bf16[16,48,128]{2,1,0:T(8,128)(2,1)S(1)}, bf16[16,48,128]{2,1,0:T(8,128)(2,1)S(1)}, u32[]{:S(2)}, u32[]{:S(2)}) collective-permute-start(bf16[16,48,128]{2,1,0:T(8,128)(2,1)S(1)} %all_to_all.10.states_ref), channel_id=1, source_target_pairs={{0,1},{1,0},{2,3},{3,2},{4,5},{5,4},{6,7},{7,6},{8,9},{9,8},{10,11... | collective-permute-start | bytes 589832 | tf_op jit(solution)/shard_map/ppermute | solution.py:83
  93.3 0.6 project.2.refs_0_
  93.9 0.0 collective-permute-done.7.w_ref
  93.9 0.5 collective-permute-done.6.states_ref
  94.3 0.6 project.3
  94.9 3.3 %collective-permute-start.8 = (bf16[32,512]{1,0:T(8,128)(2,1)S(1)}, bf16[32,512]{1,0:T(8,128)(2,1)S(1)}, u32[]{:S(2)}, u32[]{:S(2)}) collective-permute-start(bf16[32,512]{1,0:T(8,128)(2,1)S(1)} %project.3), channel_id=1, source_target_pairs={{0,2},{1,7},{2,0},{3,5},{4,6},{5,3},{6,4},{7,1},{8,10},{9,15},{10,... | collective-permute-start | bytes 98312 | tf_op jit(solution)/shard_map/ppermute | solution.py:402
  98.2 0.1 collective-permute-start.10
  98.3 1.2 %collective-permute-done.8 = bf16[32,512]{1,0:T(8,128)(2,1)S(1)} collective-permute-done((bf16[32,512]{1,0:T(8,128)(2,1)S(1)}, bf16[32,512]{1,0:T(8,128)(2,1)S(1)}, u32[]{:S(2)}, u32[]{:S(2)}) %collective-permute-start.8) | collective-permute-done | bytes 32800 | tf_op jit(solution)/shard_map/ppermute | solution.py:402
  99.5 0.8 collective-permute-start.9
  100.3 2.2 %collective-permute-done.10 = bf16[32,512]{1,0:T(8,128)(2,1)S(1)} collective-permute-done((bf16[32,512]{1,0:T(8,128)(2,1)S(1)}, bf16[32,512]{1,0:T(8,128)(2,1)S(1)}, u32[]{:S(2)}, u32[]{:S(2)}) %collective-permute-start.10) | collective-permute-done | bytes 32800 | tf_op jit(solution)/shard_map/ppermute | solution.py:83
  102.5 0.0 collective-permute-done.9
  102.5 0.6 add_convert_fusion
  (5 shorter events, 0.1 us)
Async XLA Ops:
  5.8 12.0 %copy-start = (bf16[512,1280]{1,0:T(8,128)(2,1)S(1)}, bf16[512,1280]{1,0:T(8,128)(2,1)}, u32[]{:S(2)}) copy-start(bf16[512,1280]{1,0:T(8,128)(2,1)} %w_ref.1) | copy-start | bytes 3932164
  5.8 12.0 %copy-start.2 = (bf16[32,512]{1,0:T(8,128)(2,1)S(1)}, bf16[32,512]{1,0:T(8,128)(2,1)}, u32[]{:S(2)}) copy-start(bf16[32,512]{1,0:T(8,128)(2,1)} %hidden_ref) | copy-start | bytes 98308
  5.8 12.0 %copy-start.3 = (bf16[512]{0:T(512)(128)(2,1)S(1)}, bf16[512]{0:T(512)(128)(2,1)}, u32[]{:S(2)}) copy-start(bf16[512]{0:T(512)(128)(2,1)} %gain_ref.1) | copy-start | bytes 3076
  5.8 16.3 %copy-start.1 = (bf16[1024,512]{1,0:T(8,128)(2,1)S(1)}, bf16[1024,512]{1,0:T(8,128)(2,1)}, u32[]{:S(2)}) copy-start(bf16[1024,512]{1,0:T(8,128)(2,1)} %w_ref.2) | copy-start | bytes 3145732
  5.8 18.3 %copy-start.4 = (s32[8]{0:T(128)S(1)}, s32[8]{0:T(128)}, u32[]{:S(2)}) copy-start(s32[8]{0:T(128)} %param.8) | copy-start | bytes 100
  5.8 68.2 %all-to-all-start = ((bf16[128,128,128]{2,1,0:T(8,128)(2,1)}), bf16[128,128,128]{2,1,0:T(8,128)(2,1)}, u32[]{:S(2)}, u32[]{:S(2)}) async-start(bf16[128,128,128]{2,1,0:T(8,128)(2,1)} %bitcast.11), calls=%async_computation | async-start | bytes 8388608 | tf_op jit(solution)/shard_map/all_to_all | solution.py:375
  18.3 46.6 %collective-permute-start = (f32[8,1408]{1,0:T(8,128)S(1)}, f32[8,1408]{1,0:T(8,128)S(1)}, u32[]{:S(2)}, u32[]{:S(2)}) collective-permute-start(f32[8,1408]{1,0:T(8,128)S(1)} %get-tuple-element.20), channel_id=1, source_target_pairs={{0,32},{32,0},{64,96},{96,64},{1,33},{33,1},{65,97},{97,65},{2,34}... | collective-permute-start | bytes 135176 | tf_op jit(solution)/shard_map/ppermute | solution.py:83
  19.7 47.7 %collective-permute-start.1 = (f32[8,1408]{1,0:T(8,128)S(1)}, f32[8,1408]{1,0:T(8,128)S(1)}, u32[]{:S(2)}, u32[]{:S(2)}) collective-permute-start(f32[8,1408]{1,0:T(8,128)S(1)} %get-tuple-element.21), channel_id=1, source_target_pairs={{0,64},{32,96},{64,0},{96,32},{1,65},{33,97},{65,1},{97,33},{2,66}... | collective-permute-start | bytes 135176 | tf_op jit(solution)/shard_map/ppermute | solution.py:83
  22.0 45.3 %collective-permute-start.2 = (f32[8,1408]{1,0:T(8,128)S(1)}, f32[8,1408]{1,0:T(8,128)S(1)}, u32[]{:S(2)}, u32[]{:S(2)}) collective-permute-start(f32[8,1408]{1,0:T(8,128)S(1)} %get-tuple-element.22), channel_id=1, source_target_pairs={{0,96},{32,64},{64,32},{96,0},{1,97},{33,65},{65,33},{97,1},{2,98}... | collective-permute-start | bytes 135176 | tf_op jit(solution)/shard_map/ppermute | solution.py:83
  22.1 71.7 %collective-permute-start.7 = (bf16[1024,512]{1,0:T(8,128)(2,1)S(1)}, bf16[1024,512]{1,0:T(8,128)(2,1)S(1)}, u32[]{:S(2)}, u32[]{:S(2)}) collective-permute-start(bf16[1024,512]{1,0:T(8,128)(2,1)S(1)} %copy-done.1), channel_id=1, source_target_pairs={{0,1},{1,0},{2,3},{3,2},{4,5},{5,4},{6,7},{7,6},{8,9},{9,8},{10,11... | collective-permute-start | bytes 3145736 | tf_op jit(solution)/shard_map/ppermute | solution.py:83
  67.4 4.3 %collective-permute-start.5 = (f32[4,1408]{1,0:T(4,128)S(1)}, f32[4,1408]{1,0:T(4,128)S(1)}, u32[]{:S(2)}, u32[]{:S(2)}) collective-permute-start(f32[4,1408]{1,0:T(4,128)S(1)} %get-tuple-element.26), channel_id=1, source_target_pairs={{0,16},{8,24},{16,0},{24,8},{1,17},{9,25},{17,1},{25,9},{2,18},{10... | collective-permute-start | bytes 67592 | tf_op jit(solution)/shard_map/ppermute | solution.py:83
  70.2 3.9 %collective-permute-start.4 = (f32[4,1408]{1,0:T(4,128)S(1)}, f32[4,1408]{1,0:T(4,128)S(1)}, u32[]{:S(2)}, u32[]{:S(2)}) collective-permute-start(f32[4,1408]{1,0:T(4,128)S(1)} %get-tuple-element.26), channel_id=1, source_target_pairs={{0,24},{8,16},{16,8},{24,0},{1,25},{9,17},{17,9},{25,1},{2,26},{10... | collective-permute-start | bytes 67592 | tf_op jit(solution)/shard_map/ppermute | solution.py:83
  70.9 3.1 %collective-permute-start.3 = (f32[4,1408]{1,0:T(4,128)S(1)}, f32[4,1408]{1,0:T(4,128)S(1)}, u32[]{:S(2)}, u32[]{:S(2)}) collective-permute-start(f32[4,1408]{1,0:T(4,128)S(1)} %get-tuple-element.27.own_ref), channel_id=1, source_target_pairs={{0,8},{8,0},{16,24},{24,16},{1,9},{9,1},{17,25},{25,17},{2,10},{10... | collective-permute-start | bytes 67592 | tf_op jit(solution)/shard_map/ppermute | solution.py:83
  89.5 4.9 %collective-permute-start.6 = (bf16[16,48,128]{2,1,0:T(8,128)(2,1)S(1)}, bf16[16,48,128]{2,1,0:T(8,128)(2,1)S(1)}, u32[]{:S(2)}, u32[]{:S(2)}) collective-permute-start(bf16[16,48,128]{2,1,0:T(8,128)(2,1)S(1)} %all_to_all.10.states_ref), channel_id=1, source_target_pairs={{0,1},{1,0},{2,3},{3,2},{4,5},{5,4},{6,7},{7,6},{8,9},{9,8},{10,11... | collective-permute-start | bytes 589832 | tf_op jit(solution)/shard_map/ppermute | solution.py:83
  94.9 4.6 %collective-permute-start.8 = (bf16[32,512]{1,0:T(8,128)(2,1)S(1)}, bf16[32,512]{1,0:T(8,128)(2,1)S(1)}, u32[]{:S(2)}, u32[]{:S(2)}) collective-permute-start(bf16[32,512]{1,0:T(8,128)(2,1)S(1)} %project.3), channel_id=1, source_target_pairs={{0,2},{1,7},{2,0},{3,5},{4,6},{5,3},{6,4},{7,1},{8,10},{9,15},{10,... | collective-permute-start | bytes 98312 | tf_op jit(solution)/shard_map/ppermute | solution.py:402
  98.2 4.3 %collective-permute-start.10 = (bf16[32,512]{1,0:T(8,128)(2,1)S(1)}, bf16[32,512]{1,0:T(8,128)(2,1)S(1)}, u32[]{:S(2)}, u32[]{:S(2)}) collective-permute-start(bf16[32,512]{1,0:T(8,128)(2,1)S(1)} %project.3), channel_id=1, source_target_pairs={{0,4},{2,6},{4,0},{6,2},{1,5},{3,7},{5,1},{7,3},{8,12},{10,14},{12... | collective-permute-start | bytes 98312 | tf_op jit(solution)/shard_map/ppermute | solution.py:83
  99.5 3.0 %collective-permute-start.9 = (bf16[32,512]{1,0:T(8,128)(2,1)S(1)}, bf16[32,512]{1,0:T(8,128)(2,1)S(1)}, u32[]{:S(2)}, u32[]{:S(2)}) collective-permute-start(bf16[32,512]{1,0:T(8,128)(2,1)S(1)} %collective-permute-done.8), channel_id=1, source_target_pairs={{0,1},{1,0},{2,3},{3,2},{4,5},{5,4},{6,7},{7,6},{8,9},{9,8},{10,11... | collective-permute-start | bytes 98312 | tf_op jit(solution)/shard_map/ppermute | solution.py:83

commit v5 on v4

--- a/solution.py
+++ b/solution.py
@@ -83,37 +83,28 @@
     return lax.ppermute(value, axis, pairs)
 
 
-PARTS = 2
+GROUP = 2
 
 
 def prep_kernel(kv_ref, out_ref, held, ready, in_sems, out_sems):
-    depth = PIECE // PARTS
-    heads = TP // PARTS
-
-    def fetch(receiver, part):
-        span = pl.ds(part * depth, depth)
-        return pltpu.make_async_copy(
-            kv_ref.at[receiver, span], held.at[receiver, span], in_sems.at[receiver, part]
-        )
-
-    def place(receiver, part):
-        span = pl.ds(part * heads, heads)
-        return pltpu.make_async_copy(
-            ready.at[receiver, span], out_ref.at[receiver, span], out_sems.at[receiver, part]
-        )
-
-    every = [(receiver, part) for receiver in range(CTX) for part in range(PARTS)]
-    for spot in every:
-        fetch(*spot).start()
-    for receiver in range(CTX):
-        for part in range(PARTS):
-            fetch(receiver, part).wait()
-        for part in range(PARTS):
-            for head in range(part * heads, (part + 1) * heads):
+    def fetch(index):
+        span = pl.ds(index * GROUP, GROUP)
+        return pltpu.make_async_copy(kv_ref.at[span], held.at[span], in_sems.at[index])
+
+    def place(index):
+        span = pl.ds(index * GROUP, GROUP)
+        return pltpu.make_async_copy(ready.at[span], out_ref.at[span], out_sems.at[index])
+
+    for index in range(CTX // GROUP):
+        fetch(index).start()
+    for index in range(CTX // GROUP):
+        fetch(index).wait()
+        for receiver in range(index * GROUP, (index + 1) * GROUP):
+            for head in range(TP):
                 ready[receiver, head] = held[receiver, :, :, pl.ds(head * HD, HD)]
-            place(receiver, part).start()
-    for spot in every:
-        place(*spot).wait()
+        place(index).start()
+    for index in range(CTX // GROUP):
+        place(index).wait()
 
 
 def prep(kv_cache):
@@ -126,8 +117,8 @@
         scratch_shapes=[
             pltpu.VMEM((CTX, PIECE, 2, TP * HD), jnp.bfloat16),
             pltpu.VMEM((CTX, TP, PIECE, 2, HD), jnp.bfloat16),
-            pltpu.SemaphoreType.DMA((CTX, PARTS)),
-            pltpu.SemaphoreType.DMA((CTX, PARTS)),
+            pltpu.SemaphoreType.DMA((CTX // GROUP,)),
+            pltpu.SemaphoreType.DMA((CTX // GROUP,)),
         ],
         compiler_params=pltpu.CompilerParams(vmem_limit_bytes=56 * 1024 * 1024),
         cost_estimate=pl.CostEstimate(
@@ -154,21 +145,16 @@
     part = info_ref[1]
     left = length - part * PIECE
 
-    def fetch(ctx, part):
-        span = pl.ds(part * (TP // PARTS), TP // PARTS)
-        return pltpu.make_async_copy(
-            kv_ref.at[ctx, span], held.at[ctx, span], in_sems.at[ctx, part]
-        )
-
-    def place(ctx, part):
-        span = pl.ds(part * (TP // PARTS), TP // PARTS)
-        return pltpu.make_async_copy(
-            held.at[ctx, span], kv_out_ref.at[ctx, span], out_sems.at[ctx, part]
-        )
-
-    every = [(ctx, part) for ctx in range(CTX) for part in range(PARTS)]
-    for spot in every:
-        fetch(*spot).start()
+    def fetch(index):
+        span = pl.ds(index * GROUP, GROUP)
+        return pltpu.make_async_copy(kv_ref.at[span], held.at[span], in_sems.at[index])
+
+    def place(index):
+        span = pl.ds(index * GROUP, GROUP)
+        return pltpu.make_async_copy(held.at[span], kv_out_ref.at[span], out_sems.at[index])
+
+    for index in range(CTX // GROUP):
+        fetch(index).start()
 
     row = lax.broadcasted_iota(jnp.int32, (HEAD_ROWS, HD), 0)
     lane = lax.broadcasted_iota(jnp.int32, (HEAD_ROWS, HD), 1)
@@ -199,9 +185,9 @@
     acc[...] = jnp.dot(weight.astype(jnp.bfloat16), values, preferred_element_type=jnp.float32)
 
     def arrive(chunk):
-        for spot in every[chunk * CHUNK_CTX * PARTS:(chunk + 1) * CHUNK_CTX * PARTS]:
-            fetch(*spot).wait()
-            place(*spot).start()
+        for index in range(chunk * CHUNK_CTX // GROUP, (chunk + 1) * CHUNK_CTX // GROUP):
+            fetch(index).wait()
+            place(index).start()
 
     def score(chunk):
         wide[...] = held[pl.ds(chunk * CHUNK_CTX, CHUNK_CTX)].reshape(CHUNK_ROWS, HD).astype(
@@ -272,8 +258,8 @@
     parts = jnp.where(place_in == 0, first, jnp.where(place_in == 1, second, third))
     out_ref[pl.ds(HEAD_ROWS, 16), :] = parts.astype(jnp.bfloat16)
 
-    for spot in every:
-        place(*spot).wait()
+    for index in range(CTX // GROUP):
+        place(index).wait()
 
 
 def attend(info, moved, sums, cosine, sine):
@@ -293,8 +279,8 @@
             pltpu.VMEM((HEAD_ROWS, HD), jnp.float32),
             pltpu.VMEM((HEAD_ROWS, HD), jnp.float32),
             pltpu.VMEM((HEAD_ROWS, HD), jnp.float32),
-            pltpu.SemaphoreType.DMA((CTX, PARTS)),
-            pltpu.SemaphoreType.DMA((CTX, PARTS)),
+            pltpu.SemaphoreType.DMA((CTX // GROUP,)),
+            pltpu.SemaphoreType.DMA((CTX // GROUP,)),
         ],
         out_shape=[
             jax.ShapeDtypeStruct((CTX, TP, 2 * PIECE, HD), jnp.bfloat16),

time: 103 us -> 102 us (level)
  transfers between devices with their start and end apart: 12 -> 12, of which waited for: 6 -> 6; matrix products, arithmetic and copies ran while one was open for 2% -> 2% of each run, Pallas kernels for 6% -> 5%
where the time goes in v5:
time: 102 us
  waiting for transfers between devices  47.8 us (47%)
  starting transfers between devices  29.4 us (29%)
  Pallas kernels  10.9 us (11%)
  blocking collectives  10 us (10%)
  other arithmetic  2.33 us (2%)
    ppermute x10, waiting for transfers between devices, swap(): return lax.ppermute(value, axis, pairs)  46.6 us
    ppermute x10, starting transfers between devices, swap(): return lax.ppermute(value, axis, pairs)  14.1 us
    all_to_all x1, starting transfers between devices, per_device(): lax.all_to_all(ready, everyone, split_axis=0, concat_axis=0, tiled=True)  12 us
    all_to_all x1, blocking collectives, per_device(): lax.all_to_all(states, ('x', 'y'), split_axis=0, concat_axis=0, tiled=True)  10 us
    pallas_call x1, Pallas kernels, prep(): pl.pallas_call(prep_kernel, out_shape=jax.ShapeDtypeStruct((CTX, TP, PIEC...  4.86 us
    pallas_call x1, Pallas kernels, attend(): pl.pallas_call(attend_kernel, in_specs=[pl.BlockSpec(memory_space=pltpu.S...  4.49 us
    ppermute x1, starting transfers between devices, per_device(): near = lax.ppermute(out, ('z', 'core'), pairs)  3.27 us
  transfers between devices with their start and end apart: 12, of which 6 were waited for; matrix products, arithmetic and copies ran while one was open for 2% of the time, Pallas kernels for 5%

profile of v5, /device:TPU:1, one launch (start us, length us, event | category | flops | bytes accessed | tf_op | source)
XLA Modules:
  0.0 102.0 jit_solution(10412859897785152018)
XLA Ops:
  0.6 4.9 %cache_by_receiver.1 = bf16[16,8,64,2,128]{4,3,2,1,0:T(2,128)(2,1)} custom-call(bf16[16,64,2,1024]{3,2,1,0:T(2,128)(2,1)} %bitcast.12), custom_call_target="tpu_custom_call" | custom-call | bytes 8388608 | tf_op jit(solution)/shard_map/cache_by_receiver/pallas_call | solution.py:112
  5.5 0.0 copy-start
  5.5 0.0 copy-start.2
  5.5 0.0 copy-start.3
  5.5 0.0 copy-start.1
  5.5 0.0 copy-start.4
  5.6 12.0 %all-to-all-start = ((bf16[128,128,128]{2,1,0:T(8,128)(2,1)}), bf16[128,128,128]{2,1,0:T(8,128)(2,1)}, u32[]{:S(2)}, u32[]{:S(2)}) async-start(bf16[128,128,128]{2,1,0:T(8,128)(2,1)} %bitcast.11), calls=%async_computation | async-start | bytes 8388608 | tf_op jit(solution)/shard_map/all_to_all | solution.py:361
  17.5 0.0 copy-done
  17.5 0.0 copy-done.2
  17.6 0.0 copy-done.3
  17.6 0.4 partial_projection.1
  18.0 1.4 %collective-permute-start = (f32[8,1408]{1,0:T(8,128)S(1)}, f32[8,1408]{1,0:T(8,128)S(1)}, u32[]{:S(2)}, u32[]{:S(2)}) collective-permute-start(f32[8,1408]{1,0:T(8,128)S(1)} %get-tuple-element.20), channel_id=1, source_target_pairs={{0,32},{32,0},{64,96},{96,64},{1,33},{33,1},{65,97},{97,65},{2,34}... | collective-permute-start | bytes 135176 | tf_op jit(solution)/shard_map/ppermute | solution.py:83
  19.4 2.4 %collective-permute-start.1 = (f32[8,1408]{1,0:T(8,128)S(1)}, f32[8,1408]{1,0:T(8,128)S(1)}, u32[]{:S(2)}, u32[]{:S(2)}) collective-permute-start(f32[8,1408]{1,0:T(8,128)S(1)} %get-tuple-element.21), channel_id=1, source_target_pairs={{0,64},{32,96},{64,0},{96,32},{1,65},{33,97},{65,1},{97,33},{2,66}... | collective-permute-start | bytes 135176 | tf_op jit(solution)/shard_map/ppermute | solution.py:83
  21.8 0.1 collective-permute-start.2
  21.9 0.0 copy-done.1
  21.9 2.0 %collective-permute-start.7 = (bf16[1024,512]{1,0:T(8,128)(2,1)S(1)}, bf16[1024,512]{1,0:T(8,128)(2,1)S(1)}, u32[]{:S(2)}, u32[]{:S(2)}) collective-permute-start(bf16[1024,512]{1,0:T(8,128)(2,1)S(1)} %copy-done.1), channel_id=1, source_target_pairs={{0,1},{1,0},{2,3},{3,2},{4,5},{5,4},{6,7},{7,6},{8,9},{9,8},{10,11... | collective-permute-start | bytes 3145736 | tf_op jit(solution)/shard_map/ppermute | solution.py:83
  23.8 0.0 copy-done.4
  23.8 0.7 dynamic_slice.11
  24.5 0.7 add_convert_fusion.1
  25.2 0.1 fusion
  25.4 0.1 pad_maximum_fusion
  25.4 39.1 %collective-permute-done = f32[8,1408]{1,0:T(8,128)S(1)} collective-permute-done((f32[8,1408]{1,0:T(8,128)S(1)}, f32[8,1408]{1,0:T(8,128)S(1)}, u32[]{:S(2)}, u32[]{:S(2)}) %collective-permute-start) | collective-permute-done | bytes 45088 | tf_op jit(solution)/shard_map/ppermute | solution.py:83
  64.6 2.5 %collective-permute-done.1 = f32[8,1408]{1,0:T(8,128)S(1)} collective-permute-done((f32[8,1408]{1,0:T(8,128)S(1)}, f32[8,1408]{1,0:T(8,128)S(1)}, u32[]{:S(2)}, u32[]{:S(2)}) %collective-permute-start.1) | collective-permute-done | bytes 45088 | tf_op jit(solution)/shard_map/ppermute | solution.py:83
  67.0 0.0 collective-permute-done.2
  67.1 2.8 %collective-permute-start.5 = (f32[4,1408]{1,0:T(4,128)S(1)}, f32[4,1408]{1,0:T(4,128)S(1)}, u32[]{:S(2)}, u32[]{:S(2)}) collective-permute-start(f32[4,1408]{1,0:T(4,128)S(1)} %get-tuple-element.26), channel_id=1, source_target_pairs={{0,16},{8,24},{16,0},{24,8},{1,17},{9,25},{17,1},{25,9},{2,18},{10... | collective-permute-start | bytes 67592 | tf_op jit(solution)/shard_map/ppermute | solution.py:83
  69.9 0.8 collective-permute-start.4
  70.7 0.0 collective-permute-start.3
  70.7 0.8 pad_add_fusion.info_ref
  71.4 0.0 collective-permute-done.5.third_ref
  71.4 2.3 %collective-permute-done.4.second_ref = f32[4,1408]{1,0:T(4,128)S(1)} collective-permute-done((f32[4,1408]{1,0:T(4,128)S(1)}, f32[4,1408]{1,0:T(4,128)S(1)}, u32[]{:S(2)}, u32[]{:S(2)}) %collective-permute-start.4) | collective-permute-done | bytes 22560 | tf_op jit(solution)/shard_map/ppermute | solution.py:83
  73.8 0.0 collective-permute-done.3.first_ref
  73.8 0.0 all-to-all-done
  73.8 4.5 %attend.1 = (bf16[16,8,128,128]{3,2,1,0:T(8,128)(2,1)}, bf16[48,128]{1,0:T(8,128)(2,1)S(1)}) custom-call(s32[2]{0:T(128)S(1)} %pad_add_fusion.info_ref, bf16[16,8,128,128]{3,2,1,0:T(8,128)(2,1)} %bitcast.3.kv_ref, f32[4,1408]{1,0:T(4,128)S(1)} %get-tuple-element.27.own_ref, f32[4,1408]{1,0:T(4,128)S(1)} %collective-permute-done.3.first_ref, ...), custom_call_target="tpu_custom_call" | custom-call | tf_op jit(solution)/shard_map/attend/pallas_call | solution.py:268
  78.3 10.0 %all_to_all.10.states_ref = bf16[16,48,128]{2,1,0:T(8,128)(2,1)S(1)} all-to-all(bf16[16,48,128]{2,1,0:T(8,128)(2,1)S(1)} %broadcast_in_dim.2), channel_id=1, replica_groups=mesh['x'=4,'y'=4,'z'=4,'core'=2] {'x','y'}, dimensions={0} | all-to-all | bytes 393216 | tf_op jit(solution)/shard_map/all_to_all | solution.py:384
  88.3 3.8 %collective-permute-start.6 = (bf16[16,48,128]{2,1,0:T(8,128)(2,1)S(1)}, bf16[16,48,128]{2,1,0:T(8,128)(2,1)S(1)}, u32[]{:S(2)}, u32[]{:S(2)}) collective-permute-start(bf16[16,48,128]{2,1,0:T(8,128)(2,1)S(1)} %all_to_all.10.states_ref), channel_id=1, source_target_pairs={{0,1},{1,0},{2,3},{3,2},{4,5},{5,4},{6,7},{7,6},{8,9},{9,8},{10,11... | collective-permute-start | bytes 589832 | tf_op jit(solution)/shard_map/ppermute | solution.py:83
  92.1 0.6 project.2.refs_0_
  92.7 0.0 collective-permute-done.7.w_ref
  92.7 0.5 collective-permute-done.6.states_ref
  93.2 0.6 project.3
  93.8 3.3 %collective-permute-start.8 = (bf16[32,512]{1,0:T(8,128)(2,1)S(1)}, bf16[32,512]{1,0:T(8,128)(2,1)S(1)}, u32[]{:S(2)}, u32[]{:S(2)}) collective-permute-start(bf16[32,512]{1,0:T(8,128)(2,1)S(1)} %project.3), channel_id=1, source_target_pairs={{0,2},{1,7},{2,0},{3,5},{4,6},{5,3},{6,4},{7,1},{8,10},{9,15},{10,... | collective-permute-start | bytes 98312 | tf_op jit(solution)/shard_map/ppermute | solution.py:388
  97.1 0.1 collective-permute-start.10
  97.2 1.2 %collective-permute-done.8 = bf16[32,512]{1,0:T(8,128)(2,1)S(1)} collective-permute-done((bf16[32,512]{1,0:T(8,128)(2,1)S(1)}, bf16[32,512]{1,0:T(8,128)(2,1)S(1)}, u32[]{:S(2)}, u32[]{:S(2)}) %collective-permute-start.8) | collective-permute-done | bytes 32800 | tf_op jit(solution)/shard_map/ppermute | solution.py:388
  98.4 0.8 collective-permute-start.9
  99.2 2.1 %collective-permute-done.10 = bf16[32,512]{1,0:T(8,128)(2,1)S(1)} collective-permute-done((bf16[32,512]{1,0:T(8,128)(2,1)S(1)}, bf16[32,512]{1,0:T(8,128)(2,1)S(1)}, u32[]{:S(2)}, u32[]{:S(2)}) %collective-permute-start.10) | collective-permute-done | bytes 32800 | tf_op jit(solution)/shard_map/ppermute | solution.py:83
  101.3 0.0 collective-permute-done.9
  101.3 0.6 add_convert_fusion
  (5 shorter events, 0.1 us)
Async XLA Ops:
  5.5 12.0 %copy-start = (bf16[512,1280]{1,0:T(8,128)(2,1)S(1)}, bf16[512,1280]{1,0:T(8,128)(2,1)}, u32[]{:S(2)}) copy-start(bf16[512,1280]{1,0:T(8,128)(2,1)} %w_ref.1) | copy-start | bytes 3932164
  5.5 12.0 %copy-start.2 = (bf16[32,512]{1,0:T(8,128)(2,1)S(1)}, bf16[32,512]{1,0:T(8,128)(2,1)}, u32[]{:S(2)}) copy-start(bf16[32,512]{1,0:T(8,128)(2,1)} %hidden_ref) | copy-start | bytes 98308
  5.5 12.0 %copy-start.3 = (bf16[512]{0:T(512)(128)(2,1)S(1)}, bf16[512]{0:T(512)(128)(2,1)}, u32[]{:S(2)}) copy-start(bf16[512]{0:T(512)(128)(2,1)} %gain_ref.1) | copy-start | bytes 3076
  5.5 16.3 %copy-start.1 = (bf16[1024,512]{1,0:T(8,128)(2,1)S(1)}, bf16[1024,512]{1,0:T(8,128)(2,1)}, u32[]{:S(2)}) copy-start(bf16[1024,512]{1,0:T(8,128)(2,1)} %w_ref.2) | copy-start | bytes 3145732
  5.5 18.3 %copy-start.4 = (s32[8]{0:T(128)S(1)}, s32[8]{0:T(128)}, u32[]{:S(2)}) copy-start(s32[8]{0:T(128)} %param.8) | copy-start | bytes 100
  5.6 68.2 %all-to-all-start = ((bf16[128,128,128]{2,1,0:T(8,128)(2,1)}), bf16[128,128,128]{2,1,0:T(8,128)(2,1)}, u32[]{:S(2)}, u32[]{:S(2)}) async-start(bf16[128,128,128]{2,1,0:T(8,128)(2,1)} %bitcast.11), calls=%async_computation | async-start | bytes 8388608 | tf_op jit(solution)/shard_map/all_to_all | solution.py:361
  18.0 46.6 %collective-permute-start = (f32[8,1408]{1,0:T(8,128)S(1)}, f32[8,1408]{1,0:T(8,128)S(1)}, u32[]{:S(2)}, u32[]{:S(2)}) collective-permute-start(f32[8,1408]{1,0:T(8,128)S(1)} %get-tuple-element.20), channel_id=1, source_target_pairs={{0,32},{32,0},{64,96},{96,64},{1,33},{33,1},{65,97},{97,65},{2,34}... | collective-permute-start | bytes 135176 | tf_op jit(solution)/shard_map/ppermute | solution.py:83
  19.4 47.7 %collective-permute-start.1 = (f32[8,1408]{1,0:T(8,128)S(1)}, f32[8,1408]{1,0:T(8,128)S(1)}, u32[]{:S(2)}, u32[]{:S(2)}) collective-permute-start(f32[8,1408]{1,0:T(8,128)S(1)} %get-tuple-element.21), channel_id=1, source_target_pairs={{0,64},{32,96},{64,0},{96,32},{1,65},{33,97},{65,1},{97,33},{2,66}... | collective-permute-start | bytes 135176 | tf_op jit(solution)/shard_map/ppermute | solution.py:83
  21.8 45.3 %collective-permute-start.2 = (f32[8,1408]{1,0:T(8,128)S(1)}, f32[8,1408]{1,0:T(8,128)S(1)}, u32[]{:S(2)}, u32[]{:S(2)}) collective-permute-start(f32[8,1408]{1,0:T(8,128)S(1)} %get-tuple-element.22), channel_id=1, source_target_pairs={{0,96},{32,64},{64,32},{96,0},{1,97},{33,65},{65,33},{97,1},{2,98}... | collective-permute-start | bytes 135176 | tf_op jit(solution)/shard_map/ppermute | solution.py:83
  21.9 70.9 %collective-permute-start.7 = (bf16[1024,512]{1,0:T(8,128)(2,1)S(1)}, bf16[1024,512]{1,0:T(8,128)(2,1)S(1)}, u32[]{:S(2)}, u32[]{:S(2)}) collective-permute-start(bf16[1024,512]{1,0:T(8,128)(2,1)S(1)} %copy-done.1), channel_id=1, source_target_pairs={{0,1},{1,0},{2,3},{3,2},{4,5},{5,4},{6,7},{7,6},{8,9},{9,8},{10,11... | collective-permute-start | bytes 3145736 | tf_op jit(solution)/shard_map/ppermute | solution.py:83
  67.1 4.3 %collective-permute-start.5 = (f32[4,1408]{1,0:T(4,128)S(1)}, f32[4,1408]{1,0:T(4,128)S(1)}, u32[]{:S(2)}, u32[]{:S(2)}) collective-permute-start(f32[4,1408]{1,0:T(4,128)S(1)} %get-tuple-element.26), channel_id=1, source_target_pairs={{0,16},{8,24},{16,0},{24,8},{1,17},{9,25},{17,1},{25,9},{2,18},{10... | collective-permute-start | bytes 67592 | tf_op jit(solution)/shard_map/ppermute | solution.py:83
  69.9 3.9 %collective-permute-start.4 = (f32[4,1408]{1,0:T(4,128)S(1)}, f32[4,1408]{1,0:T(4,128)S(1)}, u32[]{:S(2)}, u32[]{:S(2)}) collective-permute-start(f32[4,1408]{1,0:T(4,128)S(1)} %get-tuple-element.26), channel_id=1, source_target_pairs={{0,24},{8,16},{16,8},{24,0},{1,25},{9,17},{17,9},{25,1},{2,26},{10... | collective-permute-start | bytes 67592 | tf_op jit(solution)/shard_map/ppermute | solution.py:83
  70.7 3.1 %collective-permute-start.3 = (f32[4,1408]{1,0:T(4,128)S(1)}, f32[4,1408]{1,0:T(4,128)S(1)}, u32[]{:S(2)}, u32[]{:S(2)}) collective-permute-start(f32[4,1408]{1,0:T(4,128)S(1)} %get-tuple-element.27.own_ref), channel_id=1, source_target_pairs={{0,8},{8,0},{16,24},{24,16},{1,9},{9,1},{17,25},{25,17},{2,10},{10... | collective-permute-start | bytes 67592 | tf_op jit(solution)/shard_map/ppermute | solution.py:83
  88.3 4.9 %collective-permute-start.6 = (bf16[16,48,128]{2,1,0:T(8,128)(2,1)S(1)}, bf16[16,48,128]{2,1,0:T(8,128)(2,1)S(1)}, u32[]{:S(2)}, u32[]{:S(2)}) collective-permute-start(bf16[16,48,128]{2,1,0:T(8,128)(2,1)S(1)} %all_to_all.10.states_ref), channel_id=1, source_target_pairs={{0,1},{1,0},{2,3},{3,2},{4,5},{5,4},{6,7},{7,6},{8,9},{9,8},{10,11... | collective-permute-start | bytes 589832 | tf_op jit(solution)/shard_map/ppermute | solution.py:83
  93.8 4.6 %collective-permute-start.8 = (bf16[32,512]{1,0:T(8,128)(2,1)S(1)}, bf16[32,512]{1,0:T(8,128)(2,1)S(1)}, u32[]{:S(2)}, u32[]{:S(2)}) collective-permute-start(bf16[32,512]{1,0:T(8,128)(2,1)S(1)} %project.3), channel_id=1, source_target_pairs={{0,2},{1,7},{2,0},{3,5},{4,6},{5,3},{6,4},{7,1},{8,10},{9,15},{10,... | collective-permute-start | bytes 98312 | tf_op jit(solution)/shard_map/ppermute | solution.py:388
  97.1 4.3 %collective-permute-start.10 = (bf16[32,512]{1,0:T(8,128)(2,1)S(1)}, bf16[32,512]{1,0:T(8,128)(2,1)S(1)}, u32[]{:S(2)}, u32[]{:S(2)}) collective-permute-start(bf16[32,512]{1,0:T(8,128)(2,1)S(1)} %project.3), channel_id=1, source_target_pairs={{0,4},{2,6},{4,0},{6,2},{1,5},{3,7},{5,1},{7,3},{8,12},{10,14},{12... | collective-permute-start | bytes 98312 | tf_op jit(solution)/shard_map/ppermute | solution.py:83
  98.4 3.0 %collective-permute-start.9 = (bf16[32,512]{1,0:T(8,128)(2,1)S(1)}, bf16[32,512]{1,0:T(8,128)(2,1)S(1)}, u32[]{:S(2)}, u32[]{:S(2)}) collective-permute-start(bf16[32,512]{1,0:T(8,128)(2,1)S(1)} %collective-permute-done.8), channel_id=1, source_target_pairs={{0,1},{1,0},{2,3},{3,2},{4,5},{5,4},{6,7},{7,6},{8,9},{9,8},{10,11... | collective-permute-start | bytes 98312 | tf_op jit(solution)/shard_map/ppermute | solution.py:83

commit v6 on v5

--- a/solution.py
+++ b/solution.py
@@ -136,11 +136,53 @@
 STATE_ROWS = HEAD_ROWS + 16
 
 
+EARLY = CTX // GROUP // 2
+
+
+def copy_kernel(kv_ref, out_ref, held, in_sems, out_sems):
+    def fetch(index):
+        span = pl.ds(index * GROUP, GROUP)
+        return pltpu.make_async_copy(kv_ref.at[span], held.at[span], in_sems.at[index])
+
+    def place(index):
+        span = pl.ds(index * GROUP, GROUP)
+        return pltpu.make_async_copy(held.at[span], out_ref.at[span], out_sems.at[index])
+
+    for index in range(EARLY):
+        fetch(index).start()
+    for index in range(EARLY):
+        fetch(index).wait()
+        place(index).start()
+    for index in range(EARLY):
+        place(index).wait()
+
+
+def copy_first(moved):
+    anywhere = pl.BlockSpec(memory_space=pl.ANY)
+    return pl.pallas_call(
+        copy_kernel,
+        in_specs=[anywhere],
+        out_specs=anywhere,
+        scratch_shapes=[
+            pltpu.VMEM((EARLY * GROUP,) + moved.shape[1:], moved.dtype),
+            pltpu.SemaphoreType.DMA((EARLY,)),
+            pltpu.SemaphoreType.DMA((EARLY,)),
+        ],
+        out_shape=jax.ShapeDtypeStruct(moved.shape, moved.dtype),
+        compiler_params=pltpu.CompilerParams(vmem_limit_bytes=56 * 1024 * 1024),
+        cost_estimate=pl.CostEstimate(
+            flops=0, transcendentals=0, bytes_accessed=2 * moved.size
+        ),
+        name="copy_first",
+    )(moved)
+
+
 def attend_kernel(
-    info_ref, kv_ref, own_ref, first_ref, second_ref, third_ref, cos_ref, sin_ref,
+    info_ref, kv_ref, own_ref, first_ref, second_ref, third_ref, cos_ref, sin_ref, part_ref,
     kv_out_ref, out_ref,
     held, wide, pairs, query, scores, peaks, top, total, acc, in_sems, out_sems,
 ):
+    del part_ref
     length = info_ref[0]
     part = info_ref[1]
     left = length - part * PIECE
@@ -187,7 +229,8 @@
     def arrive(chunk):
         for index in range(chunk * CHUNK_CTX // GROUP, (chunk + 1) * CHUNK_CTX // GROUP):
             fetch(index).wait()
-            place(index).start()
+            if index >= EARLY:
+                place(index).start()
 
     def score(chunk):
         wide[...] = held[pl.ds(chunk * CHUNK_CTX, CHUNK_CTX)].reshape(CHUNK_ROWS, HD).astype(
@@ -258,16 +301,17 @@
     parts = jnp.where(place_in == 0, first, jnp.where(place_in == 1, second, third))
     out_ref[pl.ds(HEAD_ROWS, 16), :] = parts.astype(jnp.bfloat16)
 
-    for index in range(CTX // GROUP):
+    for index in range(EARLY, CTX // GROUP):
         place(index).wait()
 
 
-def attend(info, moved, sums, cosine, sine):
+def attend(info, moved, sums, cosine, sine, copied):
     anywhere = pl.BlockSpec(memory_space=pl.ANY)
     vmem = pl.BlockSpec(memory_space=pltpu.VMEM)
     return pl.pallas_call(
         attend_kernel,
-        in_specs=[pl.BlockSpec(memory_space=pltpu.SMEM), anywhere] + [vmem] * 6,
+        in_specs=[pl.BlockSpec(memory_space=pltpu.SMEM), anywhere] + [vmem] * 6 + [anywhere],
+        input_output_aliases={8: 0},
         out_specs=[anywhere, vmem],
         scratch_shapes=[
             pltpu.VMEM((CTX, TP, 2 * PIECE, HD), jnp.bfloat16),
@@ -288,7 +332,7 @@
         ],
         compiler_params=pltpu.CompilerParams(vmem_limit_bytes=24 * 1024 * 1024),
         name="attend",
-    )(info, moved, *sums, cosine, sine)
+    )(info, moved, *sums, cosine, sine, copied)
 
 
 def project_kernel(states_ref, w_ref, *refs):
@@ -377,7 +421,7 @@
     cosine = jnp.concatenate([cosine, cosine], axis=1)
     sine = jnp.concatenate([-sine, sine], axis=1)
     info = jnp.stack([length, part]).astype(jnp.int32)
-    kv_decode, state = attend(info, moved, sums, cosine, sine)
+    kv_decode, state = attend(info, moved, sums, cosine, sine, copy_first(moved))
     kv_decode = kv_decode.reshape(1, SOURCES, PIECE, 2, HD)
 
     states = jnp.broadcast_to(state[None], (CTX, STATE_ROWS, HD))

time: 102 us -> 103 us (level)
  Pallas kernels: 10.9 us -> 13.4 us
  waiting for transfers between devices: 47.8 us -> 45.5 us
  blocking collectives: 10 us -> 11.5 us
  starting transfers between devices: 29.4 us -> 28.3 us
    pallas_call x0 -> x1, Pallas kernels: none -> 2.42 us  [copy_first(): pl.pallas_call(copy_kernel, in_specs=[anywhere], out_specs=anywhere, scra...]
    ppermute x10, waiting for transfers between devices: 46.6 us -> 44.3 us  [swap(): return lax.ppermute(value, axis, pairs)]
    all_to_all x1, blocking collectives: 10 us -> 11.5 us  [per_device(): lax.all_to_all(states, ('x', 'y'), split_axis=0, concat_axis=0, tiled=True)]
    ppermute x10, starting transfers between devices: 14.1 us -> 13.1 us  [swap(): return lax.ppermute(value, axis, pairs)]
  transfers between devices with their start and end apart: 12 -> 12, of which waited for: 6 -> 6; matrix products, arithmetic and copies ran while one was open for 2% -> 2% of each run, Pallas kernels for 5% -> 8%
where the time goes in v6:
time: 103 us
  waiting for transfers between devices  45.5 us (44%)
  starting transfers between devices  28.3 us (27%)
  Pallas kernels  13.4 us (13%)
  blocking collectives  11.5 us (11%)
  other arithmetic  2.33 us (2%)
    ppermute x10, waiting for transfers between devices, swap(): return lax.ppermute(value, axis, pairs)  44.3 us
    ppermute x10, starting transfers between devices, swap(): return lax.ppermute(value, axis, pairs)  13.1 us
    all_to_all x1, starting transfers between devices, per_device(): lax.all_to_all(ready, everyone, split_axis=0, concat_axis=0, tiled=True)  12 us
    all_to_all x1, blocking collectives, per_device(): lax.all_to_all(states, ('x', 'y'), split_axis=0, concat_axis=0, tiled=True)  11.5 us
    pallas_call x1, Pallas kernels, prep(): pl.pallas_call(prep_kernel, out_shape=jax.ShapeDtypeStruct((CTX, TP, PIEC...  4.86 us
    pallas_call x1, Pallas kernels, attend(): pl.pallas_call(attend_kernel, in_specs=[pl.BlockSpec(memory_space=pltpu.S...  4.5 us
    ppermute x1, starting transfers between devices, per_device(): near = lax.ppermute(out, ('z', 'core'), pairs)  3.27 us
    pallas_call x1, Pallas kernels, copy_first(): pl.pallas_call(copy_kernel, in_specs=[anywhere], out_specs=anywhere, scra...  2.42 us
  transfers between devices with their start and end apart: 12, of which 6 were waited for; matrix products, arithmetic and copies ran while one was open for 2% of the time, Pallas kernels for 8%

profile of v6, /device:TPU:1, one launch (start us, length us, event | category | flops | bytes accessed | tf_op | source)
XLA Modules:
  0.0 102.5 jit_solution(12236530895647599672)
XLA Ops:
  0.6 4.9 %cache_by_receiver.1 = bf16[16,8,64,2,128]{4,3,2,1,0:T(2,128)(2,1)} custom-call(bf16[16,64,2,1024]{3,2,1,0:T(2,128)(2,1)} %bitcast.13), custom_call_target="tpu_custom_call" | custom-call | bytes 8388608 | tf_op jit(solution)/shard_map/cache_by_receiver/pallas_call | solution.py:112
  5.5 0.0 copy-start
  5.5 0.0 copy-start.2
  5.5 0.0 copy-start.3
  5.5 0.0 copy-start.1
  5.5 0.0 copy-start.4
  5.6 12.0 %all-to-all-start = ((bf16[128,128,128]{2,1,0:T(8,128)(2,1)}), bf16[128,128,128]{2,1,0:T(8,128)(2,1)}, u32[]{:S(2)}, u32[]{:S(2)}) async-start(bf16[128,128,128]{2,1,0:T(8,128)(2,1)} %bitcast.12), calls=%async_computation | async-start | bytes 8388608 | tf_op jit(solution)/shard_map/all_to_all | solution.py:405
  17.5 0.0 copy-done
  17.5 0.0 copy-done.2
  17.6 0.0 copy-done.3
  17.6 0.4 partial_projection.1
  18.0 1.4 %collective-permute-start = (f32[8,1408]{1,0:T(8,128)S(1)}, f32[8,1408]{1,0:T(8,128)S(1)}, u32[]{:S(2)}, u32[]{:S(2)}) collective-permute-start(f32[8,1408]{1,0:T(8,128)S(1)} %get-tuple-element.20), channel_id=1, source_target_pairs={{0,32},{32,0},{64,96},{96,64},{1,33},{33,1},{65,97},{97,65},{2,34}... | collective-permute-start | bytes 135176 | tf_op jit(solution)/shard_map/ppermute | solution.py:83
  19.4 2.4 %collective-permute-start.1 = (f32[8,1408]{1,0:T(8,128)S(1)}, f32[8,1408]{1,0:T(8,128)S(1)}, u32[]{:S(2)}, u32[]{:S(2)}) collective-permute-start(f32[8,1408]{1,0:T(8,128)S(1)} %get-tuple-element.21), channel_id=1, source_target_pairs={{0,64},{32,96},{64,0},{96,32},{1,65},{33,97},{65,1},{97,33},{2,66}... | collective-permute-start | bytes 135176 | tf_op jit(solution)/shard_map/ppermute | solution.py:83
  21.8 0.1 collective-permute-start.2
  21.9 0.0 copy-done.1
  21.9 2.0 %collective-permute-start.7 = (bf16[1024,512]{1,0:T(8,128)(2,1)S(1)}, bf16[1024,512]{1,0:T(8,128)(2,1)S(1)}, u32[]{:S(2)}, u32[]{:S(2)}) collective-permute-start(bf16[1024,512]{1,0:T(8,128)(2,1)S(1)} %copy-done.1), channel_id=1, source_target_pairs={{0,1},{1,0},{2,3},{3,2},{4,5},{5,4},{6,7},{7,6},{8,9},{9,8},{10,11... | collective-permute-start | bytes 3145736 | tf_op jit(solution)/shard_map/ppermute | solution.py:83
  23.8 0.0 copy-done.4
  23.8 0.7 dynamic_slice.11
  24.5 0.7 add_convert_fusion.1
  25.2 0.1 fusion
  25.4 0.1 pad_maximum_fusion
  25.4 39.1 %collective-permute-done = f32[8,1408]{1,0:T(8,128)S(1)} collective-permute-done((f32[8,1408]{1,0:T(8,128)S(1)}, f32[8,1408]{1,0:T(8,128)S(1)}, u32[]{:S(2)}, u32[]{:S(2)}) %collective-permute-start) | collective-permute-done | bytes 45088 | tf_op jit(solution)/shard_map/ppermute | solution.py:83
  64.6 2.5 %collective-permute-done.1 = f32[8,1408]{1,0:T(8,128)S(1)} collective-permute-done((f32[8,1408]{1,0:T(8,128)S(1)}, f32[8,1408]{1,0:T(8,128)S(1)}, u32[]{:S(2)}, u32[]{:S(2)}) %collective-permute-start.1) | collective-permute-done | bytes 45088 | tf_op jit(solution)/shard_map/ppermute | solution.py:83
  67.0 0.0 collective-permute-done.2
  67.1 2.5 %collective-permute-start.4 = (f32[4,1408]{1,0:T(4,128)S(1)}, f32[4,1408]{1,0:T(4,128)S(1)}, u32[]{:S(2)}, u32[]{:S(2)}) collective-permute-start(f32[4,1408]{1,0:T(4,128)S(1)} %get-tuple-element.26), channel_id=1, source_target_pairs={{0,24},{8,16},{16,8},{24,0},{1,25},{9,17},{17,9},{25,1},{2,26},{10... | collective-permute-start | bytes 67592 | tf_op jit(solution)/shard_map/ppermute | solution.py:83
  69.6 0.5 collective-permute-start.5
  70.1 0.4 collective-permute-start.3
  70.4 0.8 pad_add_fusion.info_ref
  71.2 0.0 all-to-all-done
  71.2 2.4 %copy_first.1.part_ref = bf16[16,8,128,128]{3,2,1,0:T(8,128)(2,1)} custom-call(bf16[16,8,128,128]{3,2,1,0:T(8,128)(2,1)} %bitcast.3.kv_ref), custom_call_target="tpu_custom_call" | custom-call | bytes 4194304 | tf_op jit(solution)/shard_map/copy_first/pallas_call | solution.py:162
  73.6 0.0 collective-permute-done.3.first_ref
  73.6 0.0 collective-permute-done.4.second_ref
  73.7 0.1 collective-permute-done.5.third_ref
  73.7 4.5 %attend.1 = (bf16[16,8,128,128]{3,2,1,0:T(8,128)(2,1)}, bf16[48,128]{1,0:T(8,128)(2,1)S(1)}) custom-call(s32[2]{0:T(128)S(1)} %pad_add_fusion.info_ref, bf16[16,8,128,128]{3,2,1,0:T(8,128)(2,1)} %bitcast.3.kv_ref, f32[4,1408]{1,0:T(4,128)S(1)} %get-tuple-element.27.own_ref, ...), custom_call_target="tpu_custom_call", output_to_operand_aliasing={{0}: (8, {})} | custom-call | tf_op jit(solution)/shard_map/attend/pallas_call | solution.py:311
  78.3 11.5 %all_to_all.10.states_ref = bf16[16,48,128]{2,1,0:T(8,128)(2,1)S(1)} all-to-all(bf16[16,48,128]{2,1,0:T(8,128)(2,1)S(1)} %broadcast_in_dim.2), channel_id=1, replica_groups=mesh['x'=4,'y'=4,'z'=4,'core'=2] {'x','y'}, dimensions={0} | all-to-all | bytes 393216 | tf_op jit(solution)/shard_map/all_to_all | solution.py:428
  89.7 2.9 %collective-permute-start.6 = (bf16[16,48,128]{2,1,0:T(8,128)(2,1)S(1)}, bf16[16,48,128]{2,1,0:T(8,128)(2,1)S(1)}, u32[]{:S(2)}, u32[]{:S(2)}) collective-permute-start(bf16[16,48,128]{2,1,0:T(8,128)(2,1)S(1)} %all_to_all.10.states_ref), channel_id=1, source_target_pairs={{0,1},{1,0},{2,3},{3,2},{4,5},{5,4},{6,7},{7,6},{8,9},{9,8},{10,11... | collective-permute-start | bytes 589832 | tf_op jit(solution)/shard_map/ppermute | solution.py:83
  92.7 0.6 project.2.refs_0_
  93.3 0.0 collective-permute-done.7.w_ref
  93.3 0.5 collective-permute-done.6.states_ref
  93.7 0.6 project.3
  94.3 3.3 %collective-permute-start.8 = (bf16[32,512]{1,0:T(8,128)(2,1)S(1)}, bf16[32,512]{1,0:T(8,128)(2,1)S(1)}, u32[]{:S(2)}, u32[]{:S(2)}) collective-permute-start(bf16[32,512]{1,0:T(8,128)(2,1)S(1)} %project.3), channel_id=1, source_target_pairs={{0,2},{1,7},{2,0},{3,5},{4,6},{5,3},{6,4},{7,1},{8,10},{9,15},{10,... | collective-permute-start | bytes 98312 | tf_op jit(solution)/shard_map/ppermute | solution.py:432
  97.6 0.1 collective-permute-start.10
  97.7 1.2 %collective-permute-done.8 = bf16[32,512]{1,0:T(8,128)(2,1)S(1)} collective-permute-done((bf16[32,512]{1,0:T(8,128)(2,1)S(1)}, bf16[32,512]{1,0:T(8,128)(2,1)S(1)}, u32[]{:S(2)}, u32[]{:S(2)}) %collective-permute-start.8) | collective-permute-done | bytes 32800 | tf_op jit(solution)/shard_map/ppermute | solution.py:432
  98.9 0.8 collective-permute-start.9
  99.7 2.2 %collective-permute-done.10 = bf16[32,512]{1,0:T(8,128)(2,1)S(1)} collective-permute-done((bf16[32,512]{1,0:T(8,128)(2,1)S(1)}, bf16[32,512]{1,0:T(8,128)(2,1)S(1)}, u32[]{:S(2)}, u32[]{:S(2)}) %collective-permute-start.10) | collective-permute-done | bytes 32800 | tf_op jit(solution)/shard_map/ppermute | solution.py:83
  101.9 0.0 collective-permute-done.9
  101.9 0.6 add_convert_fusion
  (5 shorter events, 0.1 us)
Async XLA Ops:
  5.5 12.0 %copy-start = (bf16[512,1280]{1,0:T(8,128)(2,1)S(1)}, bf16[512,1280]{1,0:T(8,128)(2,1)}, u32[]{:S(2)}) copy-start(bf16[512,1280]{1,0:T(8,128)(2,1)} %w_ref.1) | copy-start | bytes 3932164
  5.5 12.0 %copy-start.2 = (bf16[32,512]{1,0:T(8,128)(2,1)S(1)}, bf16[32,512]{1,0:T(8,128)(2,1)}, u32[]{:S(2)}) copy-start(bf16[32,512]{1,0:T(8,128)(2,1)} %hidden_ref) | copy-start | bytes 98308
  5.5 12.0 %copy-start.3 = (bf16[512]{0:T(512)(128)(2,1)S(1)}, bf16[512]{0:T(512)(128)(2,1)}, u32[]{:S(2)}) copy-start(bf16[512]{0:T(512)(128)(2,1)} %gain_ref.1) | copy-start | bytes 3076
  5.5 16.3 %copy-start.1 = (bf16[1024,512]{1,0:T(8,128)(2,1)S(1)}, bf16[1024,512]{1,0:T(8,128)(2,1)}, u32[]{:S(2)}) copy-start(bf16[1024,512]{1,0:T(8,128)(2,1)} %w_ref.2) | copy-start | bytes 3145732
  5.5 18.3 %copy-start.4 = (s32[8]{0:T(128)S(1)}, s32[8]{0:T(128)}, u32[]{:S(2)}) copy-start(s32[8]{0:T(128)} %param.8) | copy-start | bytes 100
  5.6 65.7 %all-to-all-start = ((bf16[128,128,128]{2,1,0:T(8,128)(2,1)}), bf16[128,128,128]{2,1,0:T(8,128)(2,1)}, u32[]{:S(2)}, u32[]{:S(2)}) async-start(bf16[128,128,128]{2,1,0:T(8,128)(2,1)} %bitcast.12), calls=%async_computation | async-start | bytes 8388608 | tf_op jit(solution)/shard_map/all_to_all | solution.py:405
  18.0 46.6 %collective-permute-start = (f32[8,1408]{1,0:T(8,128)S(1)}, f32[8,1408]{1,0:T(8,128)S(1)}, u32[]{:S(2)}, u32[]{:S(2)}) collective-permute-start(f32[8,1408]{1,0:T(8,128)S(1)} %get-tuple-element.20), channel_id=1, source_target_pairs={{0,32},{32,0},{64,96},{96,64},{1,33},{33,1},{65,97},{97,65},{2,34}... | collective-permute-start | bytes 135176 | tf_op jit(solution)/shard_map/ppermute | solution.py:83
  19.4 47.7 %collective-permute-start.1 = (f32[8,1408]{1,0:T(8,128)S(1)}, f32[8,1408]{1,0:T(8,128)S(1)}, u32[]{:S(2)}, u32[]{:S(2)}) collective-permute-start(f32[8,1408]{1,0:T(8,128)S(1)} %get-tuple-element.21), channel_id=1, source_target_pairs={{0,64},{32,96},{64,0},{96,32},{1,65},{33,97},{65,1},{97,33},{2,66}... | collective-permute-start | bytes 135176 | tf_op jit(solution)/shard_map/ppermute | solution.py:83
  21.8 45.3 %collective-permute-start.2 = (f32[8,1408]{1,0:T(8,128)S(1)}, f32[8,1408]{1,0:T(8,128)S(1)}, u32[]{:S(2)}, u32[]{:S(2)}) collective-permute-start(f32[8,1408]{1,0:T(8,128)S(1)} %get-tuple-element.22), channel_id=1, source_target_pairs={{0,96},{32,64},{64,32},{96,0},{1,97},{33,65},{65,33},{97,1},{2,98}... | collective-permute-start | bytes 135176 | tf_op jit(solution)/shard_map/ppermute | solution.py:83
  21.9 71.4 %collective-permute-start.7 = (bf16[1024,512]{1,0:T(8,128)(2,1)S(1)}, bf16[1024,512]{1,0:T(8,128)(2,1)S(1)}, u32[]{:S(2)}, u32[]{:S(2)}) collective-permute-start(bf16[1024,512]{1,0:T(8,128)(2,1)S(1)} %copy-done.1), channel_id=1, source_target_pairs={{0,1},{1,0},{2,3},{3,2},{4,5},{5,4},{6,7},{7,6},{8,9},{9,8},{10,11... | collective-permute-start | bytes 3145736 | tf_op jit(solution)/shard_map/ppermute | solution.py:83
  67.1 6.5 %collective-permute-start.4 = (f32[4,1408]{1,0:T(4,128)S(1)}, f32[4,1408]{1,0:T(4,128)S(1)}, u32[]{:S(2)}, u32[]{:S(2)}) collective-permute-start(f32[4,1408]{1,0:T(4,128)S(1)} %get-tuple-element.26), channel_id=1, source_target_pairs={{0,24},{8,16},{16,8},{24,0},{1,25},{9,17},{17,9},{25,1},{2,26},{10... | collective-permute-start | bytes 67592 | tf_op jit(solution)/shard_map/ppermute | solution.py:83
  69.6 4.2 %collective-permute-start.5 = (f32[4,1408]{1,0:T(4,128)S(1)}, f32[4,1408]{1,0:T(4,128)S(1)}, u32[]{:S(2)}, u32[]{:S(2)}) collective-permute-start(f32[4,1408]{1,0:T(4,128)S(1)} %get-tuple-element.26), channel_id=1, source_target_pairs={{0,16},{8,24},{16,0},{24,8},{1,17},{9,25},{17,1},{25,9},{2,18},{10... | collective-permute-start | bytes 67592 | tf_op jit(solution)/shard_map/ppermute | solution.py:83
  70.1 3.6 %collective-permute-start.3 = (f32[4,1408]{1,0:T(4,128)S(1)}, f32[4,1408]{1,0:T(4,128)S(1)}, u32[]{:S(2)}, u32[]{:S(2)}) collective-permute-start(f32[4,1408]{1,0:T(4,128)S(1)} %get-tuple-element.27.own_ref), channel_id=1, source_target_pairs={{0,8},{8,0},{16,24},{24,16},{1,9},{9,1},{17,25},{25,17},{2,10},{10... | collective-permute-start | bytes 67592 | tf_op jit(solution)/shard_map/ppermute | solution.py:83
  89.7 4.0 %collective-permute-start.6 = (bf16[16,48,128]{2,1,0:T(8,128)(2,1)S(1)}, bf16[16,48,128]{2,1,0:T(8,128)(2,1)S(1)}, u32[]{:S(2)}, u32[]{:S(2)}) collective-permute-start(bf16[16,48,128]{2,1,0:T(8,128)(2,1)S(1)} %all_to_all.10.states_ref), channel_id=1, source_target_pairs={{0,1},{1,0},{2,3},{3,2},{4,5},{5,4},{6,7},{7,6},{8,9},{9,8},{10,11... | collective-permute-start | bytes 589832 | tf_op jit(solution)/shard_map/ppermute | solution.py:83
  94.3 4.6 %collective-permute-start.8 = (bf16[32,512]{1,0:T(8,128)(2,1)S(1)}, bf16[32,512]{1,0:T(8,128)(2,1)S(1)}, u32[]{:S(2)}, u32[]{:S(2)}) collective-permute-start(bf16[32,512]{1,0:T(8,128)(2,1)S(1)} %project.3), channel_id=1, source_target_pairs={{0,2},{1,7},{2,0},{3,5},{4,6},{5,3},{6,4},{7,1},{8,10},{9,15},{10,... | collective-permute-start | bytes 98312 | tf_op jit(solution)/shard_map/ppermute | solution.py:432
  97.6 4.3 %collective-permute-start.10 = (bf16[32,512]{1,0:T(8,128)(2,1)S(1)}, bf16[32,512]{1,0:T(8,128)(2,1)S(1)}, u32[]{:S(2)}, u32[]{:S(2)}) collective-permute-start(bf16[32,512]{1,0:T(8,128)(2,1)S(1)} %project.3), channel_id=1, source_target_pairs={{0,4},{2,6},{4,0},{6,2},{1,5},{3,7},{5,1},{7,3},{8,12},{10,14},{12... | collective-permute-start | bytes 98312 | tf_op jit(solution)/shard_map/ppermute | solution.py:83
  98.9 3.0 %collective-permute-start.9 = (bf16[32,512]{1,0:T(8,128)(2,1)S(1)}, bf16[32,512]{1,0:T(8,128)(2,1)S(1)}, u32[]{:S(2)}, u32[]{:S(2)}) collective-permute-start(bf16[32,512]{1,0:T(8,128)(2,1)S(1)} %collective-permute-done.8), channel_id=1, source_target_pairs={{0,1},{1,0},{2,3},{3,2},{4,5},{5,4},{6,7},{7,6},{8,9},{9,8},{10,11... | collective-permute-start | bytes 98312 | tf_op jit(solution)/shard_map/ppermute | solution.py:83

commit v7 on v5

--- a/solution.py
+++ b/solution.py
@@ -60,14 +60,19 @@
     scaled = (values * gain).astype(jnp.bfloat16)
     proj = jnp.dot(scaled, w_ref[...], preferred_element_type=jnp.float32)
     square = jnp.broadcast_to(square, (rows, HD))
+    first = square.astype(jnp.bfloat16).astype(jnp.float32)
+    second = (square - first).astype(jnp.bfloat16).astype(jnp.float32)
+    terms = (first, second, square - first - second)
     for index, out_ref in enumerate(out_refs):
-        out_ref[:, pl.ds(0, COLUMNS)] = proj[index * share:(index + 1) * share]
-        out_ref[:, pl.ds(COLUMNS, HD)] = square[index * share:(index + 1) * share]
+        span = slice(index * share, (index + 1) * share)
+        out_ref[:, pl.ds(0, COLUMNS)] = proj[span].astype(jnp.bfloat16)
+        for spot, term in enumerate(terms):
+            out_ref[:, pl.ds(COLUMNS + spot * HD, HD)] = term[span].astype(jnp.bfloat16)
 
 
 def partial_projection(x, hidden_states, norm_gain, w_qkv):
     vmem = pl.BlockSpec(memory_space=pltpu.VMEM)
-    shape = jax.ShapeDtypeStruct((STEPS * REQUESTS // SIDE, COLUMNS + HD), jnp.float32)
+    shape = jax.ShapeDtypeStruct((STEPS * REQUESTS // SIDE, COLUMNS + 3 * HD), jnp.bfloat16)
     return pl.pallas_call(
         partial_kernel,
         in_specs=[pl.BlockSpec(memory_space=pltpu.SMEM), vmem, vmem, vmem],
@@ -364,7 +369,12 @@
     _, hidden_states = lax.optimization_barrier((ready, hidden_states))
     packed = partial_projection(x, hidden_states, norm_gain, w_qkv)
     packed, w_out = lax.optimization_barrier((packed, w_out))
-    along_x = packed[0] + sum(swap(packed[k], "x", k) for k in range(1, SIDE))
+    along_x = sum(
+        term.astype(jnp.float32)
+        for term in [packed[0]] + [swap(packed[k], "x", k) for k in range(1, SIDE)]
+    )
+    squares = [along_x[:, COLUMNS + k * HD:COLUMNS + (k + 1) * HD] for k in range(3)]
+    along_x = jnp.concatenate([along_x[:, :COLUMNS], sum(squares)], axis=1)
     w_mate = swap(w_out, "core", 1)
     along_x = along_x.reshape(2, STEPS, COLUMNS + HD)
     own = lax.dynamic_index_in_dim(along_x, y // 2, 0, keepdims=False)

time: 102 us -> 102 us (level)
  transfers between devices with their start and end apart: 12 -> 12, of which waited for: 6 -> 7; matrix products, arithmetic and copies ran while one was open for 2% -> 2% of each run, Pallas kernels for 5% -> 5%
where the time goes in v7:
time: 102 us; the launch traced here: 101 us
  waiting for transfers between devices  46.8 us (46%)
  starting transfers between devices  29.5 us (29%)
  Pallas kernels  11 us (11%)
  blocking collectives  10.3 us (10%)
  other arithmetic  2.35 us (2%)
    ppermute x10, waiting for transfers between devices, swap(): return lax.ppermute(value, axis, pairs)  45.6 us
    ppermute x10, starting transfers between devices, swap(): return lax.ppermute(value, axis, pairs)  14.3 us
    all_to_all x1, starting transfers between devices, per_device(): lax.all_to_all(ready, everyone, split_axis=0, concat_axis=0, tiled=True)  12 us
    all_to_all x1, blocking collectives, per_device(): lax.all_to_all(states, ('x', 'y'), split_axis=0, concat_axis=0, tiled=True)  10.3 us
    pallas_call x1, Pallas kernels, prep(): pl.pallas_call(prep_kernel, out_shape=jax.ShapeDtypeStruct((CTX, TP, PIEC...  4.86 us
    pallas_call x1, Pallas kernels, attend(): pl.pallas_call(attend_kernel, in_specs=[pl.BlockSpec(memory_space=pltpu.S...  4.51 us
    ppermute x1, starting transfers between devices, per_device(): near = lax.ppermute(out, ('z', 'core'), pairs)  3.27 us
  transfers between devices with their start and end apart: 12, of which 7 were waited for; matrix products, arithmetic and copies ran while one was open for 2% of the time, Pallas kernels for 5%

profile of v7, /device:TPU:1, one launch (start us, length us, event | category | flops | bytes accessed | tf_op | source)
XLA Modules:
  0.0 101.5 jit_solution(12553358478888745444)
XLA Ops:
  0.6 4.9 %cache_by_receiver.1 = bf16[16,8,64,2,128]{4,3,2,1,0:T(2,128)(2,1)} custom-call(bf16[16,64,2,1024]{3,2,1,0:T(2,128)(2,1)} %bitcast.12), custom_call_target="tpu_custom_call" | custom-call | bytes 8388608 | tf_op jit(solution)/shard_map/cache_by_receiver/pallas_call | solution.py:117
  5.5 0.0 copy-start
  5.5 0.0 copy-start.2
  5.5 0.0 copy-start.3
  5.5 0.0 copy-start.1
  5.5 0.0 copy-start.4
  5.6 12.0 %all-to-all-start = ((bf16[128,128,128]{2,1,0:T(8,128)(2,1)}), bf16[128,128,128]{2,1,0:T(8,128)(2,1)}, u32[]{:S(2)}, u32[]{:S(2)}) async-start(bf16[128,128,128]{2,1,0:T(8,128)(2,1)} %bitcast.11), calls=%async_computation | async-start | bytes 8388608 | tf_op jit(solution)/shard_map/all_to_all | solution.py:366
  17.5 0.0 copy-done
  17.5 0.0 copy-done.2
  17.6 0.0 copy-done.3
  17.6 0.4 partial_projection.1
  18.0 1.4 %collective-permute-start = (bf16[8,1664]{1,0:T(8,128)(2,1)S(1)}, bf16[8,1664]{1,0:T(8,128)(2,1)S(1)}, u32[]{:S(2)}, u32[]{:S(2)}) collective-permute-start(bf16[8,1664]{1,0:T(8,128)(2,1)S(1)} %get-tuple-element.20), channel_id=1, source_target_pairs={{0,32},{32,0},{64,96},{96,64},{1,33},{33,1},{65,97},{97,65},{2,34}... | collective-permute-start | bytes 79880 | tf_op jit(solution)/shard_map/ppermute | solution.py:88
  19.4 2.4 %collective-permute-start.1 = (bf16[8,1664]{1,0:T(8,128)(2,1)S(1)}, bf16[8,1664]{1,0:T(8,128)(2,1)S(1)}, u32[]{:S(2)}, u32[]{:S(2)}) collective-permute-start(bf16[8,1664]{1,0:T(8,128)(2,1)S(1)} %get-tuple-element.21), channel_id=1, source_target_pairs={{0,64},{32,96},{64,0},{96,32},{1,65},{33,97},{65,1},{97,33},{2,66}... | collective-permute-start | bytes 79880 | tf_op jit(solution)/shard_map/ppermute | solution.py:88
  21.8 0.1 collective-permute-start.2
  21.9 0.0 copy-done.1
  21.9 2.0 %collective-permute-start.7 = (bf16[1024,512]{1,0:T(8,128)(2,1)S(1)}, bf16[1024,512]{1,0:T(8,128)(2,1)S(1)}, u32[]{:S(2)}, u32[]{:S(2)}) collective-permute-start(bf16[1024,512]{1,0:T(8,128)(2,1)S(1)} %copy-done.1), channel_id=1, source_target_pairs={{0,1},{1,0},{2,3},{3,2},{4,5},{5,4},{6,7},{7,6},{8,9},{9,8},{10,11... | collective-permute-start | bytes 3145736 | tf_op jit(solution)/shard_map/ppermute | solution.py:88
  23.9 0.0 copy-done.4
  23.9 0.7 dynamic_slice.11
  24.6 0.7 add_convert_fusion.1
  25.3 0.1 fusion
  25.4 0.1 pad_maximum_fusion.1
  25.5 38.7 %collective-permute-done = bf16[8,1664]{1,0:T(8,128)(2,1)S(1)} collective-permute-done((bf16[8,1664]{1,0:T(8,128)(2,1)S(1)}, bf16[8,1664]{1,0:T(8,128)(2,1)S(1)}, u32[]{:S(2)}, u32[]{:S(2)}) %collective-permute-start) | collective-permute-done | bytes 26656 | tf_op jit(solution)/shard_map/ppermute | solution.py:88
  64.2 2.1 %collective-permute-done.1 = bf16[8,1664]{1,0:T(8,128)(2,1)S(1)} collective-permute-done((bf16[8,1664]{1,0:T(8,128)(2,1)S(1)}, bf16[8,1664]{1,0:T(8,128)(2,1)S(1)}, u32[]{:S(2)}, u32[]{:S(2)}) %collective-permute-start.1) | collective-permute-done | bytes 26656 | tf_op jit(solution)/shard_map/ppermute | solution.py:88
  66.3 0.0 collective-permute-done.2
  66.4 2.8 %collective-permute-start.5 = (f32[4,1408]{1,0:T(4,128)S(1)}, f32[4,1408]{1,0:T(4,128)S(1)}, u32[]{:S(2)}, u32[]{:S(2)}) collective-permute-start(f32[4,1408]{1,0:T(4,128)S(1)} %get-tuple-element.26), channel_id=1, source_target_pairs={{0,16},{8,24},{16,0},{24,8},{1,17},{9,25},{17,1},{25,9},{2,18},{10... | collective-permute-start | bytes 67592 | tf_op jit(solution)/shard_map/ppermute | solution.py:88
  69.1 0.9 collective-permute-start.4
  70.0 0.0 collective-permute-start.3
  70.0 0.8 pad_add_fusion.info_ref
  70.8 0.2 collective-permute-done.5.third_ref
  71.0 2.0 %collective-permute-done.4.second_ref = f32[4,1408]{1,0:T(4,128)S(1)} collective-permute-done((f32[4,1408]{1,0:T(4,128)S(1)}, f32[4,1408]{1,0:T(4,128)S(1)}, u32[]{:S(2)}, u32[]{:S(2)}) %collective-permute-start.4) | collective-permute-done | bytes 22560 | tf_op jit(solution)/shard_map/ppermute | solution.py:88
  73.0 0.0 collective-permute-done.3.first_ref
  73.0 0.0 all-to-all-done
  73.0 4.5 %attend.1 = (bf16[16,8,128,128]{3,2,1,0:T(8,128)(2,1)}, bf16[48,128]{1,0:T(8,128)(2,1)S(1)}) custom-call(s32[2]{0:T(128)S(1)} %pad_add_fusion.info_ref, bf16[16,8,128,128]{3,2,1,0:T(8,128)(2,1)} %bitcast.3.kv_ref, f32[4,1408]{1,0:T(4,128)S(1)} %get-tuple-element.27.own_ref, f32[4,1408]{1,0:T(4,128)S(1)} %collective-permute-done.3.first_ref, ...), custom_call_target="tpu_custom_call" | custom-call | tf_op jit(solution)/shard_map/attend/pallas_call | solution.py:273
  77.6 10.3 %all_to_all.10.states_ref = bf16[16,48,128]{2,1,0:T(8,128)(2,1)S(1)} all-to-all(bf16[16,48,128]{2,1,0:T(8,128)(2,1)S(1)} %broadcast_in_dim.2), channel_id=1, replica_groups=mesh['x'=4,'y'=4,'z'=4,'core'=2] {'x','y'}, dimensions={0} | all-to-all | bytes 393216 | tf_op jit(solution)/shard_map/all_to_all | solution.py:394
  87.9 3.8 %collective-permute-start.6 = (bf16[16,48,128]{2,1,0:T(8,128)(2,1)S(1)}, bf16[16,48,128]{2,1,0:T(8,128)(2,1)S(1)}, u32[]{:S(2)}, u32[]{:S(2)}) collective-permute-start(bf16[16,48,128]{2,1,0:T(8,128)(2,1)S(1)} %all_to_all.10.states_ref), channel_id=1, source_target_pairs={{0,1},{1,0},{2,3},{3,2},{4,5},{5,4},{6,7},{7,6},{8,9},{9,8},{10,11... | collective-permute-start | bytes 589832 | tf_op jit(solution)/shard_map/ppermute | solution.py:88
  91.6 0.6 project.2.refs_0_
  92.2 0.0 collective-permute-done.7.w_ref
  92.2 0.5 collective-permute-done.6.states_ref
  92.7 0.6 project.3
  93.3 3.3 %collective-permute-start.8 = (bf16[32,512]{1,0:T(8,128)(2,1)S(1)}, bf16[32,512]{1,0:T(8,128)(2,1)S(1)}, u32[]{:S(2)}, u32[]{:S(2)}) collective-permute-start(bf16[32,512]{1,0:T(8,128)(2,1)S(1)} %project.3), channel_id=1, source_target_pairs={{0,2},{1,7},{2,0},{3,5},{4,6},{5,3},{6,4},{7,1},{8,10},{9,15},{10,... | collective-permute-start | bytes 98312 | tf_op jit(solution)/shard_map/ppermute | solution.py:398
  96.6 0.1 collective-permute-start.10
  96.7 1.2 %collective-permute-done.8 = bf16[32,512]{1,0:T(8,128)(2,1)S(1)} collective-permute-done((bf16[32,512]{1,0:T(8,128)(2,1)S(1)}, bf16[32,512]{1,0:T(8,128)(2,1)S(1)}, u32[]{:S(2)}, u32[]{:S(2)}) %collective-permute-start.8) | collective-permute-done | bytes 32800 | tf_op jit(solution)/shard_map/ppermute | solution.py:398
  97.9 0.8 collective-permute-start.9
  98.7 2.2 %collective-permute-done.10 = bf16[32,512]{1,0:T(8,128)(2,1)S(1)} collective-permute-done((bf16[32,512]{1,0:T(8,128)(2,1)S(1)}, bf16[32,512]{1,0:T(8,128)(2,1)S(1)}, u32[]{:S(2)}, u32[]{:S(2)}) %collective-permute-start.10) | collective-permute-done | bytes 32800 | tf_op jit(solution)/shard_map/ppermute | solution.py:88
  100.8 0.0 collective-permute-done.9
  100.9 0.6 add_convert_fusion
  (8 shorter events, 0.1 us)
Async XLA Ops:
  5.5 12.0 %copy-start = (bf16[512,1280]{1,0:T(8,128)(2,1)S(1)}, bf16[512,1280]{1,0:T(8,128)(2,1)}, u32[]{:S(2)}) copy-start(bf16[512,1280]{1,0:T(8,128)(2,1)} %w_ref.1) | copy-start | bytes 3932164
  5.5 12.0 %copy-start.2 = (bf16[32,512]{1,0:T(8,128)(2,1)S(1)}, bf16[32,512]{1,0:T(8,128)(2,1)}, u32[]{:S(2)}) copy-start(bf16[32,512]{1,0:T(8,128)(2,1)} %hidden_ref) | copy-start | bytes 98308
  5.5 12.0 %copy-start.3 = (bf16[512]{0:T(512)(128)(2,1)S(1)}, bf16[512]{0:T(512)(128)(2,1)}, u32[]{:S(2)}) copy-start(bf16[512]{0:T(512)(128)(2,1)} %gain_ref.1) | copy-start | bytes 3076
  5.5 16.4 %copy-start.1 = (bf16[1024,512]{1,0:T(8,128)(2,1)S(1)}, bf16[1024,512]{1,0:T(8,128)(2,1)}, u32[]{:S(2)}) copy-start(bf16[1024,512]{1,0:T(8,128)(2,1)} %w_ref.2) | copy-start | bytes 3145732
  5.5 18.3 %copy-start.4 = (s32[8]{0:T(128)S(1)}, s32[8]{0:T(128)}, u32[]{:S(2)}) copy-start(s32[8]{0:T(128)} %param.8) | copy-start | bytes 100
  5.6 67.5 %all-to-all-start = ((bf16[128,128,128]{2,1,0:T(8,128)(2,1)}), bf16[128,128,128]{2,1,0:T(8,128)(2,1)}, u32[]{:S(2)}, u32[]{:S(2)}) async-start(bf16[128,128,128]{2,1,0:T(8,128)(2,1)} %bitcast.11), calls=%async_computation | async-start | bytes 8388608 | tf_op jit(solution)/shard_map/all_to_all | solution.py:366
  18.0 46.2 %collective-permute-start = (bf16[8,1664]{1,0:T(8,128)(2,1)S(1)}, bf16[8,1664]{1,0:T(8,128)(2,1)S(1)}, u32[]{:S(2)}, u32[]{:S(2)}) collective-permute-start(bf16[8,1664]{1,0:T(8,128)(2,1)S(1)} %get-tuple-element.20), channel_id=1, source_target_pairs={{0,32},{32,0},{64,96},{96,64},{1,33},{33,1},{65,97},{97,65},{2,34}... | collective-permute-start | bytes 79880 | tf_op jit(solution)/shard_map/ppermute | solution.py:88
  19.4 46.8 %collective-permute-start.1 = (bf16[8,1664]{1,0:T(8,128)(2,1)S(1)}, bf16[8,1664]{1,0:T(8,128)(2,1)S(1)}, u32[]{:S(2)}, u32[]{:S(2)}) collective-permute-start(bf16[8,1664]{1,0:T(8,128)(2,1)S(1)} %get-tuple-element.21), channel_id=1, source_target_pairs={{0,64},{32,96},{64,0},{96,32},{1,65},{33,97},{65,1},{97,33},{2,66}... | collective-permute-start | bytes 79880 | tf_op jit(solution)/shard_map/ppermute | solution.py:88
  21.8 44.4 %collective-permute-start.2 = (bf16[8,1664]{1,0:T(8,128)(2,1)S(1)}, bf16[8,1664]{1,0:T(8,128)(2,1)S(1)}, u32[]{:S(2)}, u32[]{:S(2)}) collective-permute-start(bf16[8,1664]{1,0:T(8,128)(2,1)S(1)} %get-tuple-element.22), channel_id=1, source_target_pairs={{0,96},{32,64},{64,32},{96,0},{1,97},{33,65},{65,33},{97,1},{2,98}... | collective-permute-start | bytes 79880 | tf_op jit(solution)/shard_map/ppermute | solution.py:88
  21.9 70.3 %collective-permute-start.7 = (bf16[1024,512]{1,0:T(8,128)(2,1)S(1)}, bf16[1024,512]{1,0:T(8,128)(2,1)S(1)}, u32[]{:S(2)}, u32[]{:S(2)}) collective-permute-start(bf16[1024,512]{1,0:T(8,128)(2,1)S(1)} %copy-done.1), channel_id=1, source_target_pairs={{0,1},{1,0},{2,3},{3,2},{4,5},{5,4},{6,7},{7,6},{8,9},{9,8},{10,11... | collective-permute-start | bytes 3145736 | tf_op jit(solution)/shard_map/ppermute | solution.py:88
  66.4 4.6 %collective-permute-start.5 = (f32[4,1408]{1,0:T(4,128)S(1)}, f32[4,1408]{1,0:T(4,128)S(1)}, u32[]{:S(2)}, u32[]{:S(2)}) collective-permute-start(f32[4,1408]{1,0:T(4,128)S(1)} %get-tuple-element.26), channel_id=1, source_target_pairs={{0,16},{8,24},{16,0},{24,8},{1,17},{9,25},{17,1},{25,9},{2,18},{10... | collective-permute-start | bytes 67592 | tf_op jit(solution)/shard_map/ppermute | solution.py:88
  69.1 3.9 %collective-permute-start.4 = (f32[4,1408]{1,0:T(4,128)S(1)}, f32[4,1408]{1,0:T(4,128)S(1)}, u32[]{:S(2)}, u32[]{:S(2)}) collective-permute-start(f32[4,1408]{1,0:T(4,128)S(1)} %get-tuple-element.26), channel_id=1, source_target_pairs={{0,24},{8,16},{16,8},{24,0},{1,25},{9,17},{17,9},{25,1},{2,26},{10... | collective-permute-start | bytes 67592 | tf_op jit(solution)/shard_map/ppermute | solution.py:88
  70.0 3.0 %collective-permute-start.3 = (f32[4,1408]{1,0:T(4,128)S(1)}, f32[4,1408]{1,0:T(4,128)S(1)}, u32[]{:S(2)}, u32[]{:S(2)}) collective-permute-start(f32[4,1408]{1,0:T(4,128)S(1)} %get-tuple-element.27.own_ref), channel_id=1, source_target_pairs={{0,8},{8,0},{16,24},{24,16},{1,9},{9,1},{17,25},{25,17},{2,10},{10... | collective-permute-start | bytes 67592 | tf_op jit(solution)/shard_map/ppermute | solution.py:88
  87.9 4.9 %collective-permute-start.6 = (bf16[16,48,128]{2,1,0:T(8,128)(2,1)S(1)}, bf16[16,48,128]{2,1,0:T(8,128)(2,1)S(1)}, u32[]{:S(2)}, u32[]{:S(2)}) collective-permute-start(bf16[16,48,128]{2,1,0:T(8,128)(2,1)S(1)} %all_to_all.10.states_ref), channel_id=1, source_target_pairs={{0,1},{1,0},{2,3},{3,2},{4,5},{5,4},{6,7},{7,6},{8,9},{9,8},{10,11... | collective-permute-start | bytes 589832 | tf_op jit(solution)/shard_map/ppermute | solution.py:88
  93.3 4.6 %collective-permute-start.8 = (bf16[32,512]{1,0:T(8,128)(2,1)S(1)}, bf16[32,512]{1,0:T(8,128)(2,1)S(1)}, u32[]{:S(2)}, u32[]{:S(2)}) collective-permute-start(bf16[32,512]{1,0:T(8,128)(2,1)S(1)} %project.3), channel_id=1, source_target_pairs={{0,2},{1,7},{2,0},{3,5},{4,6},{5,3},{6,4},{7,1},{8,10},{9,15},{10,... | collective-permute-start | bytes 98312 | tf_op jit(solution)/shard_map/ppermute | solution.py:398
  96.6 4.3 %collective-permute-start.10 = (bf16[32,512]{1,0:T(8,128)(2,1)S(1)}, bf16[32,512]{1,0:T(8,128)(2,1)S(1)}, u32[]{:S(2)}, u32[]{:S(2)}) collective-permute-start(bf16[32,512]{1,0:T(8,128)(2,1)S(1)} %project.3), channel_id=1, source_target_pairs={{0,4},{2,6},{4,0},{6,2},{1,5},{3,7},{5,1},{7,3},{8,12},{10,14},{12... | collective-permute-start | bytes 98312 | tf_op jit(solution)/shard_map/ppermute | solution.py:88
  97.9 3.0 %collective-permute-start.9 = (bf16[32,512]{1,0:T(8,128)(2,1)S(1)}, bf16[32,512]{1,0:T(8,128)(2,1)S(1)}, u32[]{:S(2)}, u32[]{:S(2)}) collective-permute-start(bf16[32,512]{1,0:T(8,128)(2,1)S(1)} %collective-permute-done.8), channel_id=1, source_target_pairs={{0,1},{1,0},{2,3},{3,2},{4,5},{5,4},{6,7},{7,6},{8,9},{9,8},{10,11... | collective-permute-start | bytes 98312 | tf_op jit(solution)/shard_map/ppermute | solution.py:88

commit v8 on v5

--- a/solution.py
+++ b/solution.py
@@ -128,7 +128,7 @@
     )(split)
 
 
-CHUNKS = 4
+CHUNKS = 2
 CHUNK_CTX = CTX // CHUNKS
 CHUNK_SOURCES = SOURCES // CHUNKS
 CHUNK_KEYS = CHUNK_SOURCES * PIECE
@@ -286,7 +286,7 @@
             jax.ShapeDtypeStruct((CTX, TP, 2 * PIECE, HD), jnp.bfloat16),
             jax.ShapeDtypeStruct((STATE_ROWS, HD), jnp.bfloat16),
         ],
-        compiler_params=pltpu.CompilerParams(vmem_limit_bytes=24 * 1024 * 1024),
+        compiler_params=pltpu.CompilerParams(vmem_limit_bytes=32 * 1024 * 1024),
         name="attend",
     )(info, moved, *sums, cosine, sine)
 

time: 102 us -> 103 us (level)
  transfers between devices with their start and end apart: 12 -> 12, of which waited for: 6 -> 6; matrix products, arithmetic and copies ran while one was open for 2% -> 2% of each run, Pallas kernels for 5% -> 6%
where the time goes in v8:
time: 103 us
  waiting for transfers between devices  47.8 us (46%)
  starting transfers between devices  29.4 us (29%)
  Pallas kernels  11.3 us (11%)
  blocking collectives  10.3 us (10%)
  other arithmetic  2.33 us (2%)
    ppermute x10, waiting for transfers between devices, swap(): return lax.ppermute(value, axis, pairs)  46.6 us
    ppermute x10, starting transfers between devices, swap(): return lax.ppermute(value, axis, pairs)  14.1 us
    all_to_all x1, starting transfers between devices, per_device(): lax.all_to_all(ready, everyone, split_axis=0, concat_axis=0, tiled=True)  12 us
    all_to_all x1, blocking collectives, per_device(): lax.all_to_all(states, ('x', 'y'), split_axis=0, concat_axis=0, tiled=True)  10.3 us
    pallas_call x1, Pallas kernels, attend(): pl.pallas_call(attend_kernel, in_specs=[pl.BlockSpec(memory_space=pltpu.S...  4.89 us
    pallas_call x1, Pallas kernels, prep(): pl.pallas_call(prep_kernel, out_shape=jax.ShapeDtypeStruct((CTX, TP, PIEC...  4.86 us
    ppermute x1, starting transfers between devices, per_device(): near = lax.ppermute(out, ('z', 'core'), pairs)  3.27 us
  transfers between devices with their start and end apart: 12, of which 6 were waited for; matrix products, arithmetic and copies ran while one was open for 2% of the time, Pallas kernels for 6%

profile of v8, /device:TPU:1, one launch (start us, length us, event | category | flops | bytes accessed | tf_op | source)
XLA Modules:
  0.0 102.6 jit_solution(18225458184470116181)
XLA Ops:
  0.6 4.9 %cache_by_receiver.1 = bf16[16,8,64,2,128]{4,3,2,1,0:T(2,128)(2,1)} custom-call(bf16[16,64,2,1024]{3,2,1,0:T(2,128)(2,1)} %bitcast.12), custom_call_target="tpu_custom_call" | custom-call | bytes 8388608 | tf_op jit(solution)/shard_map/cache_by_receiver/pallas_call | solution.py:112
  5.5 0.0 copy-start
  5.5 0.0 copy-start.2
  5.5 0.0 copy-start.3
  5.5 0.0 copy-start.1
  5.5 0.0 copy-start.4
  5.6 12.0 %all-to-all-start = ((bf16[128,128,128]{2,1,0:T(8,128)(2,1)}), bf16[128,128,128]{2,1,0:T(8,128)(2,1)}, u32[]{:S(2)}, u32[]{:S(2)}) async-start(bf16[128,128,128]{2,1,0:T(8,128)(2,1)} %bitcast.11), calls=%async_computation | async-start | bytes 8388608 | tf_op jit(solution)/shard_map/all_to_all | solution.py:361
  17.5 0.0 copy-done
  17.5 0.0 copy-done.2
  17.6 0.0 copy-done.3
  17.6 0.4 partial_projection.1
  18.0 1.4 %collective-permute-start = (f32[8,1408]{1,0:T(8,128)S(1)}, f32[8,1408]{1,0:T(8,128)S(1)}, u32[]{:S(2)}, u32[]{:S(2)}) collective-permute-start(f32[8,1408]{1,0:T(8,128)S(1)} %get-tuple-element.20), channel_id=1, source_target_pairs={{0,32},{32,0},{64,96},{96,64},{1,33},{33,1},{65,97},{97,65},{2,34}... | collective-permute-start | bytes 135176 | tf_op jit(solution)/shard_map/ppermute | solution.py:83
  19.4 2.4 %collective-permute-start.1 = (f32[8,1408]{1,0:T(8,128)S(1)}, f32[8,1408]{1,0:T(8,128)S(1)}, u32[]{:S(2)}, u32[]{:S(2)}) collective-permute-start(f32[8,1408]{1,0:T(8,128)S(1)} %get-tuple-element.21), channel_id=1, source_target_pairs={{0,64},{32,96},{64,0},{96,32},{1,65},{33,97},{65,1},{97,33},{2,66}... | collective-permute-start | bytes 135176 | tf_op jit(solution)/shard_map/ppermute | solution.py:83
  21.8 0.1 collective-permute-start.2
  21.9 0.0 copy-done.1
  21.9 2.0 %collective-permute-start.7 = (bf16[1024,512]{1,0:T(8,128)(2,1)S(1)}, bf16[1024,512]{1,0:T(8,128)(2,1)S(1)}, u32[]{:S(2)}, u32[]{:S(2)}) collective-permute-start(bf16[1024,512]{1,0:T(8,128)(2,1)S(1)} %copy-done.1), channel_id=1, source_target_pairs={{0,1},{1,0},{2,3},{3,2},{4,5},{5,4},{6,7},{7,6},{8,9},{9,8},{10,11... | collective-permute-start | bytes 3145736 | tf_op jit(solution)/shard_map/ppermute | solution.py:83
  23.8 0.0 copy-done.4
  23.8 0.7 dynamic_slice.11
  24.5 0.7 add_convert_fusion.1
  25.2 0.1 fusion
  25.4 0.1 pad_maximum_fusion
  25.4 39.1 %collective-permute-done = f32[8,1408]{1,0:T(8,128)S(1)} collective-permute-done((f32[8,1408]{1,0:T(8,128)S(1)}, f32[8,1408]{1,0:T(8,128)S(1)}, u32[]{:S(2)}, u32[]{:S(2)}) %collective-permute-start) | collective-permute-done | bytes 45088 | tf_op jit(solution)/shard_map/ppermute | solution.py:83
  64.6 2.5 %collective-permute-done.1 = f32[8,1408]{1,0:T(8,128)S(1)} collective-permute-done((f32[8,1408]{1,0:T(8,128)S(1)}, f32[8,1408]{1,0:T(8,128)S(1)}, u32[]{:S(2)}, u32[]{:S(2)}) %collective-permute-start.1) | collective-permute-done | bytes 45088 | tf_op jit(solution)/shard_map/ppermute | solution.py:83
  67.0 0.0 collective-permute-done.2
  67.1 2.8 %collective-permute-start.5 = (f32[4,1408]{1,0:T(4,128)S(1)}, f32[4,1408]{1,0:T(4,128)S(1)}, u32[]{:S(2)}, u32[]{:S(2)}) collective-permute-start(f32[4,1408]{1,0:T(4,128)S(1)} %get-tuple-element.26), channel_id=1, source_target_pairs={{0,16},{8,24},{16,0},{24,8},{1,17},{9,25},{17,1},{25,9},{2,18},{10... | collective-permute-start | bytes 67592 | tf_op jit(solution)/shard_map/ppermute | solution.py:83
  69.9 0.8 collective-permute-start.4
  70.7 0.0 collective-permute-start.3
  70.7 0.8 pad_add_fusion.info_ref
  71.4 0.0 collective-permute-done.5.third_ref
  71.4 2.3 %collective-permute-done.4.second_ref = f32[4,1408]{1,0:T(4,128)S(1)} collective-permute-done((f32[4,1408]{1,0:T(4,128)S(1)}, f32[4,1408]{1,0:T(4,128)S(1)}, u32[]{:S(2)}, u32[]{:S(2)}) %collective-permute-start.4) | collective-permute-done | bytes 22560 | tf_op jit(solution)/shard_map/ppermute | solution.py:83
  73.8 0.0 collective-permute-done.3.first_ref
  73.8 0.0 all-to-all-done
  73.8 4.9 %attend.1 = (bf16[16,8,128,128]{3,2,1,0:T(8,128)(2,1)}, bf16[48,128]{1,0:T(8,128)(2,1)S(1)}) custom-call(s32[2]{0:T(128)S(1)} %pad_add_fusion.info_ref, bf16[16,8,128,128]{3,2,1,0:T(8,128)(2,1)} %bitcast.3.kv_ref, f32[4,1408]{1,0:T(4,128)S(1)} %get-tuple-element.27.own_ref, f32[4,1408]{1,0:T(4,128)S(1)} %collective-permute-done.3.first_ref, ...), custom_call_target="tpu_custom_call" | custom-call | tf_op jit(solution)/shard_map/attend/pallas_call | solution.py:268
  78.7 10.3 %all_to_all.10.states_ref = bf16[16,48,128]{2,1,0:T(8,128)(2,1)S(1)} all-to-all(bf16[16,48,128]{2,1,0:T(8,128)(2,1)S(1)} %broadcast_in_dim.2), channel_id=1, replica_groups=mesh['x'=4,'y'=4,'z'=4,'core'=2] {'x','y'}, dimensions={0} | all-to-all | bytes 393216 | tf_op jit(solution)/shard_map/all_to_all | solution.py:384
  89.0 3.8 %collective-permute-start.6 = (bf16[16,48,128]{2,1,0:T(8,128)(2,1)S(1)}, bf16[16,48,128]{2,1,0:T(8,128)(2,1)S(1)}, u32[]{:S(2)}, u32[]{:S(2)}) collective-permute-start(bf16[16,48,128]{2,1,0:T(8,128)(2,1)S(1)} %all_to_all.10.states_ref), channel_id=1, source_target_pairs={{0,1},{1,0},{2,3},{3,2},{4,5},{5,4},{6,7},{7,6},{8,9},{9,8},{10,11... | collective-permute-start | bytes 589832 | tf_op jit(solution)/shard_map/ppermute | solution.py:83
  92.8 0.6 project.2.refs_0_
  93.4 0.0 collective-permute-done.7.w_ref
  93.4 0.5 collective-permute-done.6.states_ref
  93.8 0.6 project.3
  94.4 3.3 %collective-permute-start.8 = (bf16[32,512]{1,0:T(8,128)(2,1)S(1)}, bf16[32,512]{1,0:T(8,128)(2,1)S(1)}, u32[]{:S(2)}, u32[]{:S(2)}) collective-permute-start(bf16[32,512]{1,0:T(8,128)(2,1)S(1)} %project.3), channel_id=1, source_target_pairs={{0,2},{1,7},{2,0},{3,5},{4,6},{5,3},{6,4},{7,1},{8,10},{9,15},{10,... | collective-permute-start | bytes 98312 | tf_op jit(solution)/shard_map/ppermute | solution.py:388
  97.7 0.1 collective-permute-start.10
  97.8 1.2 %collective-permute-done.8 = bf16[32,512]{1,0:T(8,128)(2,1)S(1)} collective-permute-done((bf16[32,512]{1,0:T(8,128)(2,1)S(1)}, bf16[32,512]{1,0:T(8,128)(2,1)S(1)}, u32[]{:S(2)}, u32[]{:S(2)}) %collective-permute-start.8) | collective-permute-done | bytes 32800 | tf_op jit(solution)/shard_map/ppermute | solution.py:388
  99.0 0.8 collective-permute-start.9
  99.8 2.2 %collective-permute-done.10 = bf16[32,512]{1,0:T(8,128)(2,1)S(1)} collective-permute-done((bf16[32,512]{1,0:T(8,128)(2,1)S(1)}, bf16[32,512]{1,0:T(8,128)(2,1)S(1)}, u32[]{:S(2)}, u32[]{:S(2)}) %collective-permute-start.10) | collective-permute-done | bytes 32800 | tf_op jit(solution)/shard_map/ppermute | solution.py:83
  102.0 0.0 collective-permute-done.9
  102.0 0.6 add_convert_fusion
  (5 shorter events, 0.1 us)
Async XLA Ops:
  5.5 12.0 %copy-start = (bf16[512,1280]{1,0:T(8,128)(2,1)S(1)}, bf16[512,1280]{1,0:T(8,128)(2,1)}, u32[]{:S(2)}) copy-start(bf16[512,1280]{1,0:T(8,128)(2,1)} %w_ref.1) | copy-start | bytes 3932164
  5.5 12.0 %copy-start.2 = (bf16[32,512]{1,0:T(8,128)(2,1)S(1)}, bf16[32,512]{1,0:T(8,128)(2,1)}, u32[]{:S(2)}) copy-start(bf16[32,512]{1,0:T(8,128)(2,1)} %hidden_ref) | copy-start | bytes 98308
  5.5 12.0 %copy-start.3 = (bf16[512]{0:T(512)(128)(2,1)S(1)}, bf16[512]{0:T(512)(128)(2,1)}, u32[]{:S(2)}) copy-start(bf16[512]{0:T(512)(128)(2,1)} %gain_ref.1) | copy-start | bytes 3076
  5.5 16.3 %copy-start.1 = (bf16[1024,512]{1,0:T(8,128)(2,1)S(1)}, bf16[1024,512]{1,0:T(8,128)(2,1)}, u32[]{:S(2)}) copy-start(bf16[1024,512]{1,0:T(8,128)(2,1)} %w_ref.2) | copy-start | bytes 3145732
  5.5 18.3 %copy-start.4 = (s32[8]{0:T(128)S(1)}, s32[8]{0:T(128)}, u32[]{:S(2)}) copy-start(s32[8]{0:T(128)} %param.8) | copy-start | bytes 100
  5.6 68.2 %all-to-all-start = ((bf16[128,128,128]{2,1,0:T(8,128)(2,1)}), bf16[128,128,128]{2,1,0:T(8,128)(2,1)}, u32[]{:S(2)}, u32[]{:S(2)}) async-start(bf16[128,128,128]{2,1,0:T(8,128)(2,1)} %bitcast.11), calls=%async_computation | async-start | bytes 8388608 | tf_op jit(solution)/shard_map/all_to_all | solution.py:361
  18.0 46.6 %collective-permute-start = (f32[8,1408]{1,0:T(8,128)S(1)}, f32[8,1408]{1,0:T(8,128)S(1)}, u32[]{:S(2)}, u32[]{:S(2)}) collective-permute-start(f32[8,1408]{1,0:T(8,128)S(1)} %get-tuple-element.20), channel_id=1, source_target_pairs={{0,32},{32,0},{64,96},{96,64},{1,33},{33,1},{65,97},{97,65},{2,34}... | collective-permute-start | bytes 135176 | tf_op jit(solution)/shard_map/ppermute | solution.py:83
  19.4 47.7 %collective-permute-start.1 = (f32[8,1408]{1,0:T(8,128)S(1)}, f32[8,1408]{1,0:T(8,128)S(1)}, u32[]{:S(2)}, u32[]{:S(2)}) collective-permute-start(f32[8,1408]{1,0:T(8,128)S(1)} %get-tuple-element.21), channel_id=1, source_target_pairs={{0,64},{32,96},{64,0},{96,32},{1,65},{33,97},{65,1},{97,33},{2,66}... | collective-permute-start | bytes 135176 | tf_op jit(solution)/shard_map/ppermute | solution.py:83
  21.8 45.3 %collective-permute-start.2 = (f32[8,1408]{1,0:T(8,128)S(1)}, f32[8,1408]{1,0:T(8,128)S(1)}, u32[]{:S(2)}, u32[]{:S(2)}) collective-permute-start(f32[8,1408]{1,0:T(8,128)S(1)} %get-tuple-element.22), channel_id=1, source_target_pairs={{0,96},{32,64},{64,32},{96,0},{1,97},{33,65},{65,33},{97,1},{2,98}... | collective-permute-start | bytes 135176 | tf_op jit(solution)/shard_map/ppermute | solution.py:83
  21.9 71.5 %collective-permute-start.7 = (bf16[1024,512]{1,0:T(8,128)(2,1)S(1)}, bf16[1024,512]{1,0:T(8,128)(2,1)S(1)}, u32[]{:S(2)}, u32[]{:S(2)}) collective-permute-start(bf16[1024,512]{1,0:T(8,128)(2,1)S(1)} %copy-done.1), channel_id=1, source_target_pairs={{0,1},{1,0},{2,3},{3,2},{4,5},{5,4},{6,7},{7,6},{8,9},{9,8},{10,11... | collective-permute-start | bytes 3145736 | tf_op jit(solution)/shard_map/ppermute | solution.py:83
  67.1 4.3 %collective-permute-start.5 = (f32[4,1408]{1,0:T(4,128)S(1)}, f32[4,1408]{1,0:T(4,128)S(1)}, u32[]{:S(2)}, u32[]{:S(2)}) collective-permute-start(f32[4,1408]{1,0:T(4,128)S(1)} %get-tuple-element.26), channel_id=1, source_target_pairs={{0,16},{8,24},{16,0},{24,8},{1,17},{9,25},{17,1},{25,9},{2,18},{10... | collective-permute-start | bytes 67592 | tf_op jit(solution)/shard_map/ppermute | solution.py:83
  69.9 3.9 %collective-permute-start.4 = (f32[4,1408]{1,0:T(4,128)S(1)}, f32[4,1408]{1,0:T(4,128)S(1)}, u32[]{:S(2)}, u32[]{:S(2)}) collective-permute-start(f32[4,1408]{1,0:T(4,128)S(1)} %get-tuple-element.26), channel_id=1, source_target_pairs={{0,24},{8,16},{16,8},{24,0},{1,25},{9,17},{17,9},{25,1},{2,26},{10... | collective-permute-start | bytes 67592 | tf_op jit(solution)/shard_map/ppermute | solution.py:83
  70.7 3.1 %collective-permute-start.3 = (f32[4,1408]{1,0:T(4,128)S(1)}, f32[4,1408]{1,0:T(4,128)S(1)}, u32[]{:S(2)}, u32[]{:S(2)}) collective-permute-start(f32[4,1408]{1,0:T(4,128)S(1)} %get-tuple-element.27.own_ref), channel_id=1, source_target_pairs={{0,8},{8,0},{16,24},{24,16},{1,9},{9,1},{17,25},{25,17},{2,10},{10... | collective-permute-start | bytes 67592 | tf_op jit(solution)/shard_map/ppermute | solution.py:83
  89.0 4.9 %collective-permute-start.6 = (bf16[16,48,128]{2,1,0:T(8,128)(2,1)S(1)}, bf16[16,48,128]{2,1,0:T(8,128)(2,1)S(1)}, u32[]{:S(2)}, u32[]{:S(2)}) collective-permute-start(bf16[16,48,128]{2,1,0:T(8,128)(2,1)S(1)} %all_to_all.10.states_ref), channel_id=1, source_target_pairs={{0,1},{1,0},{2,3},{3,2},{4,5},{5,4},{6,7},{7,6},{8,9},{9,8},{10,11... | collective-permute-start | bytes 589832 | tf_op jit(solution)/shard_map/ppermute | solution.py:83
  94.4 4.6 %collective-permute-start.8 = (bf16[32,512]{1,0:T(8,128)(2,1)S(1)}, bf16[32,512]{1,0:T(8,128)(2,1)S(1)}, u32[]{:S(2)}, u32[]{:S(2)}) collective-permute-start(bf16[32,512]{1,0:T(8,128)(2,1)S(1)} %project.3), channel_id=1, source_target_pairs={{0,2},{1,7},{2,0},{3,5},{4,6},{5,3},{6,4},{7,1},{8,10},{9,15},{10,... | collective-permute-start | bytes 98312 | tf_op jit(solution)/shard_map/ppermute | solution.py:388
  97.7 4.3 %collective-permute-start.10 = (bf16[32,512]{1,0:T(8,128)(2,1)S(1)}, bf16[32,512]{1,0:T(8,128)(2,1)S(1)}, u32[]{:S(2)}, u32[]{:S(2)}) collective-permute-start(bf16[32,512]{1,0:T(8,128)(2,1)S(1)} %project.3), channel_id=1, source_target_pairs={{0,4},{2,6},{4,0},{6,2},{1,5},{3,7},{5,1},{7,3},{8,12},{10,14},{12... | collective-permute-start | bytes 98312 | tf_op jit(solution)/shard_map/ppermute | solution.py:83
  99.0 3.0 %collective-permute-start.9 = (bf16[32,512]{1,0:T(8,128)(2,1)S(1)}, bf16[32,512]{1,0:T(8,128)(2,1)S(1)}, u32[]{:S(2)}, u32[]{:S(2)}) collective-permute-start(bf16[32,512]{1,0:T(8,128)(2,1)S(1)} %collective-permute-done.8), channel_id=1, source_target_pairs={{0,1},{1,0},{2,3},{3,2},{4,5},{5,4},{6,7},{7,6},{8,9},{9,8},{10,11... | collective-permute-start | bytes 98312 | tf_op jit(solution)/shard_map/ppermute | solution.py:83

commit v9 on v5

--- a/solution.py
+++ b/solution.py
@@ -291,8 +291,7 @@
     )(info, moved, *sums, cosine, sine)
 
 
-def project_kernel(states_ref, w_ref, *refs):
-    base_ref, out_ref = refs if len(refs) == 2 else (None, refs[0])
+def combine_kernel(states_ref, out_ref):
     row = lax.broadcasted_iota(jnp.int32, (HEAD_ROWS, HD), 0)
     lane = lax.broadcasted_iota(jnp.int32, (HEAD_ROWS, HD), 1)
     many = REQUESTS * HEAD_ROWS
@@ -318,15 +317,31 @@
             for spot, share in zip(spots, shares)
         )
         rows.append(mixed.astype(jnp.bfloat16))
-    attn = jnp.dot(
+    out_ref[...] = jnp.dot(
         moves.astype(jnp.bfloat16),
         jnp.concatenate(rows, axis=0),
         preferred_element_type=jnp.float32,
     ).astype(jnp.bfloat16)
+
+
+def combine(states):
+    vmem = pl.BlockSpec(memory_space=pltpu.VMEM)
+    return pl.pallas_call(
+        combine_kernel,
+        in_specs=[vmem],
+        out_specs=vmem,
+        out_shape=jax.ShapeDtypeStruct((REQUESTS * HEAD_ROWS, HD), jnp.bfloat16),
+        compiler_params=pltpu.CompilerParams(vmem_limit_bytes=8 * 1024 * 1024),
+        name="combine",
+    )(states)
+
+
+def project_kernel(attn_ref, w_ref, *refs):
+    base_ref, out_ref = refs if len(refs) == 2 else (None, refs[0])
     total = jnp.zeros(out_ref.shape, jnp.float32)
     for index in range(GQA):
         total = total + jnp.dot(
-            attn[index * HEAD_ROWS:(index + 1) * HEAD_ROWS],
+            attn_ref[pl.ds(index * HEAD_ROWS, HEAD_ROWS), :],
             w_ref[pl.ds(index * HD, HD), :],
             preferred_element_type=jnp.float32,
         )
@@ -335,9 +350,9 @@
     out_ref[...] = total.astype(out_ref.dtype)
 
 
-def project(states, w, base=None):
+def project(attn, w, base=None):
     vmem = pl.BlockSpec(memory_space=pltpu.VMEM)
-    operands = (states, w) if base is None else (states, w, base)
+    operands = (attn, w) if base is None else (attn, w, base)
     kind = jnp.float32 if base is None else jnp.bfloat16
     return pl.pallas_call(
         project_kernel,
@@ -382,8 +397,9 @@
 
     states = jnp.broadcast_to(state[None], (CTX, STATE_ROWS, HD))
     states = lax.all_to_all(states, ("x", "y"), split_axis=0, concat_axis=0, tiled=True)
-    mate_states = swap(states, "core", 1)
-    out = project(mate_states, w_mate, project(states, w_out))
+    attn = combine(states)
+    mate_attn = swap(attn, "core", 1)
+    out = project(mate_attn, w_mate, project(attn, w_out))
     pairs = [(z * 2 + c, (z ^ (1 + 2 * c)) * 2 + c) for z in range(SIDE) for c in range(2)]
     near = lax.ppermute(out, ("z", "core"), pairs)
     across = swap(out, "z", 2)

time: 102 us -> 102 us (level)
  no operation moved by 1% of the time
where the time goes in v9:
time: 102 us
  waiting for transfers between devices  48 us (47%)
  starting transfers between devices  29.3 us (29%)
  Pallas kernels  10.7 us (10%)
  blocking collectives  10 us (10%)
  other arithmetic  2.33 us (2%)
    ppermute x10, waiting for transfers between devices, swap(): return lax.ppermute(value, axis, pairs)  46.8 us
    ppermute x10, starting transfers between devices, swap(): return lax.ppermute(value, axis, pairs)  14.2 us
    all_to_all x1, starting transfers between devices, per_device(): lax.all_to_all(ready, everyone, split_axis=0, concat_axis=0, tiled=True)  12 us
    all_to_all x1, blocking collectives, per_device(): lax.all_to_all(states, ('x', 'y'), split_axis=0, concat_axis=0, tiled=True)  10 us
    pallas_call x1, Pallas kernels, prep(): pl.pallas_call(prep_kernel, out_shape=jax.ShapeDtypeStruct((CTX, TP, PIEC...  4.86 us
    pallas_call x1, Pallas kernels, attend(): pl.pallas_call(attend_kernel, in_specs=[pl.BlockSpec(memory_space=pltpu.S...  4.51 us
    ppermute x1, starting transfers between devices, per_device(): near = lax.ppermute(out, ('z', 'core'), pairs)  3.21 us
  transfers between devices with their start and end apart: 12, of which 6 were waited for; matrix products, arithmetic and copies ran while one was open for 2% of the time, Pallas kernels for 5%

profile of v9, /device:TPU:1, one launch (start us, length us, event | category | flops | bytes accessed | tf_op | source)
XLA Modules:
  0.0 101.8 jit_solution(7347485298085832645)
XLA Ops:
  0.6 4.9 %cache_by_receiver.1 = bf16[16,8,64,2,128]{4,3,2,1,0:T(2,128)(2,1)} custom-call(bf16[16,64,2,1024]{3,2,1,0:T(2,128)(2,1)} %bitcast.12), custom_call_target="tpu_custom_call" | custom-call | bytes 8388608 | tf_op jit(solution)/shard_map/cache_by_receiver/pallas_call | solution.py:112
  5.5 0.0 copy-start
  5.5 0.0 copy-start.2
  5.5 0.0 copy-start.3
  5.5 0.0 copy-start.1
  5.5 0.0 copy-start.4
  5.6 12.0 %all-to-all-start = ((bf16[128,128,128]{2,1,0:T(8,128)(2,1)}), bf16[128,128,128]{2,1,0:T(8,128)(2,1)}, u32[]{:S(2)}, u32[]{:S(2)}) async-start(bf16[128,128,128]{2,1,0:T(8,128)(2,1)} %bitcast.11), calls=%async_computation | async-start | bytes 8388608 | tf_op jit(solution)/shard_map/all_to_all | solution.py:376
  17.5 0.0 copy-done
  17.5 0.0 copy-done.2
  17.6 0.0 copy-done.3
  17.6 0.4 partial_projection.1
  18.0 1.4 %collective-permute-start = (f32[8,1408]{1,0:T(8,128)S(1)}, f32[8,1408]{1,0:T(8,128)S(1)}, u32[]{:S(2)}, u32[]{:S(2)}) collective-permute-start(f32[8,1408]{1,0:T(8,128)S(1)} %get-tuple-element.20), channel_id=1, source_target_pairs={{0,32},{32,0},{64,96},{96,64},{1,33},{33,1},{65,97},{97,65},{2,34}... | collective-permute-start | bytes 135176 | tf_op jit(solution)/shard_map/ppermute | solution.py:83
  19.4 2.4 %collective-permute-start.1 = (f32[8,1408]{1,0:T(8,128)S(1)}, f32[8,1408]{1,0:T(8,128)S(1)}, u32[]{:S(2)}, u32[]{:S(2)}) collective-permute-start(f32[8,1408]{1,0:T(8,128)S(1)} %get-tuple-element.21), channel_id=1, source_target_pairs={{0,64},{32,96},{64,0},{96,32},{1,65},{33,97},{65,1},{97,33},{2,66}... | collective-permute-start | bytes 135176 | tf_op jit(solution)/shard_map/ppermute | solution.py:83
  21.8 0.1 collective-permute-start.2
  21.9 0.0 copy-done.1
  21.9 2.0 %collective-permute-start.7 = (bf16[1024,512]{1,0:T(8,128)(2,1)S(1)}, bf16[1024,512]{1,0:T(8,128)(2,1)S(1)}, u32[]{:S(2)}, u32[]{:S(2)}) collective-permute-start(bf16[1024,512]{1,0:T(8,128)(2,1)S(1)} %copy-done.1), channel_id=1, source_target_pairs={{0,1},{1,0},{2,3},{3,2},{4,5},{5,4},{6,7},{7,6},{8,9},{9,8},{10,11... | collective-permute-start | bytes 3145736 | tf_op jit(solution)/shard_map/ppermute | solution.py:83
  23.8 0.0 copy-done.4
  23.8 0.7 dynamic_slice.11
  24.5 0.7 add_convert_fusion.1
  25.2 0.1 fusion
  25.4 0.1 pad_maximum_fusion
  25.4 39.1 %collective-permute-done = f32[8,1408]{1,0:T(8,128)S(1)} collective-permute-done((f32[8,1408]{1,0:T(8,128)S(1)}, f32[8,1408]{1,0:T(8,128)S(1)}, u32[]{:S(2)}, u32[]{:S(2)}) %collective-permute-start) | collective-permute-done | bytes 45088 | tf_op jit(solution)/shard_map/ppermute | solution.py:83
  64.6 2.5 %collective-permute-done.1 = f32[8,1408]{1,0:T(8,128)S(1)} collective-permute-done((f32[8,1408]{1,0:T(8,128)S(1)}, f32[8,1408]{1,0:T(8,128)S(1)}, u32[]{:S(2)}, u32[]{:S(2)}) %collective-permute-start.1) | collective-permute-done | bytes 45088 | tf_op jit(solution)/shard_map/ppermute | solution.py:83
  67.0 0.0 collective-permute-done.2
  67.1 2.8 %collective-permute-start.5 = (f32[4,1408]{1,0:T(4,128)S(1)}, f32[4,1408]{1,0:T(4,128)S(1)}, u32[]{:S(2)}, u32[]{:S(2)}) collective-permute-start(f32[4,1408]{1,0:T(4,128)S(1)} %get-tuple-element.26), channel_id=1, source_target_pairs={{0,16},{8,24},{16,0},{24,8},{1,17},{9,25},{17,1},{25,9},{2,18},{10... | collective-permute-start | bytes 67592 | tf_op jit(solution)/shard_map/ppermute | solution.py:83
  69.9 0.8 collective-permute-start.4
  70.7 0.0 collective-permute-start.3
  70.7 0.8 pad_add_fusion.info_ref
  71.4 0.0 collective-permute-done.5.third_ref
  71.4 2.3 %collective-permute-done.4.second_ref = f32[4,1408]{1,0:T(4,128)S(1)} collective-permute-done((f32[4,1408]{1,0:T(4,128)S(1)}, f32[4,1408]{1,0:T(4,128)S(1)}, u32[]{:S(2)}, u32[]{:S(2)}) %collective-permute-start.4) | collective-permute-done | bytes 22560 | tf_op jit(solution)/shard_map/ppermute | solution.py:83
  73.8 0.0 collective-permute-done.3.first_ref
  73.8 0.0 all-to-all-done
  73.8 4.5 %attend.1 = (bf16[16,8,128,128]{3,2,1,0:T(8,128)(2,1)}, bf16[48,128]{1,0:T(8,128)(2,1)S(1)}) custom-call(s32[2]{0:T(128)S(1)} %pad_add_fusion.info_ref, bf16[16,8,128,128]{3,2,1,0:T(8,128)(2,1)} %bitcast.3.kv_ref, f32[4,1408]{1,0:T(4,128)S(1)} %get-tuple-element.27.own_ref, f32[4,1408]{1,0:T(4,128)S(1)} %collective-permute-done.3.first_ref, ...), custom_call_target="tpu_custom_call" | custom-call | tf_op jit(solution)/shard_map/attend/pallas_call | solution.py:268
  78.3 10.0 %all_to_all.10.states_ref = bf16[16,48,128]{2,1,0:T(8,128)(2,1)S(1)} all-to-all(bf16[16,48,128]{2,1,0:T(8,128)(2,1)S(1)} %broadcast_in_dim.2), channel_id=1, replica_groups=mesh['x'=4,'y'=4,'z'=4,'core'=2] {'x','y'}, dimensions={0} | all-to-all | bytes 393216 | tf_op jit(solution)/shard_map/all_to_all | solution.py:399
  88.3 0.3 combine.1.attn_ref
  88.7 3.9 %collective-permute-start.6 = (bf16[256,128]{1,0:T(8,128)(2,1)S(1)}, bf16[256,128]{1,0:T(8,128)(2,1)S(1)}, u32[]{:S(2)}, u32[]{:S(2)}) collective-permute-start(bf16[256,128]{1,0:T(8,128)(2,1)S(1)} %combine.1.attn_ref), channel_id=1, source_target_pairs={{0,1},{1,0},{2,3},{3,2},{4,5},{5,4},{6,7},{7,6},{8,9},{9,8},{10,11... | collective-permute-start | bytes 196616 | tf_op jit(solution)/shard_map/ppermute | solution.py:83
  92.6 0.3 project.2.refs_0_
  92.8 0.0 collective-permute-done.7.w_ref
  92.8 0.6 collective-permute-done.6.attn_ref
  93.5 0.3 project.3
  93.7 3.2 %collective-permute-start.8 = (bf16[32,512]{1,0:T(8,128)(2,1)S(1)}, bf16[32,512]{1,0:T(8,128)(2,1)S(1)}, u32[]{:S(2)}, u32[]{:S(2)}) collective-permute-start(bf16[32,512]{1,0:T(8,128)(2,1)S(1)} %project.3), channel_id=1, source_target_pairs={{0,2},{1,7},{2,0},{3,5},{4,6},{5,3},{6,4},{7,1},{8,10},{9,15},{10,... | collective-permute-start | bytes 98312 | tf_op jit(solution)/shard_map/ppermute | solution.py:404
  96.9 0.1 collective-permute-start.10
  97.0 1.2 %collective-permute-done.8 = bf16[32,512]{1,0:T(8,128)(2,1)S(1)} collective-permute-done((bf16[32,512]{1,0:T(8,128)(2,1)S(1)}, bf16[32,512]{1,0:T(8,128)(2,1)S(1)}, u32[]{:S(2)}, u32[]{:S(2)}) %collective-permute-start.8) | collective-permute-done | bytes 32800 | tf_op jit(solution)/shard_map/ppermute | solution.py:404
  98.2 0.8 collective-permute-start.9
  99.0 2.2 %collective-permute-done.10 = bf16[32,512]{1,0:T(8,128)(2,1)S(1)} collective-permute-done((bf16[32,512]{1,0:T(8,128)(2,1)S(1)}, bf16[32,512]{1,0:T(8,128)(2,1)S(1)}, u32[]{:S(2)}, u32[]{:S(2)}) %collective-permute-start.10) | collective-permute-done | bytes 32800 | tf_op jit(solution)/shard_map/ppermute | solution.py:83
  101.2 0.0 collective-permute-done.9
  101.2 0.6 add_convert_fusion
  (5 shorter events, 0.1 us)
Async XLA Ops:
  5.5 12.0 %copy-start = (bf16[512,1280]{1,0:T(8,128)(2,1)S(1)}, bf16[512,1280]{1,0:T(8,128)(2,1)}, u32[]{:S(2)}) copy-start(bf16[512,1280]{1,0:T(8,128)(2,1)} %w_ref.1) | copy-start | bytes 3932164
  5.5 12.0 %copy-start.2 = (bf16[32,512]{1,0:T(8,128)(2,1)S(1)}, bf16[32,512]{1,0:T(8,128)(2,1)}, u32[]{:S(2)}) copy-start(bf16[32,512]{1,0:T(8,128)(2,1)} %hidden_ref) | copy-start | bytes 98308
  5.5 12.0 %copy-start.3 = (bf16[512]{0:T(512)(128)(2,1)S(1)}, bf16[512]{0:T(512)(128)(2,1)}, u32[]{:S(2)}) copy-start(bf16[512]{0:T(512)(128)(2,1)} %gain_ref.1) | copy-start | bytes 3076
  5.5 16.3 %copy-start.1 = (bf16[1024,512]{1,0:T(8,128)(2,1)S(1)}, bf16[1024,512]{1,0:T(8,128)(2,1)}, u32[]{:S(2)}) copy-start(bf16[1024,512]{1,0:T(8,128)(2,1)} %w_ref.2) | copy-start | bytes 3145732
  5.5 18.3 %copy-start.4 = (s32[8]{0:T(128)S(1)}, s32[8]{0:T(128)}, u32[]{:S(2)}) copy-start(s32[8]{0:T(128)} %param.8) | copy-start | bytes 100
  5.6 68.2 %all-to-all-start = ((bf16[128,128,128]{2,1,0:T(8,128)(2,1)}), bf16[128,128,128]{2,1,0:T(8,128)(2,1)}, u32[]{:S(2)}, u32[]{:S(2)}) async-start(bf16[128,128,128]{2,1,0:T(8,128)(2,1)} %bitcast.11), calls=%async_computation | async-start | bytes 8388608 | tf_op jit(solution)/shard_map/all_to_all | solution.py:376
  18.0 46.6 %collective-permute-start = (f32[8,1408]{1,0:T(8,128)S(1)}, f32[8,1408]{1,0:T(8,128)S(1)}, u32[]{:S(2)}, u32[]{:S(2)}) collective-permute-start(f32[8,1408]{1,0:T(8,128)S(1)} %get-tuple-element.20), channel_id=1, source_target_pairs={{0,32},{32,0},{64,96},{96,64},{1,33},{33,1},{65,97},{97,65},{2,34}... | collective-permute-start | bytes 135176 | tf_op jit(solution)/shard_map/ppermute | solution.py:83
  19.4 47.7 %collective-permute-start.1 = (f32[8,1408]{1,0:T(8,128)S(1)}, f32[8,1408]{1,0:T(8,128)S(1)}, u32[]{:S(2)}, u32[]{:S(2)}) collective-permute-start(f32[8,1408]{1,0:T(8,128)S(1)} %get-tuple-element.21), channel_id=1, source_target_pairs={{0,64},{32,96},{64,0},{96,32},{1,65},{33,97},{65,1},{97,33},{2,66}... | collective-permute-start | bytes 135176 | tf_op jit(solution)/shard_map/ppermute | solution.py:83
  21.8 45.3 %collective-permute-start.2 = (f32[8,1408]{1,0:T(8,128)S(1)}, f32[8,1408]{1,0:T(8,128)S(1)}, u32[]{:S(2)}, u32[]{:S(2)}) collective-permute-start(f32[8,1408]{1,0:T(8,128)S(1)} %get-tuple-element.22), channel_id=1, source_target_pairs={{0,96},{32,64},{64,32},{96,0},{1,97},{33,65},{65,33},{97,1},{2,98}... | collective-permute-start | bytes 135176 | tf_op jit(solution)/shard_map/ppermute | solution.py:83
  21.9 70.9 %collective-permute-start.7 = (bf16[1024,512]{1,0:T(8,128)(2,1)S(1)}, bf16[1024,512]{1,0:T(8,128)(2,1)S(1)}, u32[]{:S(2)}, u32[]{:S(2)}) collective-permute-start(bf16[1024,512]{1,0:T(8,128)(2,1)S(1)} %copy-done.1), channel_id=1, source_target_pairs={{0,1},{1,0},{2,3},{3,2},{4,5},{5,4},{6,7},{7,6},{8,9},{9,8},{10,11... | collective-permute-start | bytes 3145736 | tf_op jit(solution)/shard_map/ppermute | solution.py:83
  67.1 4.3 %collective-permute-start.5 = (f32[4,1408]{1,0:T(4,128)S(1)}, f32[4,1408]{1,0:T(4,128)S(1)}, u32[]{:S(2)}, u32[]{:S(2)}) collective-permute-start(f32[4,1408]{1,0:T(4,128)S(1)} %get-tuple-element.26), channel_id=1, source_target_pairs={{0,16},{8,24},{16,0},{24,8},{1,17},{9,25},{17,1},{25,9},{2,18},{10... | collective-permute-start | bytes 67592 | tf_op jit(solution)/shard_map/ppermute | solution.py:83
  69.9 3.9 %collective-permute-start.4 = (f32[4,1408]{1,0:T(4,128)S(1)}, f32[4,1408]{1,0:T(4,128)S(1)}, u32[]{:S(2)}, u32[]{:S(2)}) collective-permute-start(f32[4,1408]{1,0:T(4,128)S(1)} %get-tuple-element.26), channel_id=1, source_target_pairs={{0,24},{8,16},{16,8},{24,0},{1,25},{9,17},{17,9},{25,1},{2,26},{10... | collective-permute-start | bytes 67592 | tf_op jit(solution)/shard_map/ppermute | solution.py:83
  70.7 3.1 %collective-permute-start.3 = (f32[4,1408]{1,0:T(4,128)S(1)}, f32[4,1408]{1,0:T(4,128)S(1)}, u32[]{:S(2)}, u32[]{:S(2)}) collective-permute-start(f32[4,1408]{1,0:T(4,128)S(1)} %get-tuple-element.27.own_ref), channel_id=1, source_target_pairs={{0,8},{8,0},{16,24},{24,16},{1,9},{9,1},{17,25},{25,17},{2,10},{10... | collective-permute-start | bytes 67592 | tf_op jit(solution)/shard_map/ppermute | solution.py:83
  88.7 4.8 %collective-permute-start.6 = (bf16[256,128]{1,0:T(8,128)(2,1)S(1)}, bf16[256,128]{1,0:T(8,128)(2,1)S(1)}, u32[]{:S(2)}, u32[]{:S(2)}) collective-permute-start(bf16[256,128]{1,0:T(8,128)(2,1)S(1)} %combine.1.attn_ref), channel_id=1, source_target_pairs={{0,1},{1,0},{2,3},{3,2},{4,5},{5,4},{6,7},{7,6},{8,9},{9,8},{10,11... | collective-permute-start | bytes 196616 | tf_op jit(solution)/shard_map/ppermute | solution.py:83
  93.7 4.5 %collective-permute-start.8 = (bf16[32,512]{1,0:T(8,128)(2,1)S(1)}, bf16[32,512]{1,0:T(8,128)(2,1)S(1)}, u32[]{:S(2)}, u32[]{:S(2)}) collective-permute-start(bf16[32,512]{1,0:T(8,128)(2,1)S(1)} %project.3), channel_id=1, source_target_pairs={{0,2},{1,7},{2,0},{3,5},{4,6},{5,3},{6,4},{7,1},{8,10},{9,15},{10,... | collective-permute-start | bytes 98312 | tf_op jit(solution)/shard_map/ppermute | solution.py:404
  96.9 4.3 %collective-permute-start.10 = (bf16[32,512]{1,0:T(8,128)(2,1)S(1)}, bf16[32,512]{1,0:T(8,128)(2,1)S(1)}, u32[]{:S(2)}, u32[]{:S(2)}) collective-permute-start(bf16[32,512]{1,0:T(8,128)(2,1)S(1)} %project.3), channel_id=1, source_target_pairs={{0,4},{2,6},{4,0},{6,2},{1,5},{3,7},{5,1},{7,3},{8,12},{10,14},{12... | collective-permute-start | bytes 98312 | tf_op jit(solution)/shard_map/ppermute | solution.py:83
  98.2 3.0 %collective-permute-start.9 = (bf16[32,512]{1,0:T(8,128)(2,1)S(1)}, bf16[32,512]{1,0:T(8,128)(2,1)S(1)}, u32[]{:S(2)}, u32[]{:S(2)}) collective-permute-start(bf16[32,512]{1,0:T(8,128)(2,1)S(1)} %collective-permute-done.8), channel_id=1, source_target_pairs={{0,1},{1,0},{2,3},{3,2},{4,5},{5,4},{6,7},{7,6},{8,9},{9,8},{10,11... | collective-permute-start | bytes 98312 | tf_op jit(solution)/shard_map/ppermute | solution.py:83
